TPU v7x, 128 devices: a whole 4x4x4 slice. The times are simulated.
128 devices in a mesh: role: 4 (over y), dp: 32 (over x, z, core).
Axes of the slice: x: 4, y: 4, z: 4, core: 2. Of those that a mesh axis runs over, the one named last changes fastest.
Arguments:
- embedding_table: bfloat16 [131072, 128], P('dp'), may hold values from -0.796875 to 0.796875
- touched_blocks: int32 [32, 384, 16], P('dp', 'role'), may hold values from 0 to 511
- bag_index: int32 [32, 49152, 16], P('dp', 'role'), may hold values from 0 to 127
- bag_count: int32 [32, 49152, 16], P('dp', 'role'), may hold values from 0 to 3
- feature_map: int32 [32], replicated, may hold values from 0 to 31, each once
- labels: int32 [49152], P(('role', 'dp')), may hold values 0 or 1
- v_weight: bfloat16 [4096, 256], replicated, may hold values from -0.09375 to 0.09375
- u_weight: bfloat16 [256, 4096], replicated, may hold values from -0.375 to 0.375
- cross_bias: float32 [4096], replicated, may hold values from -3 to 3
- hidden_weight: bfloat16 [4096, 512], replicated, may hold values from -0.09375 to 0.09375
- hidden_bias: float32 [512], replicated, may hold values from -3 to 3
- out_weight: bfloat16 [512], replicated, may hold values from -0.25 to 0.25
Outputs:
- table_grad: float32 [131072, 128], P('dp')
- grad_v_weight: float32 [4096, 256], P(('role', 'dp'))
- grad_u_weight: float32 [256, 4096], P(None, ('role', 'dp'))
- grad_cross_bias: float32 [4096], P(('role', 'dp'))
- grad_hidden_weight: float32 [4096, 512], P(('role', 'dp'))
- grad_hidden_bias: float32 [512], P(('role', 'dp'))
- grad_out_weight: float32 [512], P(('role', 'dp'))
All inputs are finite; a program needn't handle non-finite values. No bound on the sum of `labels` on one device may be relied on, other than what follows from the above.
Results may differ from a plain program's by a relative error of at most 0.015.
Values may be sent and summed in bfloat16 or wider, within the bound.
No kernel may reach another device: no remote copies, remote signals or barrier semaphores. Data moves between devices by JAX's collectives and lax.ppermute only.
A program may use at most 128 MiB of HBM per device.

v0:
```python
import jax
import jax.numpy as jnp
from jax import lax
from jax.sharding import PartitionSpec as P

BLK = 8


LOSS_SCALE = 65536.0


def incidence(index, count, tile_rows):
    columns = lax.broadcasted_iota(jnp.int32, (1, tile_rows), 1)
    running = jnp.zeros((index.shape[0], tile_rows), jnp.int32)
    for position in range(index.shape[1]):
        running = running + jnp.where(
            index[:, position : position + 1] == columns, count[:, position : position + 1], 0
        )
    return running.astype(jnp.bfloat16)


def inner_rows(left, right):
    return lax.dot_general(
        left, right, (((0,), (0,)), ((), ())), preferred_element_type=jnp.float32
    )


def against_rows(left, right):
    return lax.dot_general(
        left, right, (((1,), (1,)), ((), ())), preferred_element_type=jnp.float32
    )


def body(
    embedding_table,
    touched_blocks,
    bag_index,
    bag_count,
    feature_map,
    labels,
    v_weight,
    u_weight,
    cross_bias,
    hidden_weight,
    hidden_bias,
    out_weight,
):
    rows_shard, embed_width = embedding_table.shape
    group_samples = bag_index.shape[1]
    tile_count = touched_blocks.shape[1]
    tile_samples = group_samples // tile_count
    tile_rows = touched_blocks.shape[2] * BLK
    row_ids = (
        touched_blocks[0][:, :, None] * BLK + lax.broadcasted_iota(jnp.int32, (1, 1, BLK), 2)
    ).reshape(tile_count, tile_rows)
    picked = embedding_table[row_ids]
    weights = incidence(bag_index[0], bag_count[0], tile_rows).reshape(
        tile_count, tile_samples, tile_rows
    )
    pooled = jnp.einsum("tnc,tce->tne", weights, picked, preferred_element_type=jnp.float32).astype(
        jnp.bfloat16
    )
    pooled = pooled.reshape(1, group_samples, embed_width)
    received = lax.all_to_all(pooled, "dp", split_axis=1, concat_axis=0, tiled=True)
    feature_count, batch = (received.shape[0], received.shape[1])
    onehot = (
        feature_map[:, None] == lax.broadcasted_iota(jnp.int32, (1, feature_count), 1)
    ).astype(jnp.bfloat16)
    interaction = jnp.einsum(
        "sf,sbe->bfe", onehot, received, preferred_element_type=jnp.float32
    ).astype(jnp.bfloat16)
    interaction = interaction.reshape(batch, feature_count * embed_width)
    total_samples = lax.axis_size("role") * lax.axis_size("dp") * batch
    low_rank = jnp.dot(interaction, v_weight, preferred_element_type=jnp.float32).astype(
        jnp.bfloat16
    )
    projected = jnp.dot(low_rank, u_weight, preferred_element_type=jnp.float32) + cross_bias
    inter_float = interaction.astype(jnp.float32)
    crossed = (inter_float * projected + inter_float).astype(jnp.bfloat16)
    hidden_pre = jnp.dot(crossed, hidden_weight, preferred_element_type=jnp.float32) + hidden_bias
    hidden_act = jax.nn.silu(hidden_pre).astype(jnp.bfloat16)
    logit = jnp.dot(hidden_act, out_weight, preferred_element_type=jnp.float32)
    d_logit = (
        LOSS_SCALE / total_samples * (jax.nn.sigmoid(logit) - labels.astype(jnp.float32))
    ).astype(jnp.bfloat16)
    grad_out = jnp.dot(d_logit, hidden_act, preferred_element_type=jnp.float32)
    gate_sig = jax.nn.sigmoid(hidden_pre)
    slope_factor = gate_sig * (1.0 + hidden_pre * (1.0 - gate_sig))
    d_hidden = (
        d_logit.astype(jnp.float32)[:, None]
        * out_weight.astype(jnp.float32)[None, :]
        * slope_factor
    ).astype(jnp.bfloat16)
    grad_hw = inner_rows(crossed, d_hidden)
    grad_hb = jnp.sum(d_hidden.astype(jnp.float32), axis=0)
    d_crossed = against_rows(d_hidden, hidden_weight)
    d_proj = d_crossed * inter_float
    grad_cb = jnp.sum(d_proj, axis=0)
    d_proj_low = d_proj.astype(jnp.bfloat16)
    grad_u = inner_rows(low_rank, d_proj_low)
    low_grad = against_rows(d_proj_low, u_weight).astype(jnp.bfloat16)
    grad_v = inner_rows(interaction, low_grad)
    d_inter = (d_crossed * (projected + 1.0) + against_rows(low_grad, v_weight)).astype(
        jnp.bfloat16
    )
    results = (
        lax.psum_scatter(grad_v, ("role", "dp"), scatter_dimension=0, tiled=True),
        lax.psum_scatter(grad_u, ("role", "dp"), scatter_dimension=1, tiled=True),
        lax.psum_scatter(grad_cb, ("role", "dp"), scatter_dimension=0, tiled=True),
        lax.psum_scatter(grad_hw, ("role", "dp"), scatter_dimension=0, tiled=True),
        lax.psum_scatter(grad_hb, ("role", "dp"), scatter_dimension=0, tiled=True),
        lax.psum_scatter(grad_out, ("role", "dp"), scatter_dimension=0, tiled=True),
    )
    d_slots = jnp.einsum(
        "sf,bfe->sbe",
        onehot,
        d_inter.reshape(batch, feature_count, embed_width),
        preferred_element_type=jnp.float32,
    ).astype(jnp.bfloat16)
    returned = lax.all_to_all(d_slots, "dp", split_axis=0, concat_axis=1, tiled=True)
    tile_grad = jnp.einsum(
        "tnc,tne->tce",
        weights,
        returned.reshape(tile_count, tile_samples, embed_width),
        preferred_element_type=jnp.float32,
    )
    local_grad = (
        jnp.zeros((rows_shard, embed_width), jnp.float32)
        .at[row_ids.reshape(-1)]
        .add(tile_grad.reshape(-1, embed_width))
    )
    table_grad = lax.psum(local_grad.astype(jnp.bfloat16), "role").astype(jnp.float32)
    return (table_grad, results[0], results[1], results[2], results[3], results[4], results[5])


def solution(mesh):
    placed = (
        P("dp", None),
        P("dp", "role", None),
        P("dp", "role", None),
        P("dp", "role", None),
        P(),
        P(("role", "dp")),
        P(),
        P(),
        P(),
        P(),
        P(),
        P(),
    )
    return jax.shard_map(
        body,
        mesh=mesh,
        in_specs=placed,
        out_specs=(
            P("dp", None),
            P(("role", "dp"), None),
            P(None, ("role", "dp")),
            P(("role", "dp")),
            P(("role", "dp"), None),
            P(("role", "dp")),
            P(("role", "dp")),
        ),
        check_vma=False,
    )
```

profile of v0, /device:TPU:1, one launch (start us, length us, event | category | flops | bytes accessed | tf_op | source)
XLA Modules:
  0.0 2359.7 jit_solution(8149531640719654287)
XLA Ops:
  8.0 5.5 fusion.32
  13.5 5.1 fusion.33
  18.6 1.3 multiply_bitcast_fusion
  19.9 0.6 add.206
  20.5 0.8 compare_select_fusion.1
  21.3 0.7 copy.34
  22.0 1.4 bitcast_clamp_fusion
  23.5 47.4 %gather_fusion = bf16[12288,128]{1,0:T(8,128)(2,1)} fusion(bf16[4096,128]{1,0:T(8,128)(2,1)S(1)} %copy-done.2, s32[12288]{0:T(1024)} %bitcast_clamp_fusion), kind=kCustom, calls=%fused_computation | custom fusion | bytes 6340608 | tf_op jit(solution)/shard_map/gather | solution.py:56
  70.9 13.7 add_convert_fusion.1
  84.6 1.2 convolution_convert_fusion.1
  85.8 49.5 %copy.70 = bf16[1,12288,128]{2,0,1:T(2,128)(2,1)} copy(bf16[1,12288,128]{2,1,0:T(8,128)(2,1)S(1)} %bitcast.111) | data formatting | bytes 6291456 | tf_op jit(solution)/shard_map/reshape | solution.py:63
  135.3 0.5 broadcast.202
  135.8 68.6 %reduce.2 = bf16[12288,128]{1,0:T(8,128)(2,1)} reduce(bf16[12288,1,128]{2,1,0:T(2,128)(2,1)} %bitcast.107, bf16[]{:T(256)} %broadcast.202), dimensions={1}, to_apply=%bitcast.99.reduce_sub_computation | reduce | bytes 6291458
  204.4 7.6 reshape.369
  212.0 9.5 all-to-all-start
  221.5 39.8 %all-to-all-done = bf16[32,2,24576]{2,1,0:T(2,128)(2,1)} async-done(((bf16[32,2,24576]{2,1,0:T(2,128)(2,1)}), bf16[32,2,24576]{2,1,0:T(2,128)(2,1)}, u32[]{:S(2)}, u32[]{:S(2)}) %all-to-all-start) | async-done | bytes 3145760 | tf_op jit(solution)/shard_map/all_to_all | solution.py:64
  261.3 18.9 reshape.370
  280.2 4.0 copy.43
  284.2 2.2 fusion.9
  286.4 1.1 fusion.15
  287.5 1.0 convolution_add_fusion
  288.5 1.2 copy-done.8
  289.7 2.7 multiply_convert_fusion.1
  292.7 0.3 convert_reduce_fusion
  293.1 2.2 fusion.1
  295.3 2.0 convolution_convert_fusion.2
  297.3 1.4 fusion.12
  298.6 0.8 copy.45
  299.5 1.2 convolution_convert_fusion
  300.7 2.9 copy.39
  303.6 5.0 all-to-all-start.1
  308.8 0.4 copy.33
  309.2 0.4 add.186
  309.6 38.9 %all-to-all-done.1 = bf16[32,384,128]{2,1,0:T(8,128)(2,1)} async-done(((bf16[32,384,128]{2,1,0:T(8,128)(2,1)}), bf16[32,384,128]{2,1,0:T(8,128)(2,1)}, u32[]{:S(2)}, u32[]{:S(2)}) %all-to-all-start.1) | async-done | bytes 3145760 | tf_op jit(solution)/shard_map/all_to_all | solution.py:120
  348.5 6.5 fusion.34
  355.0 66.5 %scatter_custom_fusion = f32[4096,128]{1,0:T(8,128)S(1)} fusion(s32[12288]{0:T(1024)S(1)} %bitcast.148, f32[12288,128]{1,0:T(8,128)} %bitcast.113, f32[]{:T(128)} %constant.6.clone.1), kind=kCustom, calls=%fused_computation.42 | custom fusion | flops 1572864 | bytes 2097664 | tf_op jit(solution)/shard_map/scatter-add | solution.py:130
  421.5 1.1 convert_element_type.79
  422.6 8.6 fusion.25
  431.6 7.1 fusion.3
  438.8 11.0 fusion.28
  450.0 65.6 %all-reduce.3 = (f32[4096]{0:T(1024)S(1)}, f32[512]{0:T(512)S(1)}, f32[512]{0:T(512)S(1)}) all-reduce(f32[4096]{0:T(1024)S(1)} %get-tuple-element.48, f32[512]{0:T(512)S(1)} %get-tuple-element.10, f32[512]{0:T(512)S(1)} %bitcast.149), channel_id=4, replica_groups=mesh['role'=4,'dp'=32] {'role','dp'}, use_global_device_ids=true, to_apply=%region_5.6.clone | all-reduce | flops 5120 | bytes 40960
  515.6 0.6 dynamic-slice.1
  516.2 0.6 dynamic-slice.2
  516.8 0.6 dynamic-slice
  517.4 2.7 convert_element_type.80
  520.0 546.1 %reduce-scatter.6.cloned.1.call-done = f32[256,32]{0,1:T(8,128)} async-done(((f32[256,4096]{0,1:T(8,128)}), f32[256,32]{0,1:T(8,128)}) %reduce-scatter.6.cloned.1.call-update) | async-done | bytes 32784 | tf_op jit(solution)/shard_map/reduce_scatter | solution.py:108
  1066.2 638.9 %reduce-scatter.4.cloned.1.call-done = f32[32,256]{1,0:T(8,128)} async-done(((f32[4096,256]{1,0:T(8,128)}), f32[32,256]{1,0:T(8,128)}) %reduce-scatter.4.cloned.1.call-update) | async-done | bytes 32784 | tf_op jit(solution)/shard_map/reduce_scatter | solution.py:107
  1705.1 646.6 %reduce-scatter.8.cloned.1.call-done = f32[32,512]{1,0:T(8,128)} async-done(((f32[4096,512]{1,0:T(8,128)}), f32[32,512]{1,0:T(8,128)}) %reduce-scatter.8.cloned.1.call-update) | async-done | bytes 65552 | tf_op jit(solution)/shard_map/reduce_scatter | solution.py:110
  (51 shorter events, 1.1 us)
Async XLA Ops:
  8.0 279.5 %copy-start = (bf16[256,4096]{1,0:T(8,128)(2,1)S(1)}, bf16[256,4096]{1,0:T(8,128)(2,1)}, u32[]{:S(2)}) copy-start(bf16[256,4096]{1,0:T(8,128)(2,1)} %param.19) | copy-start | bytes 6291460
  8.0 15.4 copy-start.2
  23.5 47.4 %copy-start.10 = (s32[12288,1]{0,1:T(1,128)S(1)}, s32[12288,1]{0,1:T(1,128)}, u32[]{:S(2)}) copy-start(s32[12288,1]{0,1:T(1,128)} %get-tuple-element.21) | copy-start | bytes 147460
  70.9 13.7 copy-start.7
  84.6 50.8 %copy-start.6 = (bf16[96,128,128]{1,2,0:T(8,128)(2,1)}, bf16[96,128,128]{1,2,0:T(8,128)(2,1)S(1)}, u32[]{:S(2)}) copy-start(bf16[96,128,128]{1,2,0:T(8,128)(2,1)S(1)} %add_convert_fusion.1) | copy-start | bytes 9437188
  204.4 17.1 copy-start.13
  212.0 49.3 %all-to-all-start = ((bf16[32,2,24576]{2,1,0:T(2,128)(2,1)}), bf16[32,2,24576]{2,1,0:T(2,128)(2,1)}, u32[]{:S(2)}, u32[]{:S(2)}) async-start(bf16[32,2,24576]{2,1,0:T(2,128)(2,1)} %reshape.369), calls=%async_computation | async-start | bytes 6291456 | tf_op jit(solution)/shard_map/all_to_all | solution.py:64
  280.2 4.0 copy-start.14
  280.2 6.2 copy-start.9
  284.2 3.4 copy-start.11
  286.4 8.9 copy-start.3
  286.4 3.3 copy-start.8
  286.4 3.3 copy-start.16
  289.7 7.6 copy-start.5
  289.7 3.0 copy-start.15
  295.2 3.4 copy-start.4
  300.7 8.0 copy-start.12
  303.6 44.9 %all-to-all-start.1 = ((bf16[32,384,128]{2,1,0:T(8,128)(2,1)}), bf16[32,384,128]{2,1,0:T(8,128)(2,1)}, u32[]{:S(2)}, u32[]{:S(2)}) async-start(bf16[32,384,128]{2,1,0:T(8,128)(2,1)} %copy.39), calls=%async_computation.1 | async-start | bytes 6291456 | tf_op jit(solution)/shard_map/all_to_all | solution.py:120
  308.7 208.7 %all-reduce.6.cloned.1.call-start = ((), (), s32[]{:S(2)}) async-start(), calls=%async_computation.5 | async-start | bytes 2097152 | tf_op jit(solution)/shard_map/psum | solution.py:132
  422.6 643.6 %reduce-scatter.6.cloned.1.call-start = ((), (), s32[]{:S(2)}) async-start(), calls=%async_computation.7 | async-start | bytes 4227072 | tf_op jit(solution)/shard_map/reduce_scatter | solution.py:108
  431.3 1273.8 %reduce-scatter.4.cloned.1.call-start = ((), (), s32[]{:S(2)}) async-start(), calls=%async_computation.6 | async-start | bytes 4227072 | tf_op jit(solution)/shard_map/reduce_scatter | solution.py:107
  438.7 1913.0 %reduce-scatter.8.cloned.1.call-start = ((), (), s32[]{:S(2)}) async-start(), calls=%async_computation.8 | async-start | bytes 8454144 | tf_op jit(solution)/shard_map/reduce_scatter | solution.py:110
  438.8 1912.9 %copy-start.1 = (bf16[256,4096]{1,0:T(8,128)(2,1)S(1)}, bf16[256,4096]{1,0:T(8,128)(2,1)}, u32[]{:S(2)}) copy-start(bf16[256,4096]{1,0:T(8,128)(2,1)} %param.19) | copy-start | bytes 6291460
Sparse Core Ops, SparseCore 0:
  422.7 43.9 all-reduce.5
Sparse Core Ops, SparseCore 1:
  431.4 634.7 reduce-scatter.5
  1069.0 636.0 reduce-scatter.3
  1708.0 643.6 reduce-scatter.7
where the time goes:
time: 2380 us; the launch traced here: 2360 us
  waiting for transfers between devices  1910 us (80%)
  other arithmetic  156 us (7%)
  local copies, waits for them, and re-layouts  147 us (6%)
  blocking collectives  65.6 us (3%)
  matrix products  48.5 us (2%)
    reduce_scatter x1, waiting for transfers between devices, body(): lax.psum_scatter(grad_hw, ('role', 'dp'), scatter_dimension=0, tiled=True)  647 us
    reduce_scatter x1, waiting for transfers between devices, body(): lax.psum_scatter(grad_v, ('role', 'dp'), scatter_dimension=0, tiled=True)  639 us
    reduce_scatter x1, waiting for transfers between devices, body(): lax.psum_scatter(grad_u, ('role', 'dp'), scatter_dimension=1, tiled=True)  546 us
    unnamed x1, other arithmetic  68.6 us
    scatter-add x1, other arithmetic, body(): local_grad = jnp.zeros((rows_shard, embed_width), jnp.float32).at[row_ids...  66.5 us
    unnamed x1, blocking collectives  65.6 us
    reshape x1, local copies, waits for them, and re-layouts, body(): pooled = pooled.reshape(1, group_samples, embed_width)  49.5 us
  transfers between devices with their start and end apart: 6, of which 5 were waited for; matrix products, arithmetic and copies ran while one was open for 1% of the time, Pallas kernels for 0%

commit v1 on v0

v1 whole, which is shorter than its diff:
```python
import functools

import jax
import jax.numpy as jnp
from jax import lax
from jax.experimental import pallas as pl
from jax.experimental.pallas import tpu as pltpu
from jax.sharding import Mesh
from jax.sharding import PartitionSpec as P

BLK = 8
LOSS_SCALE = 65536.0
STEP_TILES = 8
WIDE = 512
EXTRA = 16

BF = jnp.bfloat16
F32 = jnp.float32


def nt(left, right):
    return lax.dot_general(left, right, (((1,), (1,)), ((), ())), preferred_element_type=F32)


def pool_kernel(touched, table, index, count, pooled, incidence, rows32):
    step = pl.program_id(0)
    tile = incidence.shape[1]

    @pl.when(step == 0)
    def _():
        rows32[...] = table[...].astype(F32)

    listed = lax.broadcasted_iota(jnp.int32, (tile, tile), 0).astype(BF)
    for i in range(STEP_TILES):
        t = step * STEP_TILES + i
        idx = index[:, i * tile : (i + 1) * tile].astype(BF)
        cnt = count[:, i * tile : (i + 1) * tile].astype(BF)
        total = jnp.zeros((tile, tile), BF)
        for j in range(index.shape[0]):
            total += jnp.where(idx[j : j + 1] == listed, cnt[j : j + 1], jnp.zeros((), BF))
        incidence[i] = total
        blocks = [
            rows32[pl.ds(pl.multiple_of(touched[k, t] * BLK, BLK), BLK), :]
            for k in range(touched.shape[0])
        ]
        picked = jnp.concatenate(blocks, axis=0).astype(BF)
        pooled[pl.ds(i * tile, tile), :] = lax.dot_general(
            total, picked, (((0,), (0,)), ((), ())), preferred_element_type=F32
        ).astype(BF)


def pool(touched, table, index, count, tile):
    hot, samples = index.shape
    tiles = samples // tile
    width = table.shape[1]
    span = STEP_TILES * tile
    return pl.pallas_call(
        pool_kernel,
        name="pool",
        grid_spec=pltpu.PrefetchScalarGridSpec(
            num_scalar_prefetch=1,
            grid=(tiles // STEP_TILES,),
            in_specs=[
                pl.BlockSpec(table.shape, lambda s, _: (0, 0)),
                pl.BlockSpec((hot, span), lambda s, _: (0, s)),
                pl.BlockSpec((hot, span), lambda s, _: (0, s)),
            ],
            out_specs=[
                pl.BlockSpec((span, width), lambda s, _: (s, 0)),
                pl.BlockSpec((STEP_TILES, tile, tile), lambda s, _: (s, 0, 0)),
            ],
            scratch_shapes=[pltpu.VMEM(table.shape, F32)],
        ),
        out_shape=[
            jax.ShapeDtypeStruct((samples, width), BF),
            jax.ShapeDtypeStruct((tiles, tile, tile), BF),
        ],
        compiler_params=pltpu.CompilerParams(vmem_limit_bytes=24 << 20),
    )(touched, table, index, count)


def scatter_kernel(touched, incidence, grad, out, *sums):
    step = pl.program_id(0)
    tile = incidence.shape[1]

    @pl.when(step == 0)
    def _():
        for acc in sums:
            acc[...] = jnp.zeros_like(acc)

    for i in range(STEP_TILES):
        t = step * STEP_TILES + i
        product = jnp.dot(
            incidence[i], grad[pl.ds(i * tile, tile), :], preferred_element_type=F32
        )
        for k in range(touched.shape[0]):
            acc = sums[k % len(sums)]
            rows = pl.ds(pl.multiple_of(touched[k, t] * BLK, BLK), BLK)
            acc[rows, :] += product[k * BLK : (k + 1) * BLK]

    @pl.when(step == pl.num_programs(0) - 1)
    def _():
        total = sums[0][...]
        for acc in sums[1:]:
            total = total + acc[...]
        out[...] = total.astype(out.dtype)


def scatter(touched, incidence, grad, rows):
    tiles, tile, _ = incidence.shape
    width = grad.shape[1]
    span = STEP_TILES * tile
    return pl.pallas_call(
        scatter_kernel,
        name="scatter",
        grid_spec=pltpu.PrefetchScalarGridSpec(
            num_scalar_prefetch=1,
            grid=(tiles // STEP_TILES,),
            in_specs=[
                pl.BlockSpec((STEP_TILES, tile, tile), lambda s, _: (s, 0, 0)),
                pl.BlockSpec((span, width), lambda s, _: (s, 0)),
            ],
            out_specs=pl.BlockSpec((rows, width), lambda s, _: (0, 0)),
            scratch_shapes=[pltpu.VMEM((rows, width), F32)] * 4,
        ),
        out_shape=jax.ShapeDtypeStruct((rows, width), BF),
        compiler_params=pltpu.CompilerParams(vmem_limit_bytes=24 << 20),
    )(touched, incidence, grad)


def dense_kernel(
    scale,
    fmap,
    received,
    labels,
    v_hbm,
    u_hbm,
    cross_bias,
    h_hbm,
    hidden_bias,
    out_weight,
    back,
    inter_out,
    crossed_out,
    proj_out,
    low_out,
    low_grad_out,
    d_hidden_out,
    cross_bias_grad,
    hidden_bias_grad,
    out_weight_grad,
    inter,
    crossed,
    proj_low,
    held,
    d_inter,
    v,
    u,
    h,
    hidden,
    low_sum,
    slot_of,
    in_sems,
    weight_sems,
    out_sems,
    back_sems,
):
    features, batch, width = received.shape
    total_width = features * width
    blocks = total_width // WIDE
    per_block = WIDE // width

    loads = []
    for s in range(features):
        cols = pl.ds(pl.multiple_of(fmap[s] * width, width), width)
        copy = pltpu.make_async_copy(received.at[s], inter.at[:, cols], in_sems.at[s])
        copy.start()
        loads.append(copy)
    weights = [
        pltpu.make_async_copy(source, target, weight_sems.at[i])
        for i, (source, target) in enumerate(((v_hbm, v), (u_hbm, u), (h_hbm, h)))
    ]
    for copy in weights:
        copy.start()
    for s in range(features):
        slot_of[fmap[s]] = s
    low_sum[...] = jnp.zeros_like(low_sum)
    hidden[...] = jnp.broadcast_to(hidden_bias[...], hidden.shape)
    for copy in loads:
        copy.wait()
    inter_copy = pltpu.make_async_copy(inter, inter_out, out_sems.at[0])
    inter_copy.start()
    weights[0].wait()

    @pl.loop(0, blocks)
    def _(b):
        cols = pl.ds(pl.multiple_of(b * WIDE, WIDE), WIDE)
        low_sum[...] += jnp.dot(inter[:, cols], v[cols, :], preferred_element_type=F32)

    low_out[...] = low_sum[...].astype(BF)
    weights[1].wait()
    weights[2].wait()

    @pl.loop(0, blocks)
    def _(b):
        cols = pl.ds(pl.multiple_of(b * WIDE, WIDE), WIDE)
        projected = (
            jnp.dot(low_out[...], u[:, cols], preferred_element_type=F32) + cross_bias[:, cols]
        )
        held[:, cols] = projected
        x = inter[:, cols].astype(F32)
        product = (x * projected + x).astype(BF)
        crossed[:, cols] = product
        hidden[...] += jnp.dot(product, h[cols, :], preferred_element_type=F32)

    crossed_copy = pltpu.make_async_copy(crossed, crossed_out, out_sems.at[1])
    crossed_copy.start()
    hidden_bias_grad[...] = jnp.zeros_like(hidden_bias_grad)
    out_weight_grad[...] = jnp.zeros_like(out_weight_grad)
    chunk = 64

    @pl.loop(0, batch // chunk)
    def _(r):
        rows = pl.ds(pl.multiple_of(r * chunk, chunk), chunk)
        pre = hidden[rows, :]
        gate = jax.nn.sigmoid(pre)
        act = (pre * gate).astype(BF).astype(F32)
        weight = out_weight[...].astype(F32)
        logit = jnp.sum(act * weight, axis=1, keepdims=True)
        d_logit = (scale * (jax.nn.sigmoid(logit) - labels[rows, :].astype(F32))).astype(BF)
        d_logit = d_logit.astype(F32)
        d_hidden = (d_logit * weight * (gate * (1.0 + pre * (1.0 - gate)))).astype(BF)
        d_hidden_out[rows, :] = d_hidden
        hidden_bias_grad[...] += jnp.sum(d_hidden.astype(F32), axis=0, keepdims=True)
        out_weight_grad[...] += jnp.sum(d_logit * act, axis=0, keepdims=True)

    low_sum[...] = jnp.zeros_like(low_sum)

    @pl.loop(0, blocks)
    def _(b):
        cols = pl.ds(pl.multiple_of(b * WIDE, WIDE), WIDE)
        d_crossed = nt(d_hidden_out[...], h[cols, :])
        d_proj = d_crossed * inter[:, cols].astype(F32)
        cross_bias_grad[:, cols] = jnp.sum(d_proj, axis=0, keepdims=True)
        rounded = d_proj.astype(BF)
        proj_low[:, cols] = rounded
        low_sum[...] += nt(rounded, u[:, cols])
        held[:, cols] = d_crossed * (held[:, cols] + 1.0)

    proj_copy = pltpu.make_async_copy(proj_low, proj_out, out_sems.at[2])
    proj_copy.start()
    low_grad_out[...] = low_sum[...].astype(BF)
    stores = []
    for b in range(blocks):
        cols = pl.ds(b * WIDE, WIDE)
        d_inter[:, cols] = (held[:, cols] + nt(low_grad_out[...], v[cols, :])).astype(BF)
        for i in range(per_block):
            f = b * per_block + i
            copy = pltpu.make_async_copy(
                d_inter.at[:, pl.ds(f * width, width)], back.at[slot_of[f]], back_sems.at[f]
            )
            copy.start()
            stores.append(copy)
    for copy in stores:
        copy.wait()
    inter_copy.wait()
    crossed_copy.wait()
    proj_copy.wait()


def dense(fmap, received, labels, v, u, cross_bias, h, hidden_bias, out_weight, scale):
    features, batch, width = received.shape
    total_width = features * width
    rank = v.shape[1]
    units = h.shape[1]
    vmem = pl.BlockSpec(memory_space=pltpu.VMEM)
    smem = pl.BlockSpec(memory_space=pltpu.SMEM)
    hbm = pl.BlockSpec(memory_space=pl.ANY)
    wide = jax.ShapeDtypeStruct((batch, total_width), BF)
    return pl.pallas_call(
        functools.partial(dense_kernel, scale),
        name="dense",
        in_specs=[smem, hbm, vmem, hbm, hbm, vmem, hbm, vmem, vmem],
        out_specs=[hbm, hbm, hbm, hbm, vmem, vmem, vmem, vmem, vmem, vmem],
        out_shape=[
            jax.ShapeDtypeStruct(received.shape, BF),
            wide,
            wide,
            wide,
            jax.ShapeDtypeStruct((batch, rank), BF),
            jax.ShapeDtypeStruct((batch, rank), BF),
            jax.ShapeDtypeStruct((batch, units), BF),
            jax.ShapeDtypeStruct((1, total_width), F32),
            jax.ShapeDtypeStruct((1, units), F32),
            jax.ShapeDtypeStruct((1, units), F32),
        ],
        scratch_shapes=[
            pltpu.VMEM((batch, total_width), BF),
            pltpu.VMEM((batch, total_width), BF),
            pltpu.VMEM((batch, total_width), BF),
            pltpu.VMEM((batch, total_width), F32),
            pltpu.VMEM((batch, total_width), BF),
            pltpu.VMEM(v.shape, BF),
            pltpu.VMEM(u.shape, BF),
            pltpu.VMEM(h.shape, BF),
            pltpu.VMEM((batch, units), F32),
            pltpu.VMEM((batch, rank), F32),
            pltpu.SMEM((features,), jnp.int32),
            pltpu.SemaphoreType.DMA((features,)),
            pltpu.SemaphoreType.DMA((3,)),
            pltpu.SemaphoreType.DMA((3,)),
            pltpu.SemaphoreType.DMA((features,)),
        ],
        compiler_params=pltpu.CompilerParams(vmem_limit_bytes=48 << 20),
    )(fmap, received, labels, v, u, cross_bias, h, hidden_bias, out_weight)


def gradients_kernel(
    core, inter, crossed, proj, low, low_grad, d_hidden, extra, keep, send, low_t, low_grad_t, d_hidden_t
):
    @pl.when(pl.program_id(0) == 0)
    def _():
        low_t[...] = low[...].astype(F32).T.astype(BF)
        low_grad_t[...] = low_grad[...].astype(F32).T.astype(BF)
        d_hidden_t[...] = d_hidden[...].astype(F32).T.astype(BF)

    first = core[0] == 0
    rank = low_t.shape[0]
    features, _, _, width = keep.shape
    of_v = jnp.dot(low_grad_t[...], inter[...], preferred_element_type=F32).astype(BF)
    of_u = jnp.dot(low_t[...], proj[...], preferred_element_type=F32).astype(BF)
    of_h = jnp.dot(d_hidden_t[...], crossed[...], preferred_element_type=F32).astype(BF)
    nothing = jnp.zeros((EXTRA, width), BF)

    def fill(one, other):
        for i in range(features):
            lanes = slice(i * width, (i + 1) * width)
            one[i, 0, pl.ds(0, rank), :] = of_v[:, lanes]
            one[i, 0, pl.ds(rank, EXTRA), :] = extra[i]
            one[i, 1, pl.ds(0, rank), :] = of_u[:, lanes]
            one[i, 1, pl.ds(rank, EXTRA), :] = nothing
            other[i, 0, pl.ds(0, rank), :] = of_h[:rank, lanes]
            other[i, 0, pl.ds(rank, EXTRA), :] = nothing
            other[i, 1, pl.ds(0, rank), :] = of_h[rank:, lanes]
            other[i, 1, pl.ds(rank, EXTRA), :] = nothing

    @pl.when(first)
    def _():
        fill(keep, send)

    @pl.when(jnp.logical_not(first))
    def _():
        fill(send, keep)


def gradients(core, inter, crossed, proj, low, low_grad, d_hidden, extra, width):
    batch, total_width = inter.shape
    rank, units = low.shape[1], d_hidden.shape[1]
    features = total_width // width
    pair = 2
    wide = pl.BlockSpec((batch, pair * width), lambda s, _: (0, s))
    half = jax.ShapeDtypeStruct((features, 2, rank + EXTRA, width), BF)
    half_spec = pl.BlockSpec((pair, 2, rank + EXTRA, width), lambda s, _: (s, 0, 0, 0))
    return pl.pallas_call(
        gradients_kernel,
        name="gradients",
        grid_spec=pltpu.PrefetchScalarGridSpec(
            num_scalar_prefetch=1,
            grid=(features // pair,),
            in_specs=[
                wide,
                wide,
                wide,
                pl.BlockSpec((batch, rank), lambda s, _: (0, 0)),
                pl.BlockSpec((batch, rank), lambda s, _: (0, 0)),
                pl.BlockSpec((batch, units), lambda s, _: (0, 0)),
                pl.BlockSpec((pair, EXTRA, width), lambda s, _: (s, 0, 0)),
            ],
            out_specs=[half_spec, half_spec],
            scratch_shapes=[
                pltpu.VMEM((rank, batch), BF),
                pltpu.VMEM((rank, batch), BF),
                pltpu.VMEM((units, batch), BF),
            ],
        ),
        out_shape=[half, half],
        compiler_params=pltpu.CompilerParams(vmem_limit_bytes=24 << 20),
        cost_estimate=pl.CostEstimate(
            flops=2 * batch * total_width * (2 * rank + units),
            bytes_accessed=18 << 20,
            transcendentals=0,
        ),
    )(core, inter, crossed, proj, low, low_grad, d_hidden, extra)


def body(
    embedding_table,
    touched_blocks,
    bag_index,
    bag_count,
    feature_map,
    labels,
    v_weight,
    u_weight,
    cross_bias,
    hidden_weight,
    hidden_bias,
    out_weight,
):
    dp = ("x", "zh", "zl", "core")
    features = feature_map.shape[0]
    rows, width = embedding_table.shape
    samples = bag_index.shape[1]
    tile = samples // touched_blocks.shape[1]
    batch = labels.shape[0]
    rank = v_weight.shape[1]
    units = hidden_weight.shape[1]
    roles = lax.axis_size("role")
    total = roles * lax.axis_size(dp) * batch
    core = lax.axis_index("core")

    touched = touched_blocks[0].T
    pooled, incidence = pool(touched, embedding_table, bag_index[0].T, bag_count[0].T, tile)
    received = lax.all_to_all(
        pooled.reshape(features, batch, width), dp, split_axis=0, concat_axis=0, tiled=True
    )
    back, inter, crossed, proj, low, low_grad, d_hidden, cross_g, hidden_g, out_g = dense(
        feature_map,
        received,
        labels.reshape(batch, 1),
        v_weight,
        u_weight,
        cross_bias.reshape(1, -1),
        hidden_weight,
        hidden_bias.reshape(1, -1),
        out_weight.reshape(1, -1),
        LOSS_SCALE / total,
    )
    returned = lax.all_to_all(back, dp, split_axis=0, concat_axis=0, tiled=True)

    quarters = 4
    share = width // quarters
    per = units // (features * quarters)

    def spread(values):
        values = values.reshape(features, quarters, per)
        return jnp.pad(values, ((0, 0), (0, 0), (0, share - per))).reshape(features, 1, width)

    extra = jnp.concatenate(
        [cross_g.reshape(features, 1, width), spread(hidden_g), spread(out_g)], axis=1
    )
    extra = jnp.pad(extra, ((0, 0), (0, EXTRA - 3), (0, 0))).astype(BF)
    keep, send = gradients(
        core.reshape(1), inter, crossed, proj, low, low_grad, d_hidden, extra, width
    )
    other = lax.ppermute(send, "core", [(0, 1), (1, 0)])
    chip_sum = (keep.astype(F32) + other.astype(F32)).astype(BF)
    role_sum = lax.psum_scatter(chip_sum, "role", scatter_dimension=0, tiled=True)
    pieces = lax.all_to_all(
        role_sum.reshape(features // roles * 2, rank + EXTRA, width),
        ("x", "zh", "zl"),
        split_axis=0,
        concat_axis=0,
        tiled=True,
    )
    piece = jnp.sum(pieces.astype(F32), axis=0)
    shares = lax.all_to_all(piece.T, ("zl", "core"), split_axis=0, concat_axis=0, tiled=True)
    shares = shares.reshape(quarters, share, rank + EXTRA)
    grad_v = shares[0, :, :rank]
    grad_u = shares[2, :, :rank].T
    grad_h = jnp.concatenate([shares[1, :, :rank], shares[3, :, :rank]], axis=1)
    grad_cb = shares[0, :, rank]
    grad_hb = shares[0, :per, rank + 1]
    grad_ow = shares[0, :per, rank + 2]

    local = scatter(touched, incidence, returned.reshape(samples, width), rows)
    parts = lax.all_to_all(
        local.reshape(roles, rows // roles, width), "role", split_axis=0, concat_axis=0, tiled=True
    )
    part = jnp.sum(parts.astype(F32), axis=0).astype(BF)
    table_grad = lax.all_gather(part, "role", axis=0, tiled=True).astype(F32)
    return (table_grad, grad_v, grad_u, grad_cb, grad_h, grad_hb, grad_ow)


def solution(mesh):
    fine = Mesh(mesh.devices.reshape(4, 4, 2, 2, 2), ("role", "x", "zh", "zl", "core"))
    dp = ("x", "zh", "zl", "core")
    everywhere = ("role",) + dp
    return jax.shard_map(
        body,
        mesh=fine,
        in_specs=(
            P(dp, None),
            P(dp, "role", None),
            P(dp, "role", None),
            P(dp, "role", None),
            P(),
            P(everywhere),
            P(),
            P(),
            P(),
            P(),
            P(),
            P(),
        ),
        out_specs=(
            P(dp, None),
            P(everywhere, None),
            P(None, everywhere),
            P(everywhere),
            P(everywhere, None),
            P(everywhere),
            P(everywhere),
        ),
        check_vma=False,
    )
```

time: 2380 us -> 238 us (0.10)
  waiting for transfers between devices: 1910 us -> 48.6 us
  other arithmetic: 156 us -> 7.69 us
  local copies, waits for them, and re-layouts: 147 us -> 23 us
  matrix products: 48.5 us -> 0 us
  Pallas kernels: 0 us -> 44.1 us
    reduce_scatter x3 -> x1, waiting for transfers between devices: 1830 us -> 0.02 us  [body(): lax.psum_scatter(chip_sum, 'role', scatter_dimension=0, tiled=True)]
    all_to_all x0 -> x3, blocking collectives: none -> 83 us  [the longest x1 44.3 us: body(): returned = lax.all_to_all(back, dp, split_axis=0, concat_axis=0, tiled=True)]
    unnamed x1 -> x0, other arithmetic: 68.6 us -> none
    scatter-add x1 -> x0, other arithmetic: 66.5 us -> none  [body(): local_grad = jnp.zeros((rows_shard, embed_width), jnp.float32).at[row_ids...]
    unnamed x1 -> x0, blocking collectives: 65.6 us -> none
    reshape x1 -> x6, local copies, waits for them, and re-layouts: 49.5 us -> 0.53 us  [the longest x2 0.24 us: spread(): values = values.reshape(features, quarters, per)]
    dot_general x15 -> x0, matrix products: 48.5 us -> none  [the longest x3 26.7 us: inner_rows(): lax.dot_general(left, right, (((0,), (0,)), ((), ())), preferred_element_...]
    gather x1 -> x0, local copies, waits for them, and re-layouts: 47.4 us -> none  [body(): picked = embedding_table[row_ids]]
  transfers between devices with their start and end apart: 6 -> 5, of which waited for: 5 -> 3; matrix products, arithmetic and copies ran while one was open for 1% -> 2% of each run, Pallas kernels for 0% -> 2%
where the time goes in v1:
time: 238 us; the launch traced here: 237 us
  blocking collectives  83 us (35%)
  waiting for transfers between devices  48.6 us (20%)
  Pallas kernels  44.1 us (19%)
  local copies, waits for them, and re-layouts  23 us (10%)
  starting transfers between devices  16.1 us (7%)
  between operations  14.2 us (6%)
  other arithmetic  7.69 us (3%)
    all_to_all x1, blocking collectives, body(): returned = lax.all_to_all(back, dp, split_axis=0, concat_axis=0, tiled=True)  44.3 us
    all_to_all x1, waiting for transfers between devices, body(): lax.all_to_all(pooled.reshape(features, batch, width), dp, split_axis=0,...  39.6 us
    all_to_all x1, blocking collectives, body(): lax.all_to_all(role_sum.reshape(features // roles * 2, rank + EXTRA, widt...  19.9 us
    unnamed x44, local copies, waits for them, and re-layouts  19.6 us
    pallas_call x1, Pallas kernels, dense(): pl.pallas_call(functools.partial(dense_kernel, scale), name='dense', in_s...  19 us
    all_to_all x1, blocking collectives, body(): lax.all_to_all(local.reshape(roles, rows // roles, width), 'role', split_...  18.8 us
    pallas_call x1, Pallas kernels, pool(): pl.pallas_call(pool_kernel, name='pool', grid_spec=pltpu.PrefetchScalarGr...  9.98 us
    pallas_call x1, Pallas kernels, gradients(): pl.pallas_call(gradients_kernel, name='gradients', grid_spec=pltpu.Prefet...  9.66 us
  transfers between devices with their start and end apart: 5, of which 3 were waited for; matrix products, arithmetic and copies ran while one was open for 2% of the time, Pallas kernels for 2%

profile of v1, /device:TPU:1, one launch (start us, length us, event | category | flops | bytes accessed | tf_op | source)
XLA Modules:
  0.0 236.8 jit_solution(17439635818894422372)
XLA Ops:
  7.2 1.2 copy-done.3
  8.4 1.1 copy-done.4
  9.5 1.1 copy-done.5
  10.7 0.7 copy-done.6
  11.4 10.0 %pool.1 = (bf16[12288,128]{1,0:T(8,128)(2,1)S(1)}, bf16[96,128,128]{2,1,0:T(8,128)(2,1)S(1)}) custom-call(s32[16,96]{1,0:T(8,128)S(1)} %bitcast.35, bf16[4096,128]{1,0:T(8,128)(2,1)S(1)} %copy-done.3, s32[16,12288]{1,0:T(8,128)S(1)} %bitcast.33, s32[16,12288]{1,0:T(8,128)S(1)} %bitcast.34), custom_call_target="tpu_custom_call" | custom-call | tf_op jit(solution)/shard_map/pool/pallas_call | solution.py:57
  21.4 1.6 copy-done
  23.0 9.6 %all-to-all-start = ((bf16[32,384,128]{2,1,0:T(8,128)(2,1)}), bf16[32,384,128]{2,1,0:T(8,128)(2,1)}, u32[]{:S(2)}, u32[]{:S(2)}) async-start(bf16[32,384,128]{2,1,0:T(8,128)(2,1)} %bitcast.32), calls=%async_computation | async-start | bytes 6291456 | tf_op jit(solution)/shard_map/all_to_all | solution.py:424
  32.6 0.0 reduce-scatter.2.cloned.1.call-start
  32.7 0.1 reshape.79.labels
  32.8 39.6 %all-to-all-done.received = bf16[32,384,128]{2,1,0:T(8,128)(2,1)} async-done(((bf16[32,384,128]{2,1,0:T(8,128)(2,1)}), bf16[32,384,128]{2,1,0:T(8,128)(2,1)}, u32[]{:S(2)}, u32[]{:S(2)}) %all-to-all-start) | async-done | bytes 3145760 | tf_op jit(solution)/shard_map/all_to_all | solution.py:424
  72.5 1.6 copy-done.1
  74.1 1.6 copy-done.2
  75.7 19.0 %dense.1 = (bf16[32,384,128]{2,1,0:T(8,128)(2,1)}, bf16[384,4096]{1,0:T(8,128)(2,1)}, bf16[384,4096]{1,0:T(8,128)(2,1)}, bf16[384,4096]{1,0:T(8,128)(2,1)}, bf16...) custom-call(s32[32]{0:T(128)S(1)} %copy-done.10, ...), custom_call_target="tpu_custom_call" | custom-call | tf_op jit(solution)/shard_map/dense/pallas_call | solution.py:280
  94.7 0.7 copy-done.14
  95.4 0.7 copy-done.16
  96.1 0.7 copy-done.18
  96.8 0.1 reshape.76
  97.0 0.1 reshape.81
  97.1 0.1 reshape.74
  97.2 0.1 reshape.80
  97.3 0.1 fusion.4.extra
  97.4 1.9 copy-done.11
  99.3 1.9 copy-done.12
  101.2 1.9 copy-done.13
  103.1 1.0 copy-done.15
  104.1 0.9 copy-done.17
  105.0 0.9 copy-done.19
  105.9 9.7 %gradients.1 = (bf16[32,2,272,128]{3,2,1,0:T(8,128)(2,1)S(1)}, bf16[32,2,272,128]{3,2,1,0:T(8,128)(2,1)S(1)}) custom-call(s32[1]{0:T(128)} %bitcast.12.core, bf16[384,4096]{1,0:T(8,128)(2,1)S(1)} %copy-done.11, bf16[384,4096]{1,0:T(8,128)(2,1)S(1)} %copy-done.12, bf16[384,4096]{1,0:T(8,128)(2,1)S(1)} %copy-done.13, bf16[384,256]{1,0:T(8,128)(2,1)S(1)} %copy-done.17, ...), custom_call_target="tpu_custom_call" | custom-call | flops 3221225472 | bytes 18874368 | tf_op jit(solution)/shard_map/gradients/pallas_call | solution.py:364
  115.6 0.6 collective-permute-start
  116.2 7.2 %collective-permute-done = bf16[32,2,272,128]{3,2,1,0:T(8,128)(2,1)S(1)} collective-permute-done((bf16[32,2,272,128]{3,2,1,0:T(8,128)(2,1)S(1)}, bf16[32,2,272,128]{3,2,1,0:T(8,128)(2,1)S(1)}, u32[]{:S(2)}, u32[]{:S(2)}) %collective-permute-start) | collective-permute-done | bytes 4456480 | tf_op jit(solution)/shard_map/ppermute | solution.py:456
  123.3 3.2 %add_convert_fusion = bf16[32,2,272,128]{3,2,1,0:T(8,128)(2,1)} fusion(bf16[32,2,272,128]{3,2,1,0:T(8,128)(2,1)S(1)} %collective-permute-done, bf16[32,2,272,128]{3,2,1,0:T(8,128)(2,1)S(1)} %get-tuple-element.33), kind=kLoop, calls=%fused_computation | loop fusion | flops 8912896 | bytes 13369344 | tf_op jit(solution)/shard_map/convert_element_type | solution.py:457
  126.5 0.0 reduce-scatter.2.cloned.1.call-update
  126.5 0.0 all-gather.2.cloned.1.call-start
  126.6 44.3 %all_to_all.29 = bf16[32,384,128]{2,1,0:T(8,128)(2,1)S(1)} all-to-all(bf16[32,384,128]{2,1,0:T(8,128)(2,1)} %get-tuple-element.23), channel_id=1, replica_groups=mesh['role'=4,'x'=4,'zh'=2,'zl'=2,'core'=2] {'x','zh','zl','core'}, dimensions={0} | all-to-all | bytes 6291456 | tf_op jit(solution)/shard_map/all_to_all | solution.py:439
  170.9 5.5 %scatter.1 = bf16[4096,128]{1,0:T(8,128)(2,1)S(1)} custom-call(s32[16,96]{1,0:T(8,128)S(1)} %bitcast.36, bf16[96,128,128]{2,1,0:T(8,128)(2,1)S(1)} %get-tuple-element.21.incidence, bf16[12288,128]{1,0:T(8,128)(2,1)S(1)} %bitcast.30), custom_call_target="tpu_custom_call" | custom-call | tf_op jit(solution)/shard_map/scatter/pallas_call | solution.py:113
  176.4 18.8 %all_to_all.30 = bf16[4,1024,128]{2,1,0:T(8,128)(2,1)S(1)} all-to-all(bf16[4,1024,128]{2,1,0:T(8,128)(2,1)S(1)} %bitcast.31), channel_id=1, replica_groups=mesh['role'=4,'x'=4,'zh'=2,'zl'=2,'core'=2] {'role'}, dimensions={0} | all-to-all | bytes 2097152 | tf_op jit(solution)/shard_map/all_to_all | solution.py:477
  195.2 0.9 reduce_sum.21
  196.1 0.0 reduce-scatter.2.cloned.1.call-done
  196.1 19.9 %all_to_all.31 = bf16[16,272,128]{2,1,0:T(8,128)(2,1)S(1)} all-to-all(bf16[16,272,128]{2,1,0:T(8,128)(2,1)} %bitcast.39), channel_id=1, replica_groups=mesh['role'=4,'x'=4,'zh'=2,'zl'=2,'core'=2] {'x','zh','zl'}, dimensions={0} | all-to-all | bytes 2228224 | tf_op jit(solution)/shard_map/all_to_all | solution.py:459
  216.0 0.2 convert_reduce_fusion
  216.2 0.8 copy.29
  217.0 5.9 %all-to-all-start.4 = ((f32[4,32,272]{2,1,0:T(8,128)}), f32[4,32,272]{2,1,0:T(8,128)S(1)}, u32[]{:S(2)}, u32[]{:S(2)}) async-start(f32[4,32,272]{2,1,0:T(8,128)} %bitcast.16), calls=%async_computation.5 | async-start | bytes 393216 | tf_op jit(solution)/shard_map/all_to_all | solution.py:467
  222.9 2.7 %convert_element_type.23 = f32[4096,128]{1,0:T(8,128)} convert(bf16[4096,128]{1,0:T(8,128)(2,1)} %all-gather.2.cloned.1.call-done) | non-fusion elementwise | flops 524288 | bytes 3145728 | tf_op jit(solution)/shard_map/convert_element_type | solution.py:481
  225.5 1.8 all-to-all-done.4
  227.3 0.6 slice_bitcast_fusion.1
  228.0 0.6 pad_maximum_fusion
  228.6 0.6 slice_reduce_fusion
  229.2 0.7 slice_reduce_fusion.1
  (35 shorter events, 0.2 us)
Async XLA Ops:
  7.2 1.2 copy-start.3
  8.4 1.1 copy-start.4
  9.5 1.1 copy-start.5
  10.7 0.7 copy-start.6
  21.3 1.6 copy-start
  23.0 9.7 %copy-start.21 = (bf16[512]{0:T(512)(128)(2,1)S(1)}, bf16[512]{0:T(512)(128)(2,1)}, u32[]{:S(2)}) copy-start(bf16[512]{0:T(512)(128)(2,1)} %param.23) | copy-start | bytes 3076
  23.0 9.7 %copy-start.20 = (s32[384]{0:T(512)S(1)}, s32[384]{0:T(512)}, u32[]{:S(2)}) copy-start(s32[384]{0:T(512)} %param.17) | copy-start | bytes 4612
  23.0 49.5 %copy-start.8 = (f32[4096]{0:T(1024)S(1)}, f32[4096]{0:T(1024)}, u32[]{:S(2)}) copy-start(f32[4096]{0:T(1024)} %param.20) | copy-start | bytes 49156
  23.0 49.5 %copy-start.9 = (f32[512]{0:T(512)S(1)}, f32[512]{0:T(512)}, u32[]{:S(2)}) copy-start(f32[512]{0:T(512)} %param.22) | copy-start | bytes 6148
  23.0 49.5 %copy-start.10 = (s32[32]{0:T(128)S(1)}, s32[32]{0:T(128)}, u32[]{:S(2)}) copy-start(s32[32]{0:T(128)} %fmap.1) | copy-start | bytes 388
  23.0 49.5 %all-to-all-start = ((bf16[32,384,128]{2,1,0:T(8,128)(2,1)}), bf16[32,384,128]{2,1,0:T(8,128)(2,1)}, u32[]{:S(2)}, u32[]{:S(2)}) async-start(bf16[32,384,128]{2,1,0:T(8,128)(2,1)} %bitcast.32), calls=%async_computation | async-start | bytes 6291456 | tf_op jit(solution)/shard_map/all_to_all | solution.py:424
  32.6 163.5 %reduce-scatter.2.cloned.1.call-start = ((), (), s32[]{:S(2)}) async-start(), calls=%async_computation.7 | async-start | bytes 5570560 | tf_op jit(solution)/shard_map/reduce_scatter | solution.py:458
  72.5 1.6 copy-start.1
  74.1 1.6 copy-start.2
  94.7 0.7 copy-start.14
  95.4 0.7 copy-start.16
  96.1 0.7 copy-start.18
  97.4 1.9 copy-start.11
  99.3 1.9 copy-start.12
  101.2 1.9 copy-start.13
  103.1 1.0 copy-start.15
  104.1 0.9 copy-start.17
  105.0 0.9 copy-start.19
  115.6 7.7 %collective-permute-start = (bf16[32,2,272,128]{3,2,1,0:T(8,128)(2,1)S(1)}, bf16[32,2,272,128]{3,2,1,0:T(8,128)(2,1)S(1)}, u32[]{:S(2)}, u32[]{:S(2)}) collective-permute-start(bf16[32,2,272,128]{3,2,1,0:T(8,128)(2,1)S(1)} %get-tuple-element.34), channel_id=1, source_target_pairs={{0,1},{1,0},{2,3},{3,2},{4,5},{5,4},{6,7},{7,6},{8,9},{9,8},{10,11... | collective-permute-start | bytes 13369352 | tf_op jit(solution)/shard_map/ppermute | solution.py:456
  126.5 96.3 %all-gather.2.cloned.1.call-start = ((), (), s32[]{:S(2)}) async-start(), calls=%async_computation.6 | async-start | bytes 1310720 | tf_op jit(solution)/shard_map/all_gather | solution.py:481
  126.6 44.3 %copy-start.7 = (s32[1,96,16]{1,2,0:T(8,128)S(1)}, s32[1,96,16]{1,2,0:T(8,128)}, u32[]{:S(2)}) copy-start(s32[1,96,16]{1,2,0:T(8,128)} %param.13) | copy-start | bytes 18436
  217.0 10.3 %all-to-all-start.4 = ((f32[4,32,272]{2,1,0:T(8,128)}), f32[4,32,272]{2,1,0:T(8,128)S(1)}, u32[]{:S(2)}, u32[]{:S(2)}) async-start(f32[4,32,272]{2,1,0:T(8,128)} %bitcast.16), calls=%async_computation.5 | async-start | bytes 393216 | tf_op jit(solution)/shard_map/all_to_all | solution.py:467
Sparse Core Ops, SparseCore 0:
  126.7 47.7 reduce-scatter.1
  196.2 19.6 all-gather.1

commit v2 on v1

--- a/solution.py
+++ b/solution.py
@@ -13,6 +13,8 @@
 STEP_TILES = 8
 WIDE = 512
 EXTRA = 16
+ORDER = (2, 1, 3, 0)
+VMEM = 60 << 20
 
 BF = jnp.bfloat16
 F32 = jnp.float32
@@ -75,57 +77,104 @@
             jax.ShapeDtypeStruct((samples, width), BF),
             jax.ShapeDtypeStruct((tiles, tile, tile), BF),
         ],
-        compiler_params=pltpu.CompilerParams(vmem_limit_bytes=24 << 20),
+        compiler_params=pltpu.CompilerParams(vmem_limit_bytes=VMEM),
     )(touched, table, index, count)
 
 
-def scatter_kernel(touched, incidence, grad, out, *sums):
-    step = pl.program_id(0)
-    tile = incidence.shape[1]
-
-    @pl.when(step == 0)
-    def _():
-        for acc in sums:
-            acc[...] = jnp.zeros_like(acc)
-
-    for i in range(STEP_TILES):
-        t = step * STEP_TILES + i
-        product = jnp.dot(
-            incidence[i], grad[pl.ds(i * tile, tile), :], preferred_element_type=F32
+def scatter_kernel(touched, role, incidence, grad, out, *scratch):
+    sums, (tiles_in, grads_in, tile_sems, grad_sems) = scratch[:-4], scratch[-4:]
+    tiles, tile, _ = incidence.shape
+    chunks, rows, _ = out.shape
+    steps = tiles // STEP_TILES
+
+    def loads(step):
+        part = pl.ds(step * STEP_TILES, STEP_TILES)
+        span = pl.ds(step * STEP_TILES * tile, STEP_TILES * tile)
+        return (
+            pltpu.make_async_copy(incidence.at[part], tiles_in.at[part], tile_sems.at[step]),
+            pltpu.make_async_copy(grad.at[span], grads_in.at[span], grad_sems.at[step]),
         )
-        for k in range(touched.shape[0]):
-            acc = sums[k % len(sums)]
-            rows = pl.ds(pl.multiple_of(touched[k, t] * BLK, BLK), BLK)
-            acc[rows, :] += product[k * BLK : (k + 1) * BLK]
-
-    @pl.when(step == pl.num_programs(0) - 1)
-    def _():
-        total = sums[0][...]
+
+    for step in range(steps):
+        for copy in loads(step):
+            copy.start()
+    for acc in sums:
+        acc[...] = jnp.zeros_like(acc)
+
+    @pl.loop(0, steps)
+    def _(step):
+        for copy in loads(step):
+            copy.wait()
+        for i in range(STEP_TILES):
+            t = step * STEP_TILES + i
+            product = jnp.dot(
+                tiles_in[t], grads_in[pl.ds(t * tile, tile), :], preferred_element_type=F32
+            )
+            for k in range(touched.shape[0]):
+                acc = sums[k % len(sums)]
+                place = pl.ds(pl.multiple_of(touched[k, t] * BLK, BLK), BLK)
+                acc[place, :] += product[k * BLK : (k + 1) * BLK]
+
+    for i, offset in enumerate(ORDER):
+        first = lax.rem(role[0] + offset, chunks) * rows
+        place = pl.ds(pl.multiple_of(first, rows), rows)
+        total = sums[0][place, :]
         for acc in sums[1:]:
-            total = total + acc[...]
-        out[...] = total.astype(out.dtype)
-
-
-def scatter(touched, incidence, grad, rows):
+            total = total + acc[place, :]
+        out[i] = total.astype(out.dtype)
+
+
+def scatter(touched, role, incidence, grad, rows, chunks):
     tiles, tile, _ = incidence.shape
     width = grad.shape[1]
-    span = STEP_TILES * tile
+    steps = tiles // STEP_TILES
+    smem = pl.BlockSpec(memory_space=pltpu.SMEM)
+    hbm = pl.BlockSpec(memory_space=pltpu.HBM)
     return pl.pallas_call(
         scatter_kernel,
         name="scatter",
-        grid_spec=pltpu.PrefetchScalarGridSpec(
-            num_scalar_prefetch=1,
-            grid=(tiles // STEP_TILES,),
-            in_specs=[
-                pl.BlockSpec((STEP_TILES, tile, tile), lambda s, _: (s, 0, 0)),
-                pl.BlockSpec((span, width), lambda s, _: (s, 0)),
-            ],
-            out_specs=pl.BlockSpec((rows, width), lambda s, _: (0, 0)),
-            scratch_shapes=[pltpu.VMEM((rows, width), F32)] * 4,
-        ),
-        out_shape=jax.ShapeDtypeStruct((rows, width), BF),
-        compiler_params=pltpu.CompilerParams(vmem_limit_bytes=24 << 20),
-    )(touched, incidence, grad)
+        in_specs=[smem, smem, hbm, hbm],
+        out_specs=pl.BlockSpec(memory_space=pltpu.VMEM),
+        out_shape=jax.ShapeDtypeStruct((chunks, rows // chunks, width), BF),
+        scratch_shapes=[pltpu.VMEM((rows, width), F32)] * 4
+        + [
+            pltpu.VMEM(incidence.shape, BF),
+            pltpu.VMEM(grad.shape, BF),
+            pltpu.SemaphoreType.DMA((steps,)),
+            pltpu.SemaphoreType.DMA((steps,)),
+        ],
+        compiler_params=pltpu.CompilerParams(vmem_limit_bytes=VMEM),
+        cost_estimate=pl.CostEstimate(flops=1 << 33, bytes_accessed=8 << 20, transcendentals=0),
+    )(touched, role, incidence, grad)
+
+
+def spread_kernel(role, own, following, opposite_a, opposite_b, preceding, out):
+    rows = own.shape[0]
+    half = rows // 2
+    chunks = out.shape[0] // rows
+
+    def place(offset, size, piece):
+        first = lax.rem(role[0] + offset, chunks) * rows
+        out[pl.ds(pl.multiple_of(first, rows) + size, piece.shape[0]), :] = piece[...].astype(F32)
+
+    place(0, 0, own)
+    place(1, 0, following)
+    place(2, 0, opposite_a)
+    place(2, half, opposite_b)
+    place(3, 0, preceding)
+
+
+def spread_rows(role, pieces, chunks):
+    rows, width = pieces[0].shape
+    vmem = pl.BlockSpec(memory_space=pltpu.VMEM)
+    return pl.pallas_call(
+        spread_kernel,
+        name="spread_rows",
+        in_specs=[pl.BlockSpec(memory_space=pltpu.SMEM)] + [vmem] * 5,
+        out_specs=vmem,
+        out_shape=jax.ShapeDtypeStruct((chunks * rows, width), F32),
+        compiler_params=pltpu.CompilerParams(vmem_limit_bytes=16 << 20),
+    )(role, *pieces)
 
 
 def dense_kernel(
@@ -140,7 +189,6 @@
     hidden_bias,
     out_weight,
     back,
-    inter_out,
     crossed_out,
     proj_out,
     low_out,
@@ -149,6 +197,7 @@
     cross_bias_grad,
     hidden_bias_grad,
     out_weight_grad,
+    slot_of,
     inter,
     crossed,
     proj_low,
@@ -159,10 +208,10 @@
     h,
     hidden,
     low_sum,
-    slot_of,
     in_sems,
     weight_sems,
-    out_sems,
+    crossed_sems,
+    proj_sems,
     back_sems,
 ):
     features, batch, width = received.shape
@@ -188,8 +237,6 @@
     hidden[...] = jnp.broadcast_to(hidden_bias[...], hidden.shape)
     for copy in loads:
         copy.wait()
-    inter_copy = pltpu.make_async_copy(inter, inter_out, out_sems.at[0])
-    inter_copy.start()
     weights[0].wait()
 
     @pl.loop(0, blocks)
@@ -213,8 +260,15 @@
         crossed[:, cols] = product
         hidden[...] += jnp.dot(product, h[cols, :], preferred_element_type=F32)
 
-    crossed_copy = pltpu.make_async_copy(crossed, crossed_out, out_sems.at[1])
-    crossed_copy.start()
+    stores = []
+
+    def store(source, f, target, sem):
+        copy = pltpu.make_async_copy(source.at[:, pl.ds(f * width, width)], target, sem)
+        copy.start()
+        stores.append(copy)
+
+    for f in range(features):
+        store(crossed, f, crossed_out.at[f], crossed_sems.at[f])
     hidden_bias_grad[...] = jnp.zeros_like(hidden_bias_grad)
     out_weight_grad[...] = jnp.zeros_like(out_weight_grad)
     chunk = 64
@@ -247,25 +301,17 @@
         low_sum[...] += nt(rounded, u[:, cols])
         held[:, cols] = d_crossed * (held[:, cols] + 1.0)
 
-    proj_copy = pltpu.make_async_copy(proj_low, proj_out, out_sems.at[2])
-    proj_copy.start()
+    for f in range(features):
+        store(proj_low, f, proj_out.at[f], proj_sems.at[f])
     low_grad_out[...] = low_sum[...].astype(BF)
-    stores = []
     for b in range(blocks):
         cols = pl.ds(b * WIDE, WIDE)
         d_inter[:, cols] = (held[:, cols] + nt(low_grad_out[...], v[cols, :])).astype(BF)
         for i in range(per_block):
             f = b * per_block + i
-            copy = pltpu.make_async_copy(
-                d_inter.at[:, pl.ds(f * width, width)], back.at[slot_of[f]], back_sems.at[f]
-            )
-            copy.start()
-            stores.append(copy)
+            store(d_inter, f, back.at[slot_of[f]], back_sems.at[f])
     for copy in stores:
         copy.wait()
-    inter_copy.wait()
-    crossed_copy.wait()
-    proj_copy.wait()
 
 
 def dense(fmap, received, labels, v, u, cross_bias, h, hidden_bias, out_weight, scale):
@@ -275,24 +321,23 @@
     units = h.shape[1]
     vmem = pl.BlockSpec(memory_space=pltpu.VMEM)
     smem = pl.BlockSpec(memory_space=pltpu.SMEM)
-    hbm = pl.BlockSpec(memory_space=pl.ANY)
-    wide = jax.ShapeDtypeStruct((batch, total_width), BF)
+    hbm = pl.BlockSpec(memory_space=pltpu.HBM)
     return pl.pallas_call(
         functools.partial(dense_kernel, scale),
         name="dense",
         in_specs=[smem, hbm, vmem, hbm, hbm, vmem, hbm, vmem, vmem],
-        out_specs=[hbm, hbm, hbm, hbm, vmem, vmem, vmem, vmem, vmem, vmem],
+        out_specs=[hbm, hbm, hbm, vmem, vmem, vmem, vmem, vmem, vmem, smem],
         out_shape=[
             jax.ShapeDtypeStruct(received.shape, BF),
-            wide,
-            wide,
-            wide,
+            jax.ShapeDtypeStruct(received.shape, BF),
+            jax.ShapeDtypeStruct(received.shape, BF),
             jax.ShapeDtypeStruct((batch, rank), BF),
             jax.ShapeDtypeStruct((batch, rank), BF),
             jax.ShapeDtypeStruct((batch, units), BF),
             jax.ShapeDtypeStruct((1, total_width), F32),
             jax.ShapeDtypeStruct((1, units), F32),
             jax.ShapeDtypeStruct((1, units), F32),
+            jax.ShapeDtypeStruct((features,), jnp.int32),
         ],
         scratch_shapes=[
             pltpu.VMEM((batch, total_width), BF),
@@ -305,31 +350,45 @@
             pltpu.VMEM(h.shape, BF),
             pltpu.VMEM((batch, units), F32),
             pltpu.VMEM((batch, rank), F32),
-            pltpu.SMEM((features,), jnp.int32),
             pltpu.SemaphoreType.DMA((features,)),
             pltpu.SemaphoreType.DMA((3,)),
-            pltpu.SemaphoreType.DMA((3,)),
+            pltpu.SemaphoreType.DMA((features,)),
+            pltpu.SemaphoreType.DMA((features,)),
             pltpu.SemaphoreType.DMA((features,)),
         ],
-        compiler_params=pltpu.CompilerParams(vmem_limit_bytes=48 << 20),
+        compiler_params=pltpu.CompilerParams(vmem_limit_bytes=VMEM),
     )(fmap, received, labels, v, u, cross_bias, h, hidden_bias, out_weight)
 
 
 def gradients_kernel(
-    core, inter, crossed, proj, low, low_grad, d_hidden, extra, keep, send, low_t, low_grad_t, d_hidden_t
+    place,
+    slot_of,
+    inter_a,
+    inter_b,
+    crossed,
+    proj,
+    low,
+    low_grad,
+    d_hidden,
+    extra,
+    *rest,
 ):
+    outs, (low_t, low_grad_t, d_hidden_t) = rest[:-3], rest[-3:]
+    parts = len(ORDER)
     @pl.when(pl.program_id(0) == 0)
     def _():
         low_t[...] = low[...].astype(F32).T.astype(BF)
         low_grad_t[...] = low_grad[...].astype(F32).T.astype(BF)
         d_hidden_t[...] = d_hidden[...].astype(F32).T.astype(BF)
 
-    first = core[0] == 0
     rank = low_t.shape[0]
-    features, _, _, width = keep.shape
-    of_v = jnp.dot(low_grad_t[...], inter[...], preferred_element_type=F32).astype(BF)
-    of_u = jnp.dot(low_t[...], proj[...], preferred_element_type=F32).astype(BF)
-    of_h = jnp.dot(d_hidden_t[...], crossed[...], preferred_element_type=F32).astype(BF)
+    features, _, _, width = outs[0].shape
+    x = jnp.concatenate([inter_a[0], inter_b[0]], axis=1)
+    c = jnp.concatenate([crossed[0], crossed[1]], axis=1)
+    p = jnp.concatenate([proj[0], proj[1]], axis=1)
+    of_v = jnp.dot(low_grad_t[...], x, preferred_element_type=F32).astype(BF)
+    of_u = jnp.dot(low_t[...], p, preferred_element_type=F32).astype(BF)
+    of_h = jnp.dot(d_hidden_t[...], c, preferred_element_type=F32).astype(BF)
     nothing = jnp.zeros((EXTRA, width), BF)
 
     def fill(one, other):
@@ -344,53 +403,111 @@
             other[i, 1, pl.ds(0, rank), :] = of_h[rank:, lanes]
             other[i, 1, pl.ds(rank, EXTRA), :] = nothing
 
-    @pl.when(first)
-    def _():
-        fill(keep, send)
-
-    @pl.when(jnp.logical_not(first))
-    def _():
-        fill(send, keep)
-
-
-def gradients(core, inter, crossed, proj, low, low_grad, d_hidden, extra, width):
-    batch, total_width = inter.shape
+    share = pl.num_programs(0) // parts
+    first = place[0] == 0
+    for part in range(parts):
+        now = pl.program_id(0) // share == part
+
+        @pl.when(jnp.logical_and(now, first))
+        def _(part=part):
+            fill(outs[part], outs[parts + part])
+
+        @pl.when(jnp.logical_and(now, jnp.logical_not(first)))
+        def _(part=part):
+            fill(outs[parts + part], outs[part])
+
+
+def gradients(place, slot_of, received, crossed, proj, low, low_grad, d_hidden, extra):
+    features, batch, width = received.shape
     rank, units = low.shape[1], d_hidden.shape[1]
-    features = total_width // width
     pair = 2
-    wide = pl.BlockSpec((batch, pair * width), lambda s, _: (0, s))
-    half = jax.ShapeDtypeStruct((features, 2, rank + EXTRA, width), BF)
-    half_spec = pl.BlockSpec((pair, 2, rank + EXTRA, width), lambda s, _: (s, 0, 0, 0))
-    return pl.pallas_call(
+    pairs = features // pair
+    share = pairs // len(ORDER)
+
+    def pair_of(s, place):
+        part = s // share
+        offset = jnp.where(part == 0, ORDER[0], jnp.where(part == 1, ORDER[1], 0))
+        offset = jnp.where(part == 2, ORDER[2], offset)
+        return lax.rem(place[1] + offset, len(ORDER)) * share + lax.rem(s, share)
+
+    one = pl.BlockSpec((1, batch, width), lambda s, a, m: (m[pair_of(s, a) * pair], 0, 0))
+    two = pl.BlockSpec((1, batch, width), lambda s, a, m: (m[pair_of(s, a) * pair + 1], 0, 0))
+    both = pl.BlockSpec((pair, batch, width), lambda s, a, m: (pair_of(s, a), 0, 0))
+    part = jax.ShapeDtypeStruct((features // len(ORDER), 2, rank + EXTRA, width), BF)
+
+    def part_spec(i):
+        return pl.BlockSpec(
+            (pair, 2, rank + EXTRA, width),
+            lambda s, a, m: (jnp.clip(s - i * share, 0, share - 1), 0, 0, 0),
+        )
+
+    specs = [part_spec(i) for i in range(len(ORDER))] * 2
+    outs = pl.pallas_call(
         gradients_kernel,
         name="gradients",
         grid_spec=pltpu.PrefetchScalarGridSpec(
-            num_scalar_prefetch=1,
-            grid=(features // pair,),
+            num_scalar_prefetch=2,
+            grid=(pairs,),
             in_specs=[
-                wide,
-                wide,
-                wide,
-                pl.BlockSpec((batch, rank), lambda s, _: (0, 0)),
-                pl.BlockSpec((batch, rank), lambda s, _: (0, 0)),
-                pl.BlockSpec((batch, units), lambda s, _: (0, 0)),
-                pl.BlockSpec((pair, EXTRA, width), lambda s, _: (s, 0, 0)),
+                one,
+                two,
+                both,
+                both,
+                pl.BlockSpec((batch, rank), lambda s, a, m: (0, 0)),
+                pl.BlockSpec((batch, rank), lambda s, a, m: (0, 0)),
+                pl.BlockSpec((batch, units), lambda s, a, m: (0, 0)),
+                pl.BlockSpec((pair, EXTRA, width), lambda s, a, m: (pair_of(s, a), 0, 0)),
             ],
-            out_specs=[half_spec, half_spec],
+            out_specs=specs,
             scratch_shapes=[
                 pltpu.VMEM((rank, batch), BF),
                 pltpu.VMEM((rank, batch), BF),
                 pltpu.VMEM((units, batch), BF),
             ],
         ),
-        out_shape=[half, half],
-        compiler_params=pltpu.CompilerParams(vmem_limit_bytes=24 << 20),
+        out_shape=[part] * len(specs),
+        compiler_params=pltpu.CompilerParams(vmem_limit_bytes=VMEM),
         cost_estimate=pl.CostEstimate(
-            flops=2 * batch * total_width * (2 * rank + units),
+            flops=2 * batch * features * width * (2 * rank + units),
             bytes_accessed=18 << 20,
             transcendentals=0,
         ),
-    )(core, inter, crossed, proj, low, low_grad, d_hidden, extra)
+    )(place, slot_of, received, received, crossed, proj, low, low_grad, d_hidden, extra)
+    return outs[: len(ORDER)], outs[len(ORDER) :]
+
+
+def neighbours(axis):
+    size = lax.axis_size(axis)
+    up = [(i, (i + 1) % size) for i in range(size)]
+    down = [(i, (i - 1) % size) for i in range(size)]
+    return (
+        lambda value: lax.ppermute(value, axis, up),
+        lambda value: lax.ppermute(value, axis, down),
+    )
+
+
+def add(*terms):
+    total = terms[0].astype(F32)
+    for term in terms[1:]:
+        total = total + term.astype(F32)
+    return total.astype(BF)
+
+
+def ring_sum(axis, opposite, following, preceding, own, between=lambda value: value):
+    up, down = neighbours(axis)
+    passed_down, passed_up = down(opposite[0]), up(opposite[1])
+    direct_down, direct_up = down(preceding[1]), up(following[0])
+    passed_down, passed_up = between((passed_down, passed_up))
+    last_down = down(add(preceding[0], passed_down))
+    last_up = up(add(following[1], passed_up))
+    return add(own[0], direct_up, last_down), add(own[1], last_up, direct_down)
+
+
+def ring_spread(axis, own):
+    up, down = neighbours(axis)
+    preceding, following = up(own), down(own)
+    half = own.shape[0] // 2
+    return own, following, down(following[:half]), up(preceding[half:]), preceding
 
 
 def body(
@@ -418,13 +535,14 @@
     roles = lax.axis_size("role")
     total = roles * lax.axis_size(dp) * batch
     core = lax.axis_index("core")
+    role = lax.axis_index("role")
 
     touched = touched_blocks[0].T
     pooled, incidence = pool(touched, embedding_table, bag_index[0].T, bag_count[0].T, tile)
     received = lax.all_to_all(
         pooled.reshape(features, batch, width), dp, split_axis=0, concat_axis=0, tiled=True
     )
-    back, inter, crossed, proj, low, low_grad, d_hidden, cross_g, hidden_g, out_g = dense(
+    back, crossed, proj, low, low_grad, d_hidden, cross_g, hidden_g, out_g, slot_of = dense(
         feature_map,
         received,
         labels.reshape(batch, 1),
@@ -449,15 +567,27 @@
     extra = jnp.concatenate(
         [cross_g.reshape(features, 1, width), spread(hidden_g), spread(out_g)], axis=1
     )
-    extra = jnp.pad(extra, ((0, 0), (0, EXTRA - 3), (0, 0))).astype(BF)
+    extra = jnp.pad(extra, ((0, 0), (0, EXTRA - 3), (0, 0)))
+    swap = [(0, 1), (1, 0)]
+    extra = jnp.where(core == 0, extra + lax.ppermute(extra, "core", swap), 0.0).astype(BF)
     keep, send = gradients(
-        core.reshape(1), inter, crossed, proj, low, low_grad, d_hidden, extra, width
+        jnp.stack([core, role]), slot_of, received, crossed, proj, low, low_grad, d_hidden, extra
     )
-    other = lax.ppermute(send, "core", [(0, 1), (1, 0)])
-    chip_sum = (keep.astype(F32) + other.astype(F32)).astype(BF)
-    role_sum = lax.psum_scatter(chip_sum, "role", scatter_dimension=0, tiled=True)
+    each = features // roles
+    halves = []
+    for mine, sent in zip(keep, send):
+        other = lax.ppermute(sent, "core", swap)
+        cuts = (slice(0, each // 2), slice(each // 2, each))
+        halves.append([add(mine[cut], other[cut]) for cut in cuts])
+
+    def after_return(values):
+        nonlocal returned
+        values, returned = lax.optimization_barrier((values, returned))
+        return values
+
+    role_sum = jnp.concatenate(ring_sum("role", *halves, after_return), axis=0)
     pieces = lax.all_to_all(
-        role_sum.reshape(features // roles * 2, rank + EXTRA, width),
+        role_sum.reshape(each * 2, rank + EXTRA, width),
         ("x", "zh", "zl"),
         split_axis=0,
         concat_axis=0,
@@ -473,12 +603,12 @@
     grad_hb = shares[0, :per, rank + 1]
     grad_ow = shares[0, :per, rank + 2]
 
-    local = scatter(touched, incidence, returned.reshape(samples, width), rows)
-    parts = lax.all_to_all(
-        local.reshape(roles, rows // roles, width), "role", split_axis=0, concat_axis=0, tiled=True
-    )
-    part = jnp.sum(parts.astype(F32), axis=0).astype(BF)
-    table_grad = lax.all_gather(part, "role", axis=0, tiled=True).astype(F32)
+    where = role.reshape(1)
+    local = scatter(touched, where, incidence, returned.reshape(samples, width), rows, roles)
+    middle = rows // roles // 2
+    halves = [[local[i, :middle], local[i, middle:]] for i in range(roles)]
+    part = jnp.concatenate(ring_sum("role", *halves), axis=0)
+    table_grad = spread_rows(where, ring_spread("role", part), roles)
     return (table_grad, grad_v, grad_u, grad_cb, grad_h, grad_hb, grad_ow)
 
 

time: 238 us -> 229 us (0.962)
  blocking collectives: 83 us -> 0 us
  waiting for transfers between devices: 48.6 us -> 87.3 us
  starting transfers between devices: 16.1 us -> 53.3 us
  Pallas kernels: 44.1 us -> 62 us
  between operations: 14.2 us -> 0.96 us
  local copies, waits for them, and re-layouts: 23 us -> 10.7 us
  other arithmetic: 7.69 us -> 13 us
    all_to_all x3 -> x0, blocking collectives: 83 us -> none  [the longest x1 44.3 us: body(): returned = lax.all_to_all(back, dp, split_axis=0, concat_axis=0, tiled=True)]
    ppermute x1 -> x21, waiting for transfers between devices: 7.16 us -> 45.9 us  [the longest x8 39.4 us: neighbours(): lax.ppermute(value, axis, up)]
    ppermute x1 -> x21, starting transfers between devices: 0.56 us -> 20.2 us  [the longest x8 16.2 us: neighbours(): lax.ppermute(value, axis, down)]
    unnamed x44 -> x24, local copies, waits for them, and re-layouts: 19.6 us -> 4.26 us
    all_to_all x0 -> x2, starting transfers between devices: none -> 11.4 us  [the longest x1 6.41 us: body(): lax.all_to_all(role_sum.reshape(each * 2, rank + EXTRA, width), ('x', 'zh...]
    pallas_call x1, Pallas kernels: 9.66 us -> 18.2 us  [gradients(): pl.pallas_call(gradients_kernel, name='gradients', grid_spec=pltpu.Prefet...]
    all_to_all x1, starting transfers between devices: 5.87 us -> 12.1 us  [body(): lax.all_to_all(piece.T, ('zl', 'core'), split_axis=0, concat_axis=0, tile...]
    convert_element_type x2 -> x8, other arithmetic: 5.88 us -> 9.15 us  [the longest x7 7.48 us: add(): return total.astype(BF)]
  transfers between devices with their start and end apart: 5 -> 25, of which waited for: 3 -> 11; matrix products, arithmetic and copies ran while one was open for 2% -> 7% of each run, Pallas kernels for 2% -> 12%
where the time goes in v2:
time: 229 us; the launch traced here: 227 us
  waiting for transfers between devices  87.3 us (38%)
  Pallas kernels  62 us (27%)
  starting transfers between devices  53.3 us (23%)
  other arithmetic  13 us (6%)
  local copies, waits for them, and re-layouts  10.7 us (5%)
    ppermute x8, waiting for transfers between devices, neighbours(): lax.ppermute(value, axis, up)  39.4 us
    all_to_all x1, waiting for transfers between devices, body(): lax.all_to_all(pooled.reshape(features, batch, width), dp, split_axis=0,...  38.4 us
    pallas_call x1, Pallas kernels, dense(): pl.pallas_call(functools.partial(dense_kernel, scale), name='dense', in_s...  22.1 us
    pallas_call x1, Pallas kernels, gradients(): pl.pallas_call(gradients_kernel, name='gradients', grid_spec=pltpu.Prefet...  18.2 us
    ppermute x8, starting transfers between devices, neighbours(): lax.ppermute(value, axis, down)  16.2 us
    pallas_call x1, Pallas kernels, pool(): pl.pallas_call(pool_kernel, name='pool', grid_spec=pltpu.PrefetchScalarGr...  13.1 us
    all_to_all x1, starting transfers between devices, body(): lax.all_to_all(piece.T, ('zl', 'core'), split_axis=0, concat_axis=0, tile...  12.1 us
    all_to_all x1, starting transfers between devices, body(): lax.all_to_all(pooled.reshape(features, batch, width), dp, split_axis=0,...  9.57 us
  transfers between devices with their start and end apart: 25, of which 11 were waited for; matrix products, arithmetic and copies ran while one was open for 7% of the time, Pallas kernels for 12%

profile of v2, /device:TPU:1, one launch (start us, length us, event | category | flops | bytes accessed | tf_op | source)
XLA Modules:
  0.0 227.2 jit_solution(11890349561020257865)
XLA Ops:
  0.6 13.1 %pool.1 = (bf16[12288,128]{1,0:T(8,128)(2,1)}, bf16[96,128,128]{2,1,0:T(8,128)(2,1)}) custom-call(s32[16,96]{1,0:T(8,128)} %bitcast.65, bf16[4096,128]{1,0:T(8,128)(2,1)} %table.1, s32[16,12288]{1,0:T(8,128)} %bitcast.59, s32[16,12288]{1,0:T(8,128)} %bitcast.60), custom_call_target="tpu_custom_call" | custom-call | tf_op jit(solution)/shard_map/pool/pallas_call | solution.py:59
  13.7 9.6 %all-to-all-start = ((bf16[32,384,128]{2,1,0:T(8,128)(2,1)}), bf16[32,384,128]{2,1,0:T(8,128)(2,1)S(1)}, u32[]{:S(2)}, u32[]{:S(2)}) async-start(bf16[32,384,128]{2,1,0:T(8,128)(2,1)} %bitcast.58), calls=%async_computation | async-start | bytes 6291456 | tf_op jit(solution)/shard_map/all_to_all | solution.py:542
  23.9 0.8 reshape.82.labels
  24.7 38.4 %all-to-all-done.received.inter_a.inter_b = bf16[32,384,128]{2,1,0:T(8,128)(2,1)S(1)} async-done(((bf16[32,384,128]{2,1,0:T(8,128)(2,1)}), bf16[32,384,128]{2,1,0:T(8,128)(2,1)S(1)}, u32[]{:S(2)}, u32[]{:S(2)}) %all-to-all-start) | async-done | bytes 3145760 | tf_op jit(solution)/shard_map/all_to_all | solution.py:542
  63.1 1.7 copy-done
  64.8 22.1 %dense.1 = (bf16[32,384,128]{2,1,0:T(8,128)(2,1)}, bf16[32,384,128]{2,1,0:T(8,128)(2,1)}, bf16[32,384,128]{2,1,0:T(8,128)(2,1)}, bf16[384,256]{1,0:T(8,128)(2,1)...) custom-call(s32[32]{0:T(128)} %fmap.1, ...), custom_call_target="tpu_custom_call" | custom-call | tf_op jit(solution)/shard_map/dense/pallas_call | solution.py:325
  86.9 5.0 %all-to-all-start.1 = ((bf16[32,384,128]{2,1,0:T(8,128)(2,1)}), bf16[32,384,128]{2,1,0:T(8,128)(2,1)S(1)}, u32[]{:S(2)}, u32[]{:S(2)}) async-start(bf16[32,384,128]{2,1,0:T(8,128)(2,1)} %get-tuple-element.43), calls=%async_computation.1 | async-start | bytes 6291456 | tf_op jit(solution)/shard_map/all_to_all | solution.py:557
  92.4 0.7 reduce.13
  93.1 0.7 reduce.12
  94.7 0.6 pad_add_fusion.place
  95.3 0.8 collective-permute-done
  96.2 1.7 select_convert_fusion.extra
  97.8 18.2 %gradients.1 = (bf16[8,2,272,128]{3,2,1,0:T(8,128)(2,1)}, bf16[8,2,272,128]{3,2,1,0:T(8,128)(2,1)}, bf16[8,2,272,128]{3,2,1,0:T(8,128)(2,1)}, bf16[8,2,272,128]{...) custom-call(s32[2]{0:T(128)} %pad_add_fusion.place, ...), custom_call_target="tpu_custom_call" | custom-call | flops 3221225472 | bytes 18874368 | tf_op jit(solution)/shard_map/gradients/pallas_call | solution.py:445
  116.4 2.7 %collective-permute-done.1 = bf16[8,2,272,128]{3,2,1,0:T(8,128)(2,1)S(1)} collective-permute-done((bf16[8,2,272,128]{3,2,1,0:T(8,128)(2,1)}, bf16[8,2,272,128]{3,2,1,0:T(8,128)(2,1)S(1)}, u32[]{:S(2)}, u32[]{:S(2)}) %collective-permute-start.1) | collective-permute-done | bytes 1114144 | tf_op jit(solution)/shard_map/ppermute | solution.py:579
  119.1 1.5 add_convert_fusion.10
  120.7 1.4 collective-permute-start.3
  122.0 1.5 collective-permute-start.2
  123.6 0.6 collective-permute-start.15
  124.7 11.4 %collective-permute-done.3 = bf16[4,2,272,128]{3,2,1,0:T(8,128)(2,1)S(1)} collective-permute-done((bf16[4,2,272,128]{3,2,1,0:T(8,128)(2,1)S(1)}, bf16[4,2,272,128]{3,2,1,0:T(8,128)(2,1)S(1)}, u32[]{:S(2)}, u32[]{:S(2)}) %collective-permute-start.3) | collective-permute-done | bytes 557088 | tf_op jit(solution)/shard_map/ppermute | solution.py:484
  136.1 0.8 copy-done.5
  136.9 1.7 copy-done.1
  138.6 7.1 %scatter.1 = bf16[4,1024,128]{2,1,0:T(8,128)(2,1)} custom-call(s32[16,96]{1,0:T(8,128)} %bitcast.66, s32[1]{0:T(128)} %bitcast.role, bf16[96,128,128]{2,1,0:T(8,128)(2,1)} %get-tuple-element.30.incidence, bf16[12288,128]{1,0:T(8,128)(2,1)} %bitcast.57), custom_call_target="tpu_custom_call" | custom-call | flops 8589934592 | bytes 8388608 | tf_op jit(solution)/shard_map/scatter/pallas_call | solution.py:133
  145.7 1.2 slice_bitcast_fusion.6
  146.9 1.9 collective-permute-start.5
  148.8 2.0 add_convert_fusion.8
  151.2 1.9 add_convert_fusion.6
  153.1 2.7 %collective-permute-start.18 = (bf16[4,2,272,128]{3,2,1,0:T(8,128)(2,1)S(1)}, bf16[4,2,272,128]{3,2,1,0:T(8,128)(2,1)S(1)}, u32[]{:S(2)}, u32[]{:S(2)}) collective-permute-start(bf16[4,2,272,128]{3,2,1,0:T(8,128)(2,1)S(1)} %get-tuple-element.59), channel_id=1, source_target_pairs={{0,96},{32,0},{64,32},{96,64},{1,97},{33,1},{65,33},{97,65},{2,98}... | collective-permute-start | bytes 1671176 | tf_op jit(solution)/shard_map/ppermute | solution.py:485
  155.8 1.2 collective-permute-start.20
  157.4 7.3 %collective-permute-done.16 = bf16[4,2,272,128]{3,2,1,0:T(8,128)(2,1)S(1)} collective-permute-done((bf16[4,2,272,128]{3,2,1,0:T(8,128)(2,1)S(1)}, bf16[4,2,272,128]{3,2,1,0:T(8,128)(2,1)S(1)}, u32[]{:S(2)}, u32[]{:S(2)}) %collective-permute-start.16) | collective-permute-done | bytes 557088 | tf_op jit(solution)/shard_map/ppermute | solution.py:484
  164.8 11.9 %collective-permute-done.19 = bf16[4,2,272,128]{3,2,1,0:T(8,128)(2,1)S(1)} collective-permute-done((bf16[4,2,272,128]{3,2,1,0:T(8,128)(2,1)S(1)}, bf16[4,2,272,128]{3,2,1,0:T(8,128)(2,1)S(1)}, u32[]{:S(2)}, u32[]{:S(2)}) %collective-permute-start.19) | collective-permute-done | bytes 557088 | tf_op jit(solution)/shard_map/ppermute | solution.py:484
  176.7 1.2 collective-permute-done.20
  177.9 1.9 add_convert_fusion.5
  179.8 1.1 pad_maximum_fusion
  180.9 6.4 %all-to-all-start.2 = ((bf16[16,272,128]{2,1,0:T(8,128)(2,1)}), bf16[16,272,128]{2,1,0:T(8,128)(2,1)S(1)}, u32[]{:S(2)}, u32[]{:S(2)}) async-start(bf16[16,272,128]{2,1,0:T(8,128)(2,1)} %bitcast.22), calls=%async_computation.2 | async-start | bytes 2228224 | tf_op jit(solution)/shard_map/all_to_all | solution.py:589
  187.3 3.5 %collective-permute-start.9 = (bf16[512,128]{1,0:T(8,128)(2,1)S(1)}, bf16[512,128]{1,0:T(8,128)(2,1)S(1)}, u32[]{:S(2)}, u32[]{:S(2)}) collective-permute-start(bf16[512,128]{1,0:T(8,128)(2,1)S(1)} %get-tuple-element.66), channel_id=1, source_target_pairs={{0,96},{32,0},{64,32},{96,64},{1,97},{33,1},{65,33},{97,65},{2,98}... | collective-permute-start | bytes 393224 | tf_op jit(solution)/shard_map/ppermute | solution.py:485
  191.0 1.8 collective-permute-done.9
  192.7 3.3 %collective-permute-done.8 = bf16[512,128]{1,0:T(8,128)(2,1)S(1)} collective-permute-done((bf16[512,128]{1,0:T(8,128)(2,1)S(1)}, bf16[512,128]{1,0:T(8,128)(2,1)S(1)}, u32[]{:S(2)}, u32[]{:S(2)}) %collective-permute-start.8) | collective-permute-done | bytes 131104 | tf_op jit(solution)/shard_map/ppermute | solution.py:484
  196.1 2.7 %collective-permute-start.10 = (bf16[1024,128]{1,0:T(8,128)(2,1)S(1)}, bf16[1024,128]{1,0:T(8,128)(2,1)S(1)}, u32[]{:S(2)}, u32[]{:S(2)}) collective-permute-start(bf16[1024,128]{1,0:T(8,128)(2,1)S(1)} %pad_maximum_fusion.1.own), channel_id=1, source_target_pairs={{0,96},{32,0},{64,32},{96,64},{1,97},{33,1},{65,33},{97,65},{2,98}... | collective-permute-start | bytes 786440 | tf_op jit(solution)/shard_map/ppermute | solution.py:485
  198.8 5.5 %collective-permute-done.12.preceding = bf16[1024,128]{1,0:T(8,128)(2,1)S(1)} collective-permute-done((bf16[1024,128]{1,0:T(8,128)(2,1)S(1)}, bf16[1024,128]{1,0:T(8,128)(2,1)S(1)}, u32[]{:S(2)}, u32[]{:S(2)}) %collective-permute-start.12) | collective-permute-done | bytes 262176 | tf_op jit(solution)/shard_map/ppermute | solution.py:484
  204.4 2.7 %collective-permute-start.11 = (bf16[512,128]{1,0:T(8,128)(2,1)S(1)}, bf16[512,128]{1,0:T(8,128)(2,1)S(1)}, u32[]{:S(2)}, u32[]{:S(2)}) collective-permute-start(bf16[512,128]{1,0:T(8,128)(2,1)S(1)} %slice.142), channel_id=1, source_target_pairs={{0,96},{32,0},{64,32},{96,64},{1,97},{33,1},{65,33},{97,65},{2,98}... | collective-permute-start | bytes 393224 | tf_op jit(solution)/shard_map/ppermute | solution.py:485
  207.3 0.8 copy.23
  208.1 12.1 %all-to-all-start.3 = ((f32[4,32,272]{2,1,0:T(8,128)}), f32[4,32,272]{2,1,0:T(8,128)S(1)}, u32[]{:S(2)}, u32[]{:S(2)}) async-start(f32[4,32,272]{2,1,0:T(8,128)} %bitcast.24), calls=%async_computation.3 | async-start | bytes 393216 | tf_op jit(solution)/shard_map/all_to_all | solution.py:597
  220.2 1.5 spread_rows.1
  221.6 3.0 %all-to-all-done.3 = f32[4,32,272]{2,1,0:T(8,128)S(1)} async-done(((f32[4,32,272]{2,1,0:T(8,128)}), f32[4,32,272]{2,1,0:T(8,128)S(1)}, u32[]{:S(2)}, u32[]{:S(2)}) %all-to-all-start.3) | async-done | bytes 139296 | tf_op jit(solution)/shard_map/all_to_all | solution.py:597
  224.6 0.6 slice_bitcast_fusion.9
  225.3 0.6 pad_maximum_fusion.2
  225.9 0.6 slice_reduce_fusion
  226.5 0.7 slice_reduce_fusion.1
  (63 shorter events, 4.2 us)
Async XLA Ops:
  13.7 9.6 %copy-start.11 = (bf16[512]{0:T(512)(128)(2,1)S(1)}, bf16[512]{0:T(512)(128)(2,1)}, u32[]{:S(2)}) copy-start(bf16[512]{0:T(512)(128)(2,1)} %param.23) | copy-start | bytes 3076
  13.7 10.2 %copy-start.8 = (s32[384]{0:T(512)S(1)}, s32[384]{0:T(512)}, u32[]{:S(2)}) copy-start(s32[384]{0:T(512)} %param.17) | copy-start | bytes 4612
  13.7 49.3 %all-to-all-start = ((bf16[32,384,128]{2,1,0:T(8,128)(2,1)}), bf16[32,384,128]{2,1,0:T(8,128)(2,1)S(1)}, u32[]{:S(2)}, u32[]{:S(2)}) async-start(bf16[32,384,128]{2,1,0:T(8,128)(2,1)} %bitcast.58), calls=%async_computation | async-start | bytes 6291456 | tf_op jit(solution)/shard_map/all_to_all | solution.py:542
  63.1 1.7 copy-start
  86.9 5.5 %copy-start.10 = (f32[1,512]{1,0:T(1,128)S(1)}, f32[1,512]{1,0:T(1,128)}, u32[]{:S(2)}) copy-start(f32[1,512]{1,0:T(1,128)} %get-tuple-element.39) | copy-start | bytes 6148
  86.9 6.2 %copy-start.9 = (f32[1,512]{1,0:T(1,128)S(1)}, f32[1,512]{1,0:T(1,128)}, u32[]{:S(2)}) copy-start(f32[1,512]{1,0:T(1,128)} %get-tuple-element.40) | copy-start | bytes 6148
  86.9 7.4 %copy-start.7 = (f32[1,4096]{1,0:T(1,128)S(1)}, f32[1,4096]{1,0:T(1,128)}, u32[]{:S(2)}) copy-start(f32[1,4096]{1,0:T(1,128)} %get-tuple-element.38) | copy-start | bytes 49156
  86.9 50.0 %all-to-all-start.1 = ((bf16[32,384,128]{2,1,0:T(8,128)(2,1)}), bf16[32,384,128]{2,1,0:T(8,128)(2,1)S(1)}, u32[]{:S(2)}, u32[]{:S(2)}) async-start(bf16[32,384,128]{2,1,0:T(8,128)(2,1)} %get-tuple-element.43), calls=%async_computation.1 | async-start | bytes 6291456 | tf_op jit(solution)/shard_map/all_to_all | solution.py:557
  94.4 1.7 collective-permute-start
  116.1 3.0 %collective-permute-start.1 = (bf16[8,2,272,128]{3,2,1,0:T(8,128)(2,1)}, bf16[8,2,272,128]{3,2,1,0:T(8,128)(2,1)S(1)}, u32[]{:S(2)}, u32[]{:S(2)}) collective-permute-start(bf16[8,2,272,128]{3,2,1,0:T(8,128)(2,1)} %get-tuple-element.42), channel_id=1, source_target_pairs={{0,1},{1,0},{2,3},{3,2},{4,5},{5,4},{6,7},{7,6},{8,9},{9,8},{10,11... | collective-permute-start | bytes 3342344 | tf_op jit(solution)/shard_map/ppermute | solution.py:579
  120.7 15.4 %collective-permute-start.3 = (bf16[4,2,272,128]{3,2,1,0:T(8,128)(2,1)S(1)}, bf16[4,2,272,128]{3,2,1,0:T(8,128)(2,1)S(1)}, u32[]{:S(2)}, u32[]{:S(2)}) collective-permute-start(bf16[4,2,272,128]{3,2,1,0:T(8,128)(2,1)S(1)} %get-tuple-element.61), channel_id=1, source_target_pairs={{0,32},{32,64},{64,96},{96,0},{1,33},{33,65},{65,97},{97,1},{2,34}... | collective-permute-start | bytes 1671176 | tf_op jit(solution)/shard_map/ppermute | solution.py:484
  122.0 14.9 %collective-permute-start.2 = (bf16[4,2,272,128]{3,2,1,0:T(8,128)(2,1)S(1)}, bf16[4,2,272,128]{3,2,1,0:T(8,128)(2,1)}, u32[]{:S(2)}, u32[]{:S(2)}) collective-permute-start(bf16[4,2,272,128]{3,2,1,0:T(8,128)(2,1)S(1)} %get-tuple-element.62), channel_id=1, source_target_pairs={{0,96},{32,0},{64,32},{96,64},{1,97},{33,1},{65,33},{97,65},{2,98}... | collective-permute-start | bytes 1671176 | tf_op jit(solution)/shard_map/ppermute | solution.py:485
  123.6 25.3 %collective-permute-start.15 = (bf16[8,2,272,128]{3,2,1,0:T(8,128)(2,1)}, bf16[8,2,272,128]{3,2,1,0:T(8,128)(2,1)}, u32[]{:S(2)}, u32[]{:S(2)}) collective-permute-start(bf16[8,2,272,128]{3,2,1,0:T(8,128)(2,1)} %get-tuple-element.48), channel_id=1, source_target_pairs={{0,1},{1,0},{2,3},{3,2},{4,5},{5,4},{6,7},{7,6},{8,9},{9,8},{10,11... | collective-permute-start | bytes 3342344 | tf_op jit(solution)/shard_map/ppermute | solution.py:579
  124.2 32.9 %collective-permute-start.14 = (bf16[8,2,272,128]{3,2,1,0:T(8,128)(2,1)}, bf16[8,2,272,128]{3,2,1,0:T(8,128)(2,1)}, u32[]{:S(2)}, u32[]{:S(2)}) collective-permute-start(bf16[8,2,272,128]{3,2,1,0:T(8,128)(2,1)} %get-tuple-element.46), channel_id=1, source_target_pairs={{0,1},{1,0},{2,3},{3,2},{4,5},{5,4},{6,7},{7,6},{8,9},{9,8},{10,11... | collective-permute-start | bytes 3342344 | tf_op jit(solution)/shard_map/ppermute | solution.py:579
  124.2 27.0 %collective-permute-start.17 = (bf16[8,2,272,128]{3,2,1,0:T(8,128)(2,1)}, bf16[8,2,272,128]{3,2,1,0:T(8,128)(2,1)}, u32[]{:S(2)}, u32[]{:S(2)}) collective-permute-start(bf16[8,2,272,128]{3,2,1,0:T(8,128)(2,1)} %get-tuple-element.50), channel_id=1, source_target_pairs={{0,1},{1,0},{2,3},{3,2},{4,5},{5,4},{6,7},{7,6},{8,9},{9,8},{10,11... | collective-permute-start | bytes 3342344 | tf_op jit(solution)/shard_map/ppermute | solution.py:579
  136.1 0.8 copy-start.5
  136.9 1.7 copy-start.1
  145.7 3.1 %copy-start.6 = (bf16[4,2,272,128]{3,2,1,0:T(8,128)(2,1)S(1)}, bf16[4,2,272,128]{3,2,1,0:T(8,128)(2,1)}, u32[]{:S(2)}) copy-start(bf16[4,2,272,128]{3,2,1,0:T(8,128)(2,1)} %copy-done.5) | copy-start | bytes 1671172
  146.9 8.9 %collective-permute-start.5 = (bf16[512,128]{1,0:T(8,128)(2,1)S(1)}, bf16[512,128]{1,0:T(8,128)(2,1)S(1)}, u32[]{:S(2)}, u32[]{:S(2)}) collective-permute-start(bf16[512,128]{1,0:T(8,128)(2,1)S(1)} %get-tuple-element.68), channel_id=1, source_target_pairs={{0,96},{32,0},{64,32},{96,64},{1,97},{33,1},{65,33},{97,65},{2,98}... | collective-permute-start | bytes 393224 | tf_op jit(solution)/shard_map/ppermute | solution.py:485
  148.8 2.4 %copy-start.3 = (bf16[8,2,272,128]{3,2,1,0:T(8,128)(2,1)S(1)}, bf16[8,2,272,128]{3,2,1,0:T(8,128)(2,1)}, u32[]{:S(2)}) copy-start(bf16[8,2,272,128]{3,2,1,0:T(8,128)(2,1)} %get-tuple-element.49) | copy-start | bytes 3342340
  150.8 13.9 %collective-permute-start.16 = (bf16[4,2,272,128]{3,2,1,0:T(8,128)(2,1)S(1)}, bf16[4,2,272,128]{3,2,1,0:T(8,128)(2,1)S(1)}, u32[]{:S(2)}, u32[]{:S(2)}) collective-permute-start(bf16[4,2,272,128]{3,2,1,0:T(8,128)(2,1)S(1)} %get-tuple-element.57), channel_id=1, source_target_pairs={{0,32},{32,64},{64,96},{96,0},{1,33},{33,65},{65,97},{97,1},{2,34}... | collective-permute-start | bytes 1671176 | tf_op jit(solution)/shard_map/ppermute | solution.py:484
  150.9 25.8 %collective-permute-start.19 = (bf16[4,2,272,128]{3,2,1,0:T(8,128)(2,1)S(1)}, bf16[4,2,272,128]{3,2,1,0:T(8,128)(2,1)S(1)}, u32[]{:S(2)}, u32[]{:S(2)}) collective-permute-start(bf16[4,2,272,128]{3,2,1,0:T(8,128)(2,1)S(1)} %get-tuple-element.58), channel_id=1, source_target_pairs={{0,32},{32,64},{64,96},{96,0},{1,33},{33,65},{65,97},{97,1},{2,34}... | collective-permute-start | bytes 1671176 | tf_op jit(solution)/shard_map/ppermute | solution.py:484
  151.2 5.8 %copy-start.4 = (bf16[4,1024,128]{2,1,0:T(8,128)(2,1)S(1)}, bf16[4,1024,128]{2,1,0:T(8,128)(2,1)}, u32[]{:S(2)}) copy-start(bf16[4,1024,128]{2,1,0:T(8,128)(2,1)} %scatter.1) | copy-start | bytes 3145732
  151.2 26.7 %copy-start.2 = (bf16[8,2,272,128]{3,2,1,0:T(8,128)(2,1)S(1)}, bf16[8,2,272,128]{3,2,1,0:T(8,128)(2,1)}, u32[]{:S(2)}) copy-start(bf16[8,2,272,128]{3,2,1,0:T(8,128)(2,1)} %get-tuple-element.45) | copy-start | bytes 3342340
  153.1 23.6 %collective-permute-start.18 = (bf16[4,2,272,128]{3,2,1,0:T(8,128)(2,1)S(1)}, bf16[4,2,272,128]{3,2,1,0:T(8,128)(2,1)S(1)}, u32[]{:S(2)}, u32[]{:S(2)}) collective-permute-start(bf16[4,2,272,128]{3,2,1,0:T(8,128)(2,1)S(1)} %get-tuple-element.59), channel_id=1, source_target_pairs={{0,96},{32,0},{64,32},{96,64},{1,97},{33,1},{65,33},{97,65},{2,98}... | collective-permute-start | bytes 1671176 | tf_op jit(solution)/shard_map/ppermute | solution.py:485
  155.8 22.1 %collective-permute-start.20 = (bf16[4,2,272,128]{3,2,1,0:T(8,128)(2,1)S(1)}, bf16[4,2,272,128]{3,2,1,0:T(8,128)(2,1)S(1)}, u32[]{:S(2)}, u32[]{:S(2)}) collective-permute-start(bf16[4,2,272,128]{3,2,1,0:T(8,128)(2,1)S(1)} %get-tuple-element.60), channel_id=1, source_target_pairs={{0,96},{32,0},{64,32},{96,64},{1,97},{33,1},{65,33},{97,65},{2,98}... | collective-permute-start | bytes 1671176 | tf_op jit(solution)/shard_map/ppermute | solution.py:485
  157.1 33.7 %collective-permute-start.4 = (bf16[512,128]{1,0:T(8,128)(2,1)S(1)}, bf16[512,128]{1,0:T(8,128)(2,1)S(1)}, u32[]{:S(2)}, u32[]{:S(2)}) collective-permute-start(bf16[512,128]{1,0:T(8,128)(2,1)S(1)} %get-tuple-element.65), channel_id=1, source_target_pairs={{0,32},{32,64},{64,96},{96,0},{1,33},{33,65},{65,97},{97,1},{2,34}... | collective-permute-start | bytes 393224 | tf_op jit(solution)/shard_map/ppermute | solution.py:484
  164.7 26.0 %collective-permute-start.7 = (bf16[512,128]{1,0:T(8,128)(2,1)S(1)}, bf16[512,128]{1,0:T(8,128)(2,1)S(1)}, u32[]{:S(2)}, u32[]{:S(2)}) collective-permute-start(bf16[512,128]{1,0:T(8,128)(2,1)S(1)} %get-tuple-element.67), channel_id=1, source_target_pairs={{0,32},{32,64},{64,96},{96,0},{1,33},{33,65},{65,97},{97,1},{2,34}... | collective-permute-start | bytes 393224 | tf_op jit(solution)/shard_map/ppermute | solution.py:484
  176.7 14.1 %collective-permute-start.6 = (bf16[512,128]{1,0:T(8,128)(2,1)S(1)}, bf16[512,128]{1,0:T(8,128)(2,1)S(1)}, u32[]{:S(2)}, u32[]{:S(2)}) collective-permute-start(bf16[512,128]{1,0:T(8,128)(2,1)S(1)} %fusion.3), channel_id=1, source_target_pairs={{0,96},{32,0},{64,32},{96,64},{1,97},{33,1},{65,33},{97,65},{2,98}... | collective-permute-start | bytes 393224 | tf_op jit(solution)/shard_map/ppermute | solution.py:485
  180.9 26.2 %all-to-all-start.2 = ((bf16[16,272,128]{2,1,0:T(8,128)(2,1)}), bf16[16,272,128]{2,1,0:T(8,128)(2,1)S(1)}, u32[]{:S(2)}, u32[]{:S(2)}) async-start(bf16[16,272,128]{2,1,0:T(8,128)(2,1)} %bitcast.22), calls=%async_computation.2 | async-start | bytes 2228224 | tf_op jit(solution)/shard_map/all_to_all | solution.py:589
  187.3 5.4 %collective-permute-start.9 = (bf16[512,128]{1,0:T(8,128)(2,1)S(1)}, bf16[512,128]{1,0:T(8,128)(2,1)S(1)}, u32[]{:S(2)}, u32[]{:S(2)}) collective-permute-start(bf16[512,128]{1,0:T(8,128)(2,1)S(1)} %get-tuple-element.66), channel_id=1, source_target_pairs={{0,96},{32,0},{64,32},{96,64},{1,97},{33,1},{65,33},{97,65},{2,98}... | collective-permute-start | bytes 393224 | tf_op jit(solution)/shard_map/ppermute | solution.py:485
  190.9 5.1 %collective-permute-start.8 = (bf16[512,128]{1,0:T(8,128)(2,1)S(1)}, bf16[512,128]{1,0:T(8,128)(2,1)S(1)}, u32[]{:S(2)}, u32[]{:S(2)}) collective-permute-start(bf16[512,128]{1,0:T(8,128)(2,1)S(1)} %get-tuple-element.64), channel_id=1, source_target_pairs={{0,32},{32,64},{64,96},{96,0},{1,33},{33,65},{65,97},{97,1},{2,34}... | collective-permute-start | bytes 393224 | tf_op jit(solution)/shard_map/ppermute | solution.py:484
  196.1 8.2 %collective-permute-start.12 = (bf16[1024,128]{1,0:T(8,128)(2,1)S(1)}, bf16[1024,128]{1,0:T(8,128)(2,1)S(1)}, u32[]{:S(2)}, u32[]{:S(2)}) collective-permute-start(bf16[1024,128]{1,0:T(8,128)(2,1)S(1)} %pad_maximum_fusion.1.own), channel_id=1, source_target_pairs={{0,32},{32,64},{64,96},{96,0},{1,33},{33,65},{65,97},{97,1},{2,34}... | collective-permute-start | bytes 786440 | tf_op jit(solution)/shard_map/ppermute | solution.py:484
  196.1 8.2 %collective-permute-start.10 = (bf16[1024,128]{1,0:T(8,128)(2,1)S(1)}, bf16[1024,128]{1,0:T(8,128)(2,1)S(1)}, u32[]{:S(2)}, u32[]{:S(2)}) collective-permute-start(bf16[1024,128]{1,0:T(8,128)(2,1)S(1)} %pad_maximum_fusion.1.own), channel_id=1, source_target_pairs={{0,96},{32,0},{64,32},{96,64},{1,97},{33,1},{65,33},{97,65},{2,98}... | collective-permute-start | bytes 786440 | tf_op jit(solution)/shard_map/ppermute | solution.py:485
  204.3 15.9 %collective-permute-start.13 = (bf16[512,128]{1,0:T(8,128)(2,1)S(1)}, bf16[512,128]{1,0:T(8,128)(2,1)S(1)}, u32[]{:S(2)}, u32[]{:S(2)}) collective-permute-start(bf16[512,128]{1,0:T(8,128)(2,1)S(1)} %slice.143), channel_id=1, source_target_pairs={{0,32},{32,64},{64,96},{96,0},{1,33},{33,65},{65,97},{97,1},{2,34}... | collective-permute-start | bytes 393224 | tf_op jit(solution)/shard_map/ppermute | solution.py:484
  204.4 15.8 %collective-permute-start.11 = (bf16[512,128]{1,0:T(8,128)(2,1)S(1)}, bf16[512,128]{1,0:T(8,128)(2,1)S(1)}, u32[]{:S(2)}, u32[]{:S(2)}) collective-permute-start(bf16[512,128]{1,0:T(8,128)(2,1)S(1)} %slice.142), channel_id=1, source_target_pairs={{0,96},{32,0},{64,32},{96,64},{1,97},{33,1},{65,33},{97,65},{2,98}... | collective-permute-start | bytes 393224 | tf_op jit(solution)/shard_map/ppermute | solution.py:485
  208.1 16.5 %all-to-all-start.3 = ((f32[4,32,272]{2,1,0:T(8,128)}), f32[4,32,272]{2,1,0:T(8,128)S(1)}, u32[]{:S(2)}, u32[]{:S(2)}) async-start(f32[4,32,272]{2,1,0:T(8,128)} %bitcast.24), calls=%async_computation.3 | async-start | bytes 393216 | tf_op jit(solution)/shard_map/all_to_all | solution.py:597

commit v3 on v2

v3 whole, which is shorter than its diff:
```python
import functools

import jax
import jax.numpy as jnp
from jax import lax
from jax.experimental import pallas as pl
from jax.experimental.pallas import tpu as pltpu
from jax.sharding import Mesh
from jax.sharding import PartitionSpec as P

BLK = 8
LOSS_SCALE = 65536.0
STEP_TILES = 8
WIDE = 2048
EXTRA = 16
ORDER = (2, 1, 3, 0)
VMEM = 60 << 20
POOL_VMEM = VMEM
DENSE_VMEM = VMEM
GRADIENTS_VMEM = VMEM
SCATTER_VMEM = VMEM

BF = jnp.bfloat16
F32 = jnp.float32


def nt(left, right):
    return lax.dot_general(left, right, (((1,), (1,)), ((), ())), preferred_element_type=F32)


def pool_kernel(touched, table, index, count, pooled, incidence, *scratch):
    rows16, rows32, index_in, count_in, held, tiles_held, table_sem, in_sems, out_sems = scratch
    tiles, tile, _ = incidence.shape
    steps = tiles // STEP_TILES
    span = STEP_TILES * tile

    def loads(step):
        part = pl.ds(pl.multiple_of(step * span, span), span)
        return (
            pltpu.make_async_copy(index.at[:, part], index_in.at[:, part], in_sems.at[0, step]),
            pltpu.make_async_copy(count.at[:, part], count_in.at[:, part], in_sems.at[1, step]),
        )

    def stores(step):
        part = pl.ds(pl.multiple_of(step * span, span), span)
        some = pl.ds(step * STEP_TILES, STEP_TILES)
        return (
            pltpu.make_async_copy(held.at[part], pooled.at[part], out_sems.at[0, step]),
            pltpu.make_async_copy(tiles_held.at[some], incidence.at[some], out_sems.at[1, step]),
        )

    whole = pltpu.make_async_copy(table, rows16, table_sem)
    whole.start()
    for step in range(steps):
        for copy in loads(step):
            copy.start()
    whole.wait()
    rows32[...] = rows16[...].astype(F32)
    listed = lax.broadcasted_iota(jnp.int32, (tile, tile), 0).astype(BF)

    @pl.loop(0, steps)
    def _(step):
        for copy in loads(step):
            copy.wait()
        for i in range(STEP_TILES):
            t = step * STEP_TILES + i
            part = pl.ds(pl.multiple_of(t * tile, tile), tile)
            idx = index_in[:, part].astype(BF)
            cnt = count_in[:, part].astype(BF)
            total = jnp.zeros((tile, tile), BF)
            for j in range(index.shape[0]):
                total += jnp.where(idx[j : j + 1] == listed, cnt[j : j + 1], jnp.zeros((), BF))
            tiles_held[t] = total
            blocks = [
                rows32[pl.ds(pl.multiple_of(touched[k, t] * BLK, BLK), BLK), :]
                for k in range(touched.shape[0])
            ]
            picked = jnp.concatenate(blocks, axis=0).astype(BF)
            held[part, :] = lax.dot_general(
                total, picked, (((0,), (0,)), ((), ())), preferred_element_type=F32
            ).astype(BF)
        for copy in stores(step):
            copy.start()

    for step in range(steps):
        for copy in stores(step):
            copy.wait()


def pool(touched, table, index, count, tile):
    hot, samples = index.shape
    tiles = samples // tile
    width = table.shape[1]
    steps = tiles // STEP_TILES
    hbm = pl.BlockSpec(memory_space=pltpu.HBM)
    return pl.pallas_call(
        pool_kernel,
        name="pool",
        in_specs=[pl.BlockSpec(memory_space=pltpu.SMEM), hbm, hbm, hbm],
        out_specs=[hbm, hbm],
        out_shape=[
            jax.ShapeDtypeStruct((samples, width), BF),
            jax.ShapeDtypeStruct((tiles, tile, tile), BF),
        ],
        scratch_shapes=[
            pltpu.VMEM(table.shape, BF),
            pltpu.VMEM(table.shape, F32),
            pltpu.VMEM(index.shape, jnp.int32),
            pltpu.VMEM(count.shape, jnp.int32),
            pltpu.VMEM((samples, width), BF),
            pltpu.VMEM((tiles, tile, tile), BF),
            pltpu.SemaphoreType.DMA,
            pltpu.SemaphoreType.DMA((2, steps)),
            pltpu.SemaphoreType.DMA((2, steps)),
        ],
        compiler_params=pltpu.CompilerParams(vmem_limit_bytes=POOL_VMEM),
    )(touched, table, index, count)


def scatter_kernel(touched, incidence, grad, out, *scratch):
    sums, (tiles_in, grads_in, sems) = scratch[:-3], scratch[-3:]
    tiles, tile, _ = incidence.shape
    chunks, rows, _ = out.shape
    steps = tiles // STEP_TILES

    def loads(step):
        part = pl.ds(step * STEP_TILES, STEP_TILES)
        span = pl.ds(step * STEP_TILES * tile, STEP_TILES * tile)
        return (
            pltpu.make_async_copy(incidence.at[part], tiles_in.at[part], sems.at[0, step]),
            pltpu.make_async_copy(grad.at[span], grads_in.at[span], sems.at[1, step]),
        )

    for step in range(steps):
        for copy in loads(step):
            copy.start()
    for acc in sums:
        acc[...] = jnp.zeros_like(acc)

    @pl.loop(0, steps)
    def _(step):
        for copy in loads(step):
            copy.wait()
        for i in range(STEP_TILES):
            t = step * STEP_TILES + i
            product = jnp.dot(
                tiles_in[t], grads_in[pl.ds(t * tile, tile), :], preferred_element_type=F32
            )
            for k in range(touched.shape[0]):
                acc = sums[k % len(sums)]
                place = pl.ds(pl.multiple_of(touched[k, t] * BLK, BLK), BLK)
                acc[place, :] += product[k * BLK : (k + 1) * BLK]

    for i in range(chunks):
        place = pl.ds(i * rows, rows)
        total = sums[0][place, :]
        for acc in sums[1:]:
            total = total + acc[place, :]
        out[i] = total.astype(out.dtype)


def scatter(touched, incidence, grad, rows, chunks):
    tiles, tile, _ = incidence.shape
    width = grad.shape[1]
    steps = tiles // STEP_TILES
    smem = pl.BlockSpec(memory_space=pltpu.SMEM)
    hbm = pl.BlockSpec(memory_space=pltpu.HBM)
    vmem = pl.BlockSpec(memory_space=pltpu.VMEM)
    return pl.pallas_call(
        scatter_kernel,
        name="scatter",
        in_specs=[smem, hbm, hbm],
        out_specs=vmem,
        out_shape=jax.ShapeDtypeStruct((chunks, rows // chunks, width), BF),
        scratch_shapes=[pltpu.VMEM((rows, width), F32)] * 4
        + [
            pltpu.VMEM(incidence.shape, BF),
            pltpu.VMEM(grad.shape, BF),
            pltpu.SemaphoreType.DMA((2, steps)),
        ],
        compiler_params=pltpu.CompilerParams(vmem_limit_bytes=SCATTER_VMEM),
        cost_estimate=pl.CostEstimate(flops=1 << 33, bytes_accessed=8 << 20, transcendentals=0),
    )(touched, incidence, grad)


def spread_kernel(role, own, following, opposite_a, opposite_b, preceding, out):
    rows = own.shape[0]
    half = rows // 2
    chunks = out.shape[0] // rows

    def place(offset, size, piece):
        first = lax.rem(role[0] + offset, chunks) * rows
        out[pl.ds(pl.multiple_of(first, rows) + size, piece.shape[0]), :] = piece[...].astype(F32)

    place(0, 0, own)
    place(1, 0, following)
    place(2, 0, opposite_a)
    place(2, half, opposite_b)
    place(3, 0, preceding)


def spread_rows(role, pieces, chunks):
    rows, width = pieces[0].shape
    vmem = pl.BlockSpec(memory_space=pltpu.VMEM)
    return pl.pallas_call(
        spread_kernel,
        name="spread_rows",
        in_specs=[pl.BlockSpec(memory_space=pltpu.SMEM)] + [vmem] * 5,
        out_specs=vmem,
        out_shape=jax.ShapeDtypeStruct((chunks * rows, width), F32),
        compiler_params=pltpu.CompilerParams(vmem_limit_bytes=VMEM),
    )(role, *pieces)


def dense_kernel(
    scale,
    fmap,
    received,
    labels,
    v_hbm,
    u_hbm,
    cross_bias,
    h_hbm,
    hidden_bias,
    out_weight,
    back,
    crossed_hbm,
    proj_hbm,
    low_hbm,
    low_grad_hbm,
    d_hidden_hbm,
    cross_bias_grad,
    hidden_bias_grad,
    out_weight_grad,
    inter,
    crossed,
    proj_low,
    held,
    d_inter,
    v,
    u,
    h,
    low_out,
    low_grad_out,
    d_hidden_out,
    hidden,
    low_sum,
    in_sems,
    weight_sems,
    small_sems,
    wide_sems,
    back_sems,
):
    features, batch, width = received.shape
    total_width = features * width
    blocks = total_width // WIDE
    per_block = WIDE // width

    def load(s):
        cols = pl.ds(pl.multiple_of(fmap[s] * width, width), width)
        return pltpu.make_async_copy(received.at[s], inter.at[:, cols], in_sems.at[s])

    weights = [
        pltpu.make_async_copy(source, target, weight_sems.at[i])
        for i, (source, target) in enumerate(((v_hbm, v), (u_hbm, u), (h_hbm, h)))
    ]
    weights[0].start()
    loads = [load(s) for s in range(features)]
    for copy in loads:
        copy.start()
    weights[1].start()
    weights[2].start()

    def store(row, source, target, f):
        cols = pl.ds(pl.multiple_of(f * width, width), width)
        return pltpu.make_async_copy(source.at[:, cols], target.at[f], wide_sems.at[row, f])

    small = [
        pltpu.make_async_copy(source, target, small_sems.at[i])
        for i, (source, target) in enumerate(
            ((low_out, low_hbm), (low_grad_out, low_grad_hbm), (d_hidden_out, d_hidden_hbm))
        )
    ]
    low_sum[...] = jnp.zeros_like(low_sum)
    hidden[...] = jnp.broadcast_to(hidden_bias[...], hidden.shape)
    hidden_bias_grad[...] = jnp.zeros_like(hidden_bias_grad)
    out_weight_grad[...] = jnp.zeros_like(out_weight_grad)
    weights[0].wait()
    for b in range(blocks):
        places = []
        for s in range(b * per_block, (b + 1) * per_block):
            loads[s].wait()
            places.append(pl.ds(pl.multiple_of(fmap[s] * width, width), width))
        left = jnp.concatenate([inter[:, place] for place in places], axis=1)
        right = jnp.concatenate([v[place, :] for place in places], axis=0)
        low_sum[...] += jnp.dot(left, right, preferred_element_type=F32)

    low_out[...] = low_sum[...].astype(BF)
    small[0].start()
    weights[1].wait()
    weights[2].wait()

    @pl.loop(0, blocks)
    def _(b):
        cols = pl.ds(pl.multiple_of(b * WIDE, WIDE), WIDE)
        projected = (
            jnp.dot(low_out[...], u[:, cols], preferred_element_type=F32) + cross_bias[:, cols]
        )
        held[:, cols] = projected
        x = inter[:, cols].astype(F32)
        product = (x * projected + x).astype(BF)
        crossed[:, cols] = product
        hidden[...] += jnp.dot(product, h[cols, :], preferred_element_type=F32)
        for i in range(per_block):
            store(0, crossed, crossed_hbm, b * per_block + i).start()

    chunk = 64

    @pl.loop(0, batch // chunk)
    def _(r):
        rows = pl.ds(pl.multiple_of(r * chunk, chunk), chunk)
        pre = hidden[rows, :]
        gate = jax.nn.sigmoid(pre)
        act = (pre * gate).astype(BF).astype(F32)
        weight = out_weight[...].astype(F32)
        logit = jnp.sum(act * weight, axis=1, keepdims=True)
        d_logit = (scale * (jax.nn.sigmoid(logit) - labels[rows, :].astype(F32))).astype(BF)
        d_logit = d_logit.astype(F32)
        d_hidden = (d_logit * weight * (gate * (1.0 + pre * (1.0 - gate)))).astype(BF)
        d_hidden_out[rows, :] = d_hidden
        hidden_bias_grad[...] += jnp.sum(d_hidden.astype(F32), axis=0, keepdims=True)
        out_weight_grad[...] += jnp.sum(d_logit * act, axis=0, keepdims=True)

    small[2].start()
    low_sum[...] = jnp.zeros_like(low_sum)

    @pl.loop(0, blocks)
    def _(b):
        cols = pl.ds(pl.multiple_of(b * WIDE, WIDE), WIDE)
        d_crossed = nt(d_hidden_out[...], h[cols, :])
        d_proj = d_crossed * inter[:, cols].astype(F32)
        cross_bias_grad[:, cols] = jnp.sum(d_proj, axis=0, keepdims=True)
        rounded = d_proj.astype(BF)
        proj_low[:, cols] = rounded
        low_sum[...] += nt(rounded, u[:, cols])
        held[:, cols] = d_crossed * (held[:, cols] + 1.0)
        for i in range(per_block):
            store(1, proj_low, proj_hbm, b * per_block + i).start()

    low_grad_out[...] = low_sum[...].astype(BF)
    small[1].start()
    stores = list(small)
    for f in range(features):
        stores += [store(0, crossed, crossed_hbm, f), store(1, proj_low, proj_hbm, f)]
    for b in range(blocks):
        slots = range(b * per_block, (b + 1) * per_block)
        places = [pl.ds(pl.multiple_of(fmap[s] * width, width), width) for s in slots]
        kept = jnp.concatenate([held[:, place] for place in places], axis=1)
        right = jnp.concatenate([v[place, :] for place in places], axis=0)
        result = (kept + nt(low_grad_out[...], right)).astype(BF)
        for i, s in enumerate(slots):
            d_inter[s] = result[:, i * width : (i + 1) * width]
            copy = pltpu.make_async_copy(d_inter.at[s], back.at[s], back_sems.at[s])
            copy.start()
            stores.append(copy)
    for copy in stores:
        copy.wait()


def dense(fmap, received, labels, v, u, cross_bias, h, hidden_bias, out_weight, scale):
    features, batch, width = received.shape
    total_width = features * width
    rank = v.shape[1]
    units = h.shape[1]
    vmem = pl.BlockSpec(memory_space=pltpu.VMEM)
    smem = pl.BlockSpec(memory_space=pltpu.SMEM)
    hbm = pl.BlockSpec(memory_space=pltpu.HBM)
    return pl.pallas_call(
        functools.partial(dense_kernel, scale),
        name="dense",
        in_specs=[smem, hbm, vmem, hbm, hbm, vmem, hbm, vmem, vmem],
        out_specs=[hbm] * 6 + [vmem] * 3,
        out_shape=[
            jax.ShapeDtypeStruct(received.shape, BF),
            jax.ShapeDtypeStruct(received.shape, BF),
            jax.ShapeDtypeStruct(received.shape, BF),
            jax.ShapeDtypeStruct((batch, rank), BF),
            jax.ShapeDtypeStruct((batch, rank), BF),
            jax.ShapeDtypeStruct((batch, units), BF),
            jax.ShapeDtypeStruct((1, total_width), F32),
            jax.ShapeDtypeStruct((1, units), F32),
            jax.ShapeDtypeStruct((1, units), F32),
        ],
        scratch_shapes=[
            pltpu.VMEM((batch, total_width), BF),
            pltpu.VMEM((batch, total_width), BF),
            pltpu.VMEM((batch, total_width), BF),
            pltpu.VMEM((batch, total_width), F32),
            pltpu.VMEM(received.shape, BF),
            pltpu.VMEM(v.shape, BF),
            pltpu.VMEM(u.shape, BF),
            pltpu.VMEM(h.shape, BF),
            pltpu.VMEM((batch, rank), BF),
            pltpu.VMEM((batch, rank), BF),
            pltpu.VMEM((batch, units), BF),
            pltpu.VMEM((batch, units), F32),
            pltpu.VMEM((batch, rank), F32),
            pltpu.SemaphoreType.DMA((features,)),
            pltpu.SemaphoreType.DMA((3,)),
            pltpu.SemaphoreType.DMA((3,)),
            pltpu.SemaphoreType.DMA((2, features)),
            pltpu.SemaphoreType.DMA((features,)),
        ],
        compiler_params=pltpu.CompilerParams(vmem_limit_bytes=DENSE_VMEM),
    )(fmap, received, labels, v, u, cross_bias, h, hidden_bias, out_weight)


def gradients_kernel(
    order,
    place,
    fmap,
    received,
    crossed,
    proj,
    low_hbm,
    low_grad_hbm,
    d_hidden_hbm,
    cross_bias_grad,
    hidden_bias_grad,
    out_weight_grad,
    *rest,
):
    parts, chunks = len(order), len(ORDER)
    outs = rest[: 2 * parts]
    inter_in, crossed_in, proj_in, low, low_grad, d_hidden = rest[2 * parts : 2 * parts + 6]
    low_t, low_grad_t, d_hidden_t, small, keep, send = rest[2 * parts + 6 : -5]
    slot_of, small_sems, inter_sems, wide_sems, out_sems = rest[-5:]
    features = fmap.shape[0]
    width = keep.shape[-1]
    rank = low_t.shape[0]
    each = features // chunks
    pair = 2
    share = each // pair

    smalls = [
        pltpu.make_async_copy(source, target, small_sems.at[i])
        for i, (source, target) in enumerate(
            ((low_hbm, low), (low_grad_hbm, low_grad), (d_hidden_hbm, d_hidden))
        )
    ]
    for copy in smalls:
        copy.start()
    for s in range(features):
        slot_of[fmap[s]] = s
    loads = []
    for part, offset in enumerate(order):
        base = lax.rem(place[1] + offset, chunks) * each
        span = pl.ds(part * each, each)
        copies = [
            pltpu.make_async_copy(crossed.at[pl.ds(base, each)], crossed_in.at[span], wide_sems.at[0, part]),
            pltpu.make_async_copy(proj.at[pl.ds(base, each)], proj_in.at[span], wide_sems.at[1, part]),
        ]
        for i in range(each):
            n = part * each + i
            copies.append(
                pltpu.make_async_copy(
                    received.at[slot_of[base + i]], inter_in.at[n], inter_sems.at[n]
                )
            )
        loads.append(copies)
    for copy in loads[0]:
        copy.start()
    for copy in smalls:
        copy.wait()

    low_t[...] = low[...].astype(F32).T.astype(BF)
    low_grad_t[...] = low_grad[...].astype(F32).T.astype(BF)
    d_hidden_t[...] = d_hidden[...].astype(F32).T.astype(BF)
    quarters = 4
    units = hidden_bias_grad.shape[1]
    per = units // (features * quarters)
    mine = lax.broadcasted_iota(jnp.int32, (features, units), 0)
    unit = lax.broadcasted_iota(jnp.int32, (features, units), 1)
    mine = unit // (per * quarters) == mine
    unit = lax.broadcasted_iota(jnp.int32, (units, width), 0)
    lane = lax.broadcasted_iota(jnp.int32, (units, width), 1)
    within = unit % (per * quarters)
    spread = (within // per * (width // quarters) + within % per == lane).astype(F32)
    for i, grad in enumerate((hidden_bias_grad, out_weight_grad)):
        small[i] = jnp.dot(
            jnp.where(mine, grad[...], 0.0),
            spread,
            preferred_element_type=F32,
            precision=lax.Precision.HIGHEST,
        )
    line = lax.broadcasted_iota(jnp.int32, (EXTRA, width), 0)
    nothing = jnp.zeros((EXTRA, width), BF)
    first = place[0] == 0

    for part, offset in enumerate(order):
        for copy in loads[part]:
            copy.wait()
        if part + 1 < parts:
            for copy in loads[part + 1]:
                copy.start()

        @pl.loop(0, share)
        def _(k, part=part, offset=offset):
            base = lax.rem(place[1] + offset, chunks) * each + k * pair
            n = part * each + k * pair

            def product(left, right):
                both = jnp.concatenate([right[n + i] for i in range(pair)], axis=1)
                return jnp.dot(left[...], both, preferred_element_type=F32).astype(BF)

            of_v = product(low_grad_t, inter_in)
            of_u = product(low_t, proj_in)
            of_h = product(d_hidden_t, crossed_in)

            def fill(one, other):
                for i in range(pair):
                    lanes = slice(i * width, (i + 1) * width)
                    f = base + i
                    cross = cross_bias_grad[:, pl.ds(pl.multiple_of(f * width, width), width)]
                    extra = jnp.where(line == 0, cross, 0.0)
                    for j in range(2):
                        extra = jnp.where(line == j + 1, small[j, pl.ds(f, 1), :], extra)
                    one[n + i, 0, pl.ds(0, rank), :] = of_v[:, lanes]
                    one[n + i, 0, pl.ds(rank, EXTRA), :] = extra.astype(BF)
                    one[n + i, 1, pl.ds(0, rank), :] = of_u[:, lanes]
                    one[n + i, 1, pl.ds(rank, EXTRA), :] = nothing
                    other[n + i, 0, pl.ds(0, rank), :] = of_h[:rank, lanes]
                    other[n + i, 0, pl.ds(rank, EXTRA), :] = nothing
                    other[n + i, 1, pl.ds(0, rank), :] = of_h[rank:, lanes]
                    other[n + i, 1, pl.ds(rank, EXTRA), :] = nothing

            @pl.when(first)
            def _():
                fill(keep, send)

            @pl.when(jnp.logical_not(first))
            def _():
                fill(send, keep)

        span = pl.ds(part * each, each)
        pltpu.make_async_copy(send.at[span], outs[parts + part], out_sems.at[parts + part]).start()
        pltpu.make_async_copy(keep.at[span], outs[part], out_sems.at[part]).start()

    for part in range(parts):
        span = pl.ds(part * each, each)
        pltpu.make_async_copy(send.at[span], outs[parts + part], out_sems.at[parts + part]).wait()
        pltpu.make_async_copy(keep.at[span], outs[part], out_sems.at[part]).wait()


def gradients(order, place, fmap, received, crossed, proj, low, low_grad, d_hidden, *small):
    features, batch, width = received.shape
    rank, units = low.shape[1], d_hidden.shape[1]
    parts = len(order)
    held = features // len(ORDER) * parts
    part = jax.ShapeDtypeStruct((features // len(ORDER), 2, rank + EXTRA, width), BF)
    vmem = pl.BlockSpec(memory_space=pltpu.VMEM)
    smem = pl.BlockSpec(memory_space=pltpu.SMEM)
    hbm = pl.BlockSpec(memory_space=pltpu.HBM)
    outs = pl.pallas_call(
        functools.partial(gradients_kernel, order),
        name="gradients",
        in_specs=[smem, smem] + [hbm] * 6 + [vmem] * 3,
        out_specs=[hbm] * (2 * parts),
        out_shape=[part] * (2 * parts),
        scratch_shapes=[pltpu.VMEM((held, batch, width), BF)] * 3
        + [
            pltpu.VMEM((batch, rank), BF),
            pltpu.VMEM((batch, rank), BF),
            pltpu.VMEM((batch, units), BF),
            pltpu.VMEM((rank, batch), BF),
            pltpu.VMEM((rank, batch), BF),
            pltpu.VMEM((units, batch), BF),
            pltpu.VMEM((2, features, width), F32),
            pltpu.VMEM((held, 2, rank + EXTRA, width), BF),
            pltpu.VMEM((held, 2, rank + EXTRA, width), BF),
            pltpu.SMEM((features,), jnp.int32),
            pltpu.SemaphoreType.DMA((3,)),
            pltpu.SemaphoreType.DMA((held,)),
            pltpu.SemaphoreType.DMA((2, parts)),
            pltpu.SemaphoreType.DMA((2 * parts,)),
        ],
        compiler_params=pltpu.CompilerParams(vmem_limit_bytes=GRADIENTS_VMEM),
        cost_estimate=pl.CostEstimate(
            flops=2 * batch * held * width * (2 * rank + units),
            bytes_accessed=held << 19,
            transcendentals=0,
        ),
    )(place, fmap, received, crossed, proj, low, low_grad, d_hidden, *small)
    return outs[:parts], outs[parts:]


def neighbours(axis):
    size = lax.axis_size(axis)
    up = [(i, (i + 1) % size) for i in range(size)]
    down = [(i, (i - 1) % size) for i in range(size)]
    return (
        lambda value: lax.ppermute(value, axis, up),
        lambda value: lax.ppermute(value, axis, down),
    )


def add(*terms):
    total = terms[0].astype(F32)
    for term in terms[1:]:
        total = total + term.astype(F32)
    return total.astype(BF)


def ring_parts(axis, opposite, following, preceding):
    up, down = neighbours(axis)
    passed = (down(opposite[0]), up(opposite[1]))
    from_following = down(jnp.concatenate([add(preceding[0], passed[0]), preceding[1]], axis=0))
    from_preceding = up(jnp.concatenate([following[0], add(following[1], passed[1])], axis=0))
    return from_following, from_preceding


def ring_spread(axis, own):
    up, down = neighbours(axis)
    preceding, following = up(own), down(own)
    half = own.shape[0] // 2
    return own, following, down(following[:half]), up(preceding[half:]), preceding


def body(
    embedding_table,
    touched_blocks,
    bag_index,
    bag_count,
    feature_map,
    labels,
    v_weight,
    u_weight,
    cross_bias,
    hidden_weight,
    hidden_bias,
    out_weight,
):
    dp = ("x", "zh", "zl", "core")
    features = feature_map.shape[0]
    rows, width = embedding_table.shape
    samples = bag_index.shape[1]
    tile = samples // touched_blocks.shape[1]
    batch = labels.shape[0]
    rank = v_weight.shape[1]
    units = hidden_weight.shape[1]
    roles = lax.axis_size("role")
    total = roles * lax.axis_size(dp) * batch
    core = lax.axis_index("core")
    role = lax.axis_index("role")

    touched = touched_blocks[0].T
    pooled, incidence = pool(touched, embedding_table, bag_index[0].T, bag_count[0].T, tile)
    received = lax.all_to_all(
        pooled.reshape(features, batch, width), dp, split_axis=0, concat_axis=0, tiled=True
    )
    back, crossed, proj, low, low_grad, d_hidden, cross_g, hidden_g, out_g = dense(
        feature_map,
        received,
        labels.reshape(batch, 1),
        v_weight,
        u_weight,
        cross_bias.reshape(1, -1),
        hidden_weight,
        hidden_bias.reshape(1, -1),
        out_weight.reshape(1, -1),
        LOSS_SCALE / total,
    )
    returned = lax.all_to_all(back, dp, split_axis=0, concat_axis=0, tiled=True)

    quarters = 4
    share = width // quarters
    per = units // (features * quarters)

    swap = [(0, 1), (1, 0)]
    each = features // roles
    keep, send = gradients(
        ORDER,
        jnp.stack([core, role]),
        feature_map,
        received,
        crossed,
        proj,
        low,
        low_grad,
        d_hidden,
        cross_g,
        hidden_g,
        out_g,
    )
    halves = []
    for mine, sent in zip(keep, send):
        other = lax.ppermute(sent, "core", [(0, 1), (1, 0)])
        cuts = (slice(0, each // 2), slice(each // 2, each))
        halves.append([add(mine[cut], other[cut]) for cut in cuts])

    local = scatter(touched, incidence, returned.reshape(samples, width), rows, roles)
    parts = lax.all_to_all(local, "role", split_axis=0, concat_axis=0, tiled=True)
    others, parts = lax.optimization_barrier((ring_parts("role", *halves[:3]), parts))
    role_sum = add(jnp.concatenate(halves[3], axis=0), *others)
    pieces = lax.all_to_all(
        role_sum.reshape(each * 2, rank + EXTRA, width),
        ("x", "zh", "zl"),
        split_axis=0,
        concat_axis=0,
        tiled=True,
    )
    piece = jnp.sum(pieces.astype(F32), axis=0)
    shares = lax.all_to_all(piece.T, ("zl", "core"), split_axis=0, concat_axis=0, tiled=True)
    shares = shares.reshape(quarters, share, rank + EXTRA)
    grad_v = shares[0, :, :rank]
    grad_u = shares[2, :, :rank].T
    grad_h = jnp.concatenate([shares[1, :, :rank], shares[3, :, :rank]], axis=1)
    grad_cb = shares[0, :, rank]
    grad_hb = shares[0, :per, rank + 1]
    grad_ow = shares[0, :per, rank + 2]

    part = add(*parts)
    table_grad = spread_rows(role.reshape(1), ring_spread("role", part), roles)
    return (table_grad, grad_v, grad_u, grad_cb, grad_h, grad_hb, grad_ow)


def solution(mesh):
    fine = Mesh(mesh.devices.reshape(4, 4, 2, 2, 2), ("role", "x", "zh", "zl", "core"))
    dp = ("x", "zh", "zl", "core")
    everywhere = ("role",) + dp
    return jax.shard_map(
        body,
        mesh=fine,
        in_specs=(
            P(dp, None),
            P(dp, "role", None),
            P(dp, "role", None),
            P(dp, "role", None),
            P(),
            P(everywhere),
            P(),
            P(),
            P(),
            P(),
            P(),
            P(),
        ),
        out_specs=(
            P(dp, None),
            P(everywhere, None),
            P(None, everywhere),
            P(everywhere),
            P(everywhere, None),
            P(everywhere),
            P(everywhere),
        ),
        check_vma=False,
    )
```

time: 229 us -> 204 us (0.89)
  Pallas kernels: 62 us -> 53.6 us
  starting transfers between devices: 53.3 us -> 46.3 us
  waiting for transfers between devices: 87.3 us -> 82.7 us
  other arithmetic: 13 us -> 10.6 us
    ppermute x8 -> x4, waiting for transfers between devices: 39.4 us -> 8.36 us  [neighbours(): lax.ppermute(value, axis, up)]
    ppermute x8 -> x4, waiting for transfers between devices: 3.01 us -> 17.6 us  [neighbours(): lax.ppermute(value, axis, down)]
    all_to_all x0 -> x1, waiting for transfers between devices: none -> 10.5 us  [body(): lax.all_to_all(local, 'role', split_axis=0, concat_axis=0, tiled=True)]
    pallas_call x3, Pallas kernels: 38.4 us -> 33.1 us  [the longest x1 13.3 us: gradients(): pl.pallas_call(functools.partial(gradients_kernel, order), name='gradient...]
    all_to_all x1, waiting for transfers between devices: 0.01 us -> 5.09 us  [body(): lax.all_to_all(role_sum.reshape(each * 2, rank + EXTRA, width), ('x', 'zh...]
    all_to_all x1, starting transfers between devices: 12.1 us -> 7.69 us  [body(): lax.all_to_all(piece.T, ('zl', 'core'), split_axis=0, concat_axis=0, tile...]
    all_to_all x0 -> x1, starting transfers between devices: none -> 4.33 us  [body(): lax.all_to_all(local, 'role', split_axis=0, concat_axis=0, tiled=True)]
    pallas_call x1, Pallas kernels: 22.1 us -> 17.9 us  [dense(): pl.pallas_call(functools.partial(dense_kernel, scale), name='dense', in_s...]
  transfers between devices with their start and end apart: 25 -> 17, of which waited for: 11 -> 10; matrix products, arithmetic and copies ran while one was open for 7% -> 4% of each run, Pallas kernels for 12% -> 11%
where the time goes in v3:
time: 204 us; the launch traced here: 203 us
  waiting for transfers between devices  82.7 us (41%)
  Pallas kernels  53.6 us (26%)
  starting transfers between devices  46.3 us (23%)
  other arithmetic  10.6 us (5%)
  local copies, waits for them, and re-layouts  8.91 us (4%)
    all_to_all x1, waiting for transfers between devices, body(): lax.all_to_all(pooled.reshape(features, batch, width), dp, split_axis=0,...  37.8 us
    pallas_call x1, Pallas kernels, dense(): pl.pallas_call(functools.partial(dense_kernel, scale), name='dense', in_s...  17.9 us
    ppermute x4, waiting for transfers between devices, neighbours(): lax.ppermute(value, axis, down)  17.6 us
    pallas_call x1, Pallas kernels, gradients(): pl.pallas_call(functools.partial(gradients_kernel, order), name='gradient...  13.3 us
    pallas_call x1, Pallas kernels, pool(): pl.pallas_call(pool_kernel, name='pool', in_specs=[pl.BlockSpec(memory_sp...  12.7 us
    ppermute x4, starting transfers between devices, neighbours(): lax.ppermute(value, axis, down)  12 us
    all_to_all x1, waiting for transfers between devices, body(): lax.all_to_all(local, 'role', split_axis=0, concat_axis=0, tiled=True)  10.5 us
    all_to_all x1, starting transfers between devices, body(): lax.all_to_all(pooled.reshape(features, batch, width), dp, split_axis=0,...  9.45 us
  transfers between devices with their start and end apart: 17, of which 10 were waited for; matrix products, arithmetic and copies ran while one was open for 4% of the time, Pallas kernels for 11%

profile of v3, /device:TPU:1, one launch (start us, length us, event | category | flops | bytes accessed | tf_op | source)
XLA Modules:
  0.0 202.9 jit_solution(6169519285318279960)
XLA Ops:
  0.6 12.7 %pool.1 = (bf16[12288,128]{1,0:T(8,128)(2,1)}, bf16[96,128,128]{2,1,0:T(8,128)(2,1)}) custom-call(s32[16,96]{1,0:T(8,128)} %bitcast.36, bf16[4096,128]{1,0:T(8,128)(2,1)} %table.1, s32[16,12288]{1,0:T(8,128)} %bitcast.32, s32[16,12288]{1,0:T(8,128)} %bitcast.33), custom_call_target="tpu_custom_call" | custom-call | tf_op jit(solution)/shard_map/pool/pallas_call | solution.py:96
  13.3 9.5 %all-to-all-start = ((bf16[32,384,128]{2,1,0:T(8,128)(2,1)}), bf16[32,384,128]{2,1,0:T(8,128)(2,1)S(1)}, u32[]{:S(2)}, u32[]{:S(2)}) async-start(bf16[32,384,128]{2,1,0:T(8,128)(2,1)} %bitcast.31), calls=%async_computation | async-start | bytes 6291456 | tf_op jit(solution)/shard_map/all_to_all | solution.py:658
  22.8 0.6 reshape.55.out_weight
  23.4 0.8 reshape.58.labels
  24.2 0.6 pad_add_fusion.place
  24.8 37.8 %all-to-all-done.received = bf16[32,384,128]{2,1,0:T(8,128)(2,1)S(1)} async-done(((bf16[32,384,128]{2,1,0:T(8,128)(2,1)}), bf16[32,384,128]{2,1,0:T(8,128)(2,1)S(1)}, u32[]{:S(2)}, u32[]{:S(2)}) %all-to-all-start) | async-done | bytes 3145760 | tf_op jit(solution)/shard_map/all_to_all | solution.py:658
  62.6 1.7 copy-done
  64.3 17.9 %dense.1 = (bf16[32,384,128]{2,1,0:T(8,128)(2,1)}, bf16[32,384,128]{2,1,0:T(8,128)(2,1)}, bf16[32,384,128]{2,1,0:T(8,128)(2,1)}, bf16[384,256]{1,0:T(8,128)(2,1)...) custom-call(s32[32]{0:T(128)} %fmap.3, ...), custom_call_target="tpu_custom_call" | custom-call | tf_op jit(solution)/shard_map/dense/pallas_call | solution.py:378
  82.2 5.0 %all-to-all-start.1 = ((bf16[32,384,128]{2,1,0:T(8,128)(2,1)}), bf16[32,384,128]{2,1,0:T(8,128)(2,1)S(1)}, u32[]{:S(2)}, u32[]{:S(2)}) async-start(bf16[32,384,128]{2,1,0:T(8,128)(2,1)} %get-tuple-element.45), calls=%async_computation.1 | async-start | bytes 6291456 | tf_op jit(solution)/shard_map/all_to_all | solution.py:673
  87.2 13.3 %gradients.1 = (bf16[8,2,272,128]{3,2,1,0:T(8,128)(2,1)}, bf16[8,2,272,128]{3,2,1,0:T(8,128)(2,1)}, bf16[8,2,272,128]{3,2,1,0:T(8,128)(2,1)}, bf16[8,2,272,128]{...) custom-call(s32[2]{0:T(128)} %pad_add_fusion.place, ...), custom_call_target="tpu_custom_call" | custom-call | flops 3221225472 | bytes 16777216 | tf_op jit(solution)/shard_map/gradients/pallas_call | solution.py:564
  100.5 0.3 collective-permute-start.1
  100.8 0.3 collective-permute-start
  101.0 0.2 collective-permute-start.4
  101.3 2.2 %collective-permute-done.1 = bf16[8,2,272,128]{3,2,1,0:T(8,128)(2,1)S(1)} collective-permute-done((bf16[8,2,272,128]{3,2,1,0:T(8,128)(2,1)}, bf16[8,2,272,128]{3,2,1,0:T(8,128)(2,1)S(1)}, u32[]{:S(2)}, u32[]{:S(2)}) %collective-permute-start.1) | collective-permute-done | bytes 1114144 | tf_op jit(solution)/shard_map/ppermute | solution.py:697
  103.5 1.6 add_convert_fusion.4
  105.1 3.0 %collective-permute-start.2 = (bf16[4,2,272,128]{3,2,1,0:T(8,128)(2,1)S(1)}, bf16[4,2,272,128]{3,2,1,0:T(8,128)(2,1)S(1)}, u32[]{:S(2)}, u32[]{:S(2)}) collective-permute-start(bf16[4,2,272,128]{3,2,1,0:T(8,128)(2,1)S(1)} %get-tuple-element.58), channel_id=1, source_target_pairs={{0,96},{32,0},{64,32},{96,64},{1,97},{33,1},{65,33},{97,65},{2,98}... | collective-permute-start | bytes 1671176 | tf_op jit(solution)/shard_map/ppermute | solution.py:603
  108.1 0.5 collective-permute-start.11
  108.6 11.3 %collective-permute-done.2 = bf16[4,2,272,128]{3,2,1,0:T(8,128)(2,1)S(1)} collective-permute-done((bf16[4,2,272,128]{3,2,1,0:T(8,128)(2,1)S(1)}, bf16[4,2,272,128]{3,2,1,0:T(8,128)(2,1)S(1)}, u32[]{:S(2)}, u32[]{:S(2)}) %collective-permute-start.2) | collective-permute-done | bytes 557088 | tf_op jit(solution)/shard_map/ppermute | solution.py:603
  119.9 0.4 add_convert_fusion.8
  120.3 1.1 pad_maximum_fusion
  121.4 3.4 %collective-permute-start.3 = (bf16[8,2,272,128]{3,2,1,0:T(8,128)(2,1)}, bf16[8,2,272,128]{3,2,1,0:T(8,128)(2,1)}, u32[]{:S(2)}, u32[]{:S(2)}) collective-permute-start(bf16[8,2,272,128]{3,2,1,0:T(8,128)(2,1)} %pad_maximum_fusion), channel_id=1, source_target_pairs={{0,96},{32,0},{64,32},{96,64},{1,97},{33,1},{65,33},{97,65},{2,98}... | collective-permute-start | bytes 3342344 | tf_op jit(solution)/shard_map/ppermute | solution.py:603
  124.8 0.4 add_convert_fusion.6
  125.1 1.1 pad_maximum_fusion.1
  126.2 0.7 all-to-all-done.1
  126.9 1.7 copy-done.1
  128.6 7.1 %scatter.1 = bf16[4,1024,128]{2,1,0:T(8,128)(2,1)} custom-call(s32[16,96]{1,0:T(8,128)} %bitcast.37, bf16[96,128,128]{2,1,0:T(8,128)(2,1)} %get-tuple-element.44.incidence, bf16[12288,128]{1,0:T(8,128)(2,1)} %bitcast.30), custom_call_target="tpu_custom_call" | custom-call | flops 8589934592 | bytes 8388608 | tf_op jit(solution)/shard_map/scatter/pallas_call | solution.py:169
  135.7 4.3 %all-to-all-start.2 = ((bf16[4,1024,128]{2,1,0:T(8,128)(2,1)}), bf16[4,1024,128]{2,1,0:T(8,128)(2,1)S(1)}, u32[]{:S(2)}, u32[]{:S(2)}) async-start(bf16[4,1024,128]{2,1,0:T(8,128)(2,1)} %scatter.1), calls=%async_computation.2 | async-start | bytes 2097152 | tf_op jit(solution)/shard_map/all_to_all | solution.py:702
  140.1 1.5 add_convert_fusion.2
  141.6 6.3 %collective-permute-done.3 = bf16[8,2,272,128]{3,2,1,0:T(8,128)(2,1)} collective-permute-done((bf16[8,2,272,128]{3,2,1,0:T(8,128)(2,1)}, bf16[8,2,272,128]{3,2,1,0:T(8,128)(2,1)}, u32[]{:S(2)}, u32[]{:S(2)}) %collective-permute-start.3) | collective-permute-done | bytes 1114144 | tf_op jit(solution)/shard_map/ppermute | solution.py:603
  147.9 4.6 %collective-permute-done.6 = bf16[8,2,272,128]{3,2,1,0:T(8,128)(2,1)} collective-permute-done((bf16[8,2,272,128]{3,2,1,0:T(8,128)(2,1)}, bf16[8,2,272,128]{3,2,1,0:T(8,128)(2,1)}, u32[]{:S(2)}, u32[]{:S(2)}) %collective-permute-start.6) | collective-permute-done | bytes 1114144 | tf_op jit(solution)/shard_map/ppermute | solution.py:602
  152.5 10.5 %all-to-all-done.2 = bf16[4,1024,128]{2,1,0:T(8,128)(2,1)S(1)} async-done(((bf16[4,1024,128]{2,1,0:T(8,128)(2,1)}), bf16[4,1024,128]{2,1,0:T(8,128)(2,1)S(1)}, u32[]{:S(2)}, u32[]{:S(2)}) %all-to-all-start.2) | async-done | bytes 1048608 | tf_op jit(solution)/shard_map/all_to_all | solution.py:702
  163.0 3.0 %add_convert_fusion = bf16[8,2,272,128]{3,2,1,0:T(8,128)(2,1)} fusion(bf16[8,2,272,128]{3,2,1,0:T(8,128)(2,1)} %collective-permute-done.6, bf16[8,2,272,128]{3,2,1,0:T(8,128)(2,1)} %collective-permute-done.3, bf16[4,2,272,128]{3,2,1,0:T(8,128)(2,1)S(1)} %get-tuple-element.54, bf16[4,2,272,128]{3,2,1,0:T(8,128)(2,1)S(1)} %get-tuple-element.53), kind=kLoop, calls=%fused_computation.1 | loop fusion | flops 3899392 | bytes 4456448 | tf_op jit(solution)/shard_map/convert_element_type | solution.py:611
  166.0 6.4 %all-to-all-start.3 = ((bf16[16,272,128]{2,1,0:T(8,128)(2,1)}), bf16[16,272,128]{2,1,0:T(8,128)(2,1)S(1)}, u32[]{:S(2)}, u32[]{:S(2)}) async-start(bf16[16,272,128]{2,1,0:T(8,128)(2,1)} %bitcast.14), calls=%async_computation.3 | async-start | bytes 2228224 | tf_op jit(solution)/shard_map/all_to_all | solution.py:705
  172.6 2.7 %collective-permute-start.7 = (bf16[1024,128]{1,0:T(8,128)(2,1)S(1)}, bf16[1024,128]{1,0:T(8,128)(2,1)S(1)}, u32[]{:S(2)}, u32[]{:S(2)}) collective-permute-start(bf16[1024,128]{1,0:T(8,128)(2,1)S(1)} %fusion.own), channel_id=1, source_target_pairs={{0,96},{32,0},{64,32},{96,64},{1,97},{33,1},{65,33},{97,65},{2,98}... | collective-permute-start | bytes 786440 | tf_op jit(solution)/shard_map/ppermute | solution.py:603
  175.3 3.8 %collective-permute-done.9.preceding = bf16[1024,128]{1,0:T(8,128)(2,1)S(1)} collective-permute-done((bf16[1024,128]{1,0:T(8,128)(2,1)S(1)}, bf16[1024,128]{1,0:T(8,128)(2,1)S(1)}, u32[]{:S(2)}, u32[]{:S(2)}) %collective-permute-start.9) | collective-permute-done | bytes 262176 | tf_op jit(solution)/shard_map/ppermute | solution.py:602
  179.2 2.9 %collective-permute-start.8 = (bf16[512,128]{1,0:T(8,128)(2,1)S(1)}, bf16[512,128]{1,0:T(8,128)(2,1)S(1)}, u32[]{:S(2)}, u32[]{:S(2)}) collective-permute-start(bf16[512,128]{1,0:T(8,128)(2,1)S(1)} %slice.106), channel_id=1, source_target_pairs={{0,96},{32,0},{64,32},{96,64},{1,97},{33,1},{65,33},{97,65},{2,98}... | collective-permute-start | bytes 393224 | tf_op jit(solution)/shard_map/ppermute | solution.py:603
  182.1 5.1 %all-to-all-done.3 = bf16[16,272,128]{2,1,0:T(8,128)(2,1)S(1)} async-done(((bf16[16,272,128]{2,1,0:T(8,128)(2,1)}), bf16[16,272,128]{2,1,0:T(8,128)(2,1)S(1)}, u32[]{:S(2)}, u32[]{:S(2)}) %all-to-all-start.3) | async-done | bytes 1114144 | tf_op jit(solution)/shard_map/all_to_all | solution.py:705
  187.2 0.2 convert_reduce_fusion
  187.3 0.8 copy.23
  188.2 7.7 %all-to-all-start.4 = ((f32[4,32,272]{2,1,0:T(8,128)}), f32[4,32,272]{2,1,0:T(8,128)S(1)}, u32[]{:S(2)}, u32[]{:S(2)}) async-start(f32[4,32,272]{2,1,0:T(8,128)} %bitcast.16), calls=%async_computation.4 | async-start | bytes 393216 | tf_op jit(solution)/shard_map/all_to_all | solution.py:713
  195.9 0.6 copy-done.8
  196.5 0.6 copy-done.9
  197.1 2.7 %spread_rows.1 = f32[4096,128]{1,0:T(8,128)} custom-call(s32[1]{0:T(128)} %bitcast.role, bf16[1024,128]{1,0:T(8,128)(2,1)} %copy-done.5, bf16[1024,128]{1,0:T(8,128)(2,1)} %copy-done.7, bf16[512,128]{1,0:T(8,128)(2,1)} %copy-done.9, bf16[512,128]{1,0:T(8,128)(2,1)} %copy-done.8, bf16[1024,128]{1,0:T(8,128)(2,1)} %copy-done.6), custom_call_target="tpu_custom_call" | custom-call | tf_op jit(solution)/shard_map/spread_rows/pallas_call | solution.py:205
  199.8 0.5 all-to-all-done.4
  200.3 0.6 slice_bitcast_fusion.1
  200.9 0.6 pad_maximum_fusion.2
  201.6 0.6 slice_reduce_fusion
  202.2 0.7 slice_reduce_fusion.1
  (34 shorter events, 0.4 us)
Async XLA Ops:
  13.3 9.5 %copy-start.11 = (bf16[512]{0:T(512)(128)(2,1)S(1)}, bf16[512]{0:T(512)(128)(2,1)}, u32[]{:S(2)}) copy-start(bf16[512]{0:T(512)(128)(2,1)} %param.23) | copy-start | bytes 3076
  13.3 10.1 %copy-start.10 = (s32[384]{0:T(512)S(1)}, s32[384]{0:T(512)}, u32[]{:S(2)}) copy-start(s32[384]{0:T(512)} %param.17) | copy-start | bytes 4612
  13.3 49.2 %all-to-all-start = ((bf16[32,384,128]{2,1,0:T(8,128)(2,1)}), bf16[32,384,128]{2,1,0:T(8,128)(2,1)S(1)}, u32[]{:S(2)}, u32[]{:S(2)}) async-start(bf16[32,384,128]{2,1,0:T(8,128)(2,1)} %bitcast.31), calls=%async_computation | async-start | bytes 6291456 | tf_op jit(solution)/shard_map/all_to_all | solution.py:658
  62.6 1.7 copy-start
  82.2 44.8 %all-to-all-start.1 = ((bf16[32,384,128]{2,1,0:T(8,128)(2,1)}), bf16[32,384,128]{2,1,0:T(8,128)(2,1)S(1)}, u32[]{:S(2)}, u32[]{:S(2)}) async-start(bf16[32,384,128]{2,1,0:T(8,128)(2,1)} %get-tuple-element.45), calls=%async_computation.1 | async-start | bytes 6291456 | tf_op jit(solution)/shard_map/all_to_all | solution.py:673
  100.5 3.0 %collective-permute-start.1 = (bf16[8,2,272,128]{3,2,1,0:T(8,128)(2,1)}, bf16[8,2,272,128]{3,2,1,0:T(8,128)(2,1)S(1)}, u32[]{:S(2)}, u32[]{:S(2)}) collective-permute-start(bf16[8,2,272,128]{3,2,1,0:T(8,128)(2,1)} %get-tuple-element.41), channel_id=1, source_target_pairs={{0,1},{1,0},{2,3},{3,2},{4,5},{5,4},{6,7},{7,6},{8,9},{9,8},{10,11... | collective-permute-start | bytes 3342344 | tf_op jit(solution)/shard_map/ppermute | solution.py:697
  100.8 7.8 %collective-permute-start = (bf16[8,2,272,128]{3,2,1,0:T(8,128)(2,1)}, bf16[8,2,272,128]{3,2,1,0:T(8,128)(2,1)S(1)}, u32[]{:S(2)}, u32[]{:S(2)}) collective-permute-start(bf16[8,2,272,128]{3,2,1,0:T(8,128)(2,1)} %get-tuple-element.39), channel_id=1, source_target_pairs={{0,1},{1,0},{2,3},{3,2},{4,5},{5,4},{6,7},{7,6},{8,9},{9,8},{10,11... | collective-permute-start | bytes 3342344 | tf_op jit(solution)/shard_map/ppermute | solution.py:697
  101.0 23.7 %collective-permute-start.4 = (bf16[8,2,272,128]{3,2,1,0:T(8,128)(2,1)}, bf16[8,2,272,128]{3,2,1,0:T(8,128)(2,1)S(1)}, u32[]{:S(2)}, u32[]{:S(2)}) collective-permute-start(bf16[8,2,272,128]{3,2,1,0:T(8,128)(2,1)} %get-tuple-element.43), channel_id=1, source_target_pairs={{0,1},{1,0},{2,3},{3,2},{4,5},{5,4},{6,7},{7,6},{8,9},{9,8},{10,11... | collective-permute-start | bytes 3342344 | tf_op jit(solution)/shard_map/ppermute | solution.py:697
  103.5 16.4 %copy-start.4 = (bf16[8,2,272,128]{3,2,1,0:T(8,128)(2,1)S(1)}, bf16[8,2,272,128]{3,2,1,0:T(8,128)(2,1)}, u32[]{:S(2)}) copy-start(bf16[8,2,272,128]{3,2,1,0:T(8,128)(2,1)} %get-tuple-element.38) | copy-start | bytes 3342340
  105.1 14.8 %collective-permute-start.2 = (bf16[4,2,272,128]{3,2,1,0:T(8,128)(2,1)S(1)}, bf16[4,2,272,128]{3,2,1,0:T(8,128)(2,1)S(1)}, u32[]{:S(2)}, u32[]{:S(2)}) collective-permute-start(bf16[4,2,272,128]{3,2,1,0:T(8,128)(2,1)S(1)} %get-tuple-element.58), channel_id=1, source_target_pairs={{0,96},{32,0},{64,32},{96,64},{1,97},{33,1},{65,33},{97,65},{2,98}... | collective-permute-start | bytes 1671176 | tf_op jit(solution)/shard_map/ppermute | solution.py:603
  108.1 16.7 %collective-permute-start.5 = (bf16[4,2,272,128]{3,2,1,0:T(8,128)(2,1)S(1)}, bf16[4,2,272,128]{3,2,1,0:T(8,128)(2,1)S(1)}, u32[]{:S(2)}, u32[]{:S(2)}) collective-permute-start(bf16[4,2,272,128]{3,2,1,0:T(8,128)(2,1)S(1)} %get-tuple-element.57), channel_id=1, source_target_pairs={{0,32},{32,64},{64,96},{96,0},{1,33},{33,65},{65,97},{97,1},{2,34}... | collective-permute-start | bytes 1671176 | tf_op jit(solution)/shard_map/ppermute | solution.py:602
  108.1 32.0 %collective-permute-start.11 = (bf16[8,2,272,128]{3,2,1,0:T(8,128)(2,1)}, bf16[8,2,272,128]{3,2,1,0:T(8,128)(2,1)}, u32[]{:S(2)}, u32[]{:S(2)}) collective-permute-start(bf16[8,2,272,128]{3,2,1,0:T(8,128)(2,1)} %get-tuple-element.48), channel_id=1, source_target_pairs={{0,1},{1,0},{2,3},{3,2},{4,5},{5,4},{6,7},{7,6},{8,9},{9,8},{10,11... | collective-permute-start | bytes 3342344 | tf_op jit(solution)/shard_map/ppermute | solution.py:697
  120.2 4.5 %copy-start.3 = (bf16[8,2,272,128]{3,2,1,0:T(8,128)(2,1)S(1)}, bf16[8,2,272,128]{3,2,1,0:T(8,128)(2,1)}, u32[]{:S(2)}) copy-start(bf16[8,2,272,128]{3,2,1,0:T(8,128)(2,1)} %get-tuple-element.42) | copy-start | bytes 3342340
  121.4 26.5 %collective-permute-start.3 = (bf16[8,2,272,128]{3,2,1,0:T(8,128)(2,1)}, bf16[8,2,272,128]{3,2,1,0:T(8,128)(2,1)}, u32[]{:S(2)}, u32[]{:S(2)}) collective-permute-start(bf16[8,2,272,128]{3,2,1,0:T(8,128)(2,1)} %pad_maximum_fusion), channel_id=1, source_target_pairs={{0,96},{32,0},{64,32},{96,64},{1,97},{33,1},{65,33},{97,65},{2,98}... | collective-permute-start | bytes 3342344 | tf_op jit(solution)/shard_map/ppermute | solution.py:603
  126.2 26.3 %collective-permute-start.6 = (bf16[8,2,272,128]{3,2,1,0:T(8,128)(2,1)}, bf16[8,2,272,128]{3,2,1,0:T(8,128)(2,1)}, u32[]{:S(2)}, u32[]{:S(2)}) collective-permute-start(bf16[8,2,272,128]{3,2,1,0:T(8,128)(2,1)} %pad_maximum_fusion.1), channel_id=1, source_target_pairs={{0,32},{32,64},{64,96},{96,0},{1,33},{33,65},{65,97},{97,1},{2,34}... | collective-permute-start | bytes 3342344 | tf_op jit(solution)/shard_map/ppermute | solution.py:602
  126.9 1.7 copy-start.1
  135.7 4.3 %copy-start.2 = (bf16[8,2,272,128]{3,2,1,0:T(8,128)(2,1)S(1)}, bf16[8,2,272,128]{3,2,1,0:T(8,128)(2,1)}, u32[]{:S(2)}) copy-start(bf16[8,2,272,128]{3,2,1,0:T(8,128)(2,1)} %get-tuple-element.47) | copy-start | bytes 3342340
  135.7 27.2 %all-to-all-start.2 = ((bf16[4,1024,128]{2,1,0:T(8,128)(2,1)}), bf16[4,1024,128]{2,1,0:T(8,128)(2,1)S(1)}, u32[]{:S(2)}, u32[]{:S(2)}) async-start(bf16[4,1024,128]{2,1,0:T(8,128)(2,1)} %scatter.1), calls=%async_computation.2 | async-start | bytes 2097152 | tf_op jit(solution)/shard_map/all_to_all | solution.py:702
  166.0 21.2 %all-to-all-start.3 = ((bf16[16,272,128]{2,1,0:T(8,128)(2,1)}), bf16[16,272,128]{2,1,0:T(8,128)(2,1)S(1)}, u32[]{:S(2)}, u32[]{:S(2)}) async-start(bf16[16,272,128]{2,1,0:T(8,128)(2,1)} %bitcast.14), calls=%async_computation.3 | async-start | bytes 2228224 | tf_op jit(solution)/shard_map/all_to_all | solution.py:705
  172.5 15.6 %copy-start.5 = (bf16[1024,128]{1,0:T(8,128)(2,1)}, bf16[1024,128]{1,0:T(8,128)(2,1)S(1)}, u32[]{:S(2)}) copy-start(bf16[1024,128]{1,0:T(8,128)(2,1)S(1)} %fusion.own) | copy-start | bytes 786436
  172.5 6.5 %collective-permute-start.9 = (bf16[1024,128]{1,0:T(8,128)(2,1)S(1)}, bf16[1024,128]{1,0:T(8,128)(2,1)S(1)}, u32[]{:S(2)}, u32[]{:S(2)}) collective-permute-start(bf16[1024,128]{1,0:T(8,128)(2,1)S(1)} %fusion.own), channel_id=1, source_target_pairs={{0,32},{32,64},{64,96},{96,0},{1,33},{33,65},{65,97},{97,1},{2,34}... | collective-permute-start | bytes 786440 | tf_op jit(solution)/shard_map/ppermute | solution.py:602
  172.6 6.5 %collective-permute-start.7 = (bf16[1024,128]{1,0:T(8,128)(2,1)S(1)}, bf16[1024,128]{1,0:T(8,128)(2,1)S(1)}, u32[]{:S(2)}, u32[]{:S(2)}) collective-permute-start(bf16[1024,128]{1,0:T(8,128)(2,1)S(1)} %fusion.own), channel_id=1, source_target_pairs={{0,96},{32,0},{64,32},{96,64},{1,97},{33,1},{65,33},{97,65},{2,98}... | collective-permute-start | bytes 786440 | tf_op jit(solution)/shard_map/ppermute | solution.py:603
  179.0 9.1 %copy-start.6 = (bf16[1024,128]{1,0:T(8,128)(2,1)}, bf16[1024,128]{1,0:T(8,128)(2,1)S(1)}, u32[]{:S(2)}) copy-start(bf16[1024,128]{1,0:T(8,128)(2,1)S(1)} %collective-permute-done.9.preceding) | copy-start | bytes 786436
  179.1 16.8 %collective-permute-start.10 = (bf16[512,128]{1,0:T(8,128)(2,1)S(1)}, bf16[512,128]{1,0:T(8,128)(2,1)S(1)}, u32[]{:S(2)}, u32[]{:S(2)}) collective-permute-start(bf16[512,128]{1,0:T(8,128)(2,1)S(1)} %slice.107), channel_id=1, source_target_pairs={{0,32},{32,64},{64,96},{96,0},{1,33},{33,65},{65,97},{97,1},{2,34}... | collective-permute-start | bytes 393224 | tf_op jit(solution)/shard_map/ppermute | solution.py:602
  179.1 9.0 %copy-start.7 = (bf16[1024,128]{1,0:T(8,128)(2,1)}, bf16[1024,128]{1,0:T(8,128)(2,1)S(1)}, u32[]{:S(2)}) copy-start(bf16[1024,128]{1,0:T(8,128)(2,1)S(1)} %collective-permute-done.7.following) | copy-start | bytes 786436
  179.2 16.7 %collective-permute-start.8 = (bf16[512,128]{1,0:T(8,128)(2,1)S(1)}, bf16[512,128]{1,0:T(8,128)(2,1)S(1)}, u32[]{:S(2)}, u32[]{:S(2)}) collective-permute-start(bf16[512,128]{1,0:T(8,128)(2,1)S(1)} %slice.106), channel_id=1, source_target_pairs={{0,96},{32,0},{64,32},{96,64},{1,97},{33,1},{65,33},{97,65},{2,98}... | collective-permute-start | bytes 393224 | tf_op jit(solution)/shard_map/ppermute | solution.py:603
  188.2 12.2 %all-to-all-start.4 = ((f32[4,32,272]{2,1,0:T(8,128)}), f32[4,32,272]{2,1,0:T(8,128)S(1)}, u32[]{:S(2)}, u32[]{:S(2)}) async-start(f32[4,32,272]{2,1,0:T(8,128)} %bitcast.16), calls=%async_computation.4 | async-start | bytes 393216 | tf_op jit(solution)/shard_map/all_to_all | solution.py:713
  195.8 0.6 copy-start.8
  196.5 0.6 copy-start.9

commit v4 on v3

--- a/solution.py
+++ b/solution.py
@@ -10,9 +10,10 @@
 
 BLK = 8
 LOSS_SCALE = 65536.0
-STEP_TILES = 8
+STEP_TILES = 16
 WIDE = 2048
 EXTRA = 16
+PAIR = 4
 ORDER = (2, 1, 3, 0)
 VMEM = 60 << 20
 POOL_VMEM = VMEM
@@ -245,35 +246,38 @@
     d_hidden_out,
     hidden,
     low_sum,
-    in_sems,
+    slot_of,
+    in_sem,
     weight_sems,
     small_sems,
     wide_sems,
-    back_sems,
 ):
     features, batch, width = received.shape
     total_width = features * width
     blocks = total_width // WIDE
     per_block = WIDE // width
 
-    def load(s):
-        cols = pl.ds(pl.multiple_of(fmap[s] * width, width), width)
-        return pltpu.make_async_copy(received.at[s], inter.at[:, cols], in_sems.at[s])
-
     weights = [
         pltpu.make_async_copy(source, target, weight_sems.at[i])
         for i, (source, target) in enumerate(((v_hbm, v), (u_hbm, u), (h_hbm, h)))
     ]
     weights[0].start()
-    loads = [load(s) for s in range(features)]
-    for copy in loads:
-        copy.start()
+    load = pltpu.make_async_copy(received, inter, in_sem)
+    load.start()
     weights[1].start()
     weights[2].start()
 
-    def store(row, source, target, f):
-        cols = pl.ds(pl.multiple_of(f * width, width), width)
-        return pltpu.make_async_copy(source.at[:, cols], target.at[f], wide_sems.at[row, f])
+    def store(row, source, target, b):
+        part = pl.ds(b * per_block, per_block)
+        return pltpu.make_async_copy(source.at[part], target.at[part], wide_sems.at[row, b])
+
+    def of_block(b):
+        slots = [slot_of[b * per_block + i] for i in range(per_block)]
+        return jnp.concatenate([inter[slot] for slot in slots], axis=1).astype(F32)
+
+    def put(target, b, value):
+        for i in range(per_block):
+            target[b * per_block + i] = value[:, i * width : (i + 1) * width]
 
     small = [
         pltpu.make_async_copy(source, target, small_sems.at[i])
@@ -281,17 +285,18 @@
             ((low_out, low_hbm), (low_grad_out, low_grad_hbm), (d_hidden_out, d_hidden_hbm))
         )
     ]
+    for s in range(features):
+        slot_of[fmap[s]] = s
     low_sum[...] = jnp.zeros_like(low_sum)
     hidden[...] = jnp.broadcast_to(hidden_bias[...], hidden.shape)
     hidden_bias_grad[...] = jnp.zeros_like(hidden_bias_grad)
     out_weight_grad[...] = jnp.zeros_like(out_weight_grad)
+    load.wait()
     weights[0].wait()
     for b in range(blocks):
-        places = []
-        for s in range(b * per_block, (b + 1) * per_block):
-            loads[s].wait()
-            places.append(pl.ds(pl.multiple_of(fmap[s] * width, width), width))
-        left = jnp.concatenate([inter[:, place] for place in places], axis=1)
+        slots = range(b * per_block, (b + 1) * per_block)
+        places = [pl.ds(pl.multiple_of(fmap[s] * width, width), width) for s in slots]
+        left = jnp.concatenate([inter[s] for s in slots], axis=1)
         right = jnp.concatenate([v[place, :] for place in places], axis=0)
         low_sum[...] += jnp.dot(left, right, preferred_element_type=F32)
 
@@ -307,12 +312,11 @@
             jnp.dot(low_out[...], u[:, cols], preferred_element_type=F32) + cross_bias[:, cols]
         )
         held[:, cols] = projected
-        x = inter[:, cols].astype(F32)
+        x = of_block(b)
         product = (x * projected + x).astype(BF)
-        crossed[:, cols] = product
+        put(crossed, b, product)
         hidden[...] += jnp.dot(product, h[cols, :], preferred_element_type=F32)
-        for i in range(per_block):
-            store(0, crossed, crossed_hbm, b * per_block + i).start()
+        store(0, crossed, crossed_hbm, b).start()
 
     chunk = 64
 
@@ -338,31 +342,29 @@
     def _(b):
         cols = pl.ds(pl.multiple_of(b * WIDE, WIDE), WIDE)
         d_crossed = nt(d_hidden_out[...], h[cols, :])
-        d_proj = d_crossed * inter[:, cols].astype(F32)
+        d_proj = d_crossed * of_block(b)
         cross_bias_grad[:, cols] = jnp.sum(d_proj, axis=0, keepdims=True)
         rounded = d_proj.astype(BF)
-        proj_low[:, cols] = rounded
+        put(proj_low, b, rounded)
         low_sum[...] += nt(rounded, u[:, cols])
         held[:, cols] = d_crossed * (held[:, cols] + 1.0)
-        for i in range(per_block):
-            store(1, proj_low, proj_hbm, b * per_block + i).start()
+        store(1, proj_low, proj_hbm, b).start()
 
     low_grad_out[...] = low_sum[...].astype(BF)
     small[1].start()
     stores = list(small)
-    for f in range(features):
-        stores += [store(0, crossed, crossed_hbm, f), store(1, proj_low, proj_hbm, f)]
+    for b in range(blocks):
+        stores += [store(0, crossed, crossed_hbm, b), store(1, proj_low, proj_hbm, b)]
     for b in range(blocks):
         slots = range(b * per_block, (b + 1) * per_block)
         places = [pl.ds(pl.multiple_of(fmap[s] * width, width), width) for s in slots]
         kept = jnp.concatenate([held[:, place] for place in places], axis=1)
         right = jnp.concatenate([v[place, :] for place in places], axis=0)
         result = (kept + nt(low_grad_out[...], right)).astype(BF)
-        for i, s in enumerate(slots):
-            d_inter[s] = result[:, i * width : (i + 1) * width]
-            copy = pltpu.make_async_copy(d_inter.at[s], back.at[s], back_sems.at[s])
-            copy.start()
-            stores.append(copy)
+        put(d_inter, b, result)
+        copy = store(2, d_inter, back, b)
+        copy.start()
+        stores.append(copy)
     for copy in stores:
         copy.wait()
 
@@ -392,9 +394,9 @@
             jax.ShapeDtypeStruct((1, units), F32),
         ],
         scratch_shapes=[
-            pltpu.VMEM((batch, total_width), BF),
-            pltpu.VMEM((batch, total_width), BF),
-            pltpu.VMEM((batch, total_width), BF),
+            pltpu.VMEM(received.shape, BF),
+            pltpu.VMEM(received.shape, BF),
+            pltpu.VMEM(received.shape, BF),
             pltpu.VMEM((batch, total_width), F32),
             pltpu.VMEM(received.shape, BF),
             pltpu.VMEM(v.shape, BF),
@@ -405,11 +407,11 @@
             pltpu.VMEM((batch, units), BF),
             pltpu.VMEM((batch, units), F32),
             pltpu.VMEM((batch, rank), F32),
-            pltpu.SemaphoreType.DMA((features,)),
+            pltpu.SMEM((features,), jnp.int32),
+            pltpu.SemaphoreType.DMA,
             pltpu.SemaphoreType.DMA((3,)),
             pltpu.SemaphoreType.DMA((3,)),
-            pltpu.SemaphoreType.DMA((2, features)),
-            pltpu.SemaphoreType.DMA((features,)),
+            pltpu.SemaphoreType.DMA((3, total_width // WIDE)),
         ],
         compiler_params=pltpu.CompilerParams(vmem_limit_bytes=DENSE_VMEM),
     )(fmap, received, labels, v, u, cross_bias, h, hidden_bias, out_weight)
@@ -434,13 +436,12 @@
     outs = rest[: 2 * parts]
     inter_in, crossed_in, proj_in, low, low_grad, d_hidden = rest[2 * parts : 2 * parts + 6]
     low_t, low_grad_t, d_hidden_t, small, keep, send = rest[2 * parts + 6 : -5]
-    slot_of, small_sems, inter_sems, wide_sems, out_sems = rest[-5:]
+    slot_of, small_sems, inter_sem, wide_sems, out_sems = rest[-5:]
     features = fmap.shape[0]
     width = keep.shape[-1]
     rank = low_t.shape[0]
     each = features // chunks
-    pair = 2
-    share = each // pair
+    share = each // PAIR
 
     smalls = [
         pltpu.make_async_copy(source, target, small_sems.at[i])
@@ -460,14 +461,9 @@
             pltpu.make_async_copy(crossed.at[pl.ds(base, each)], crossed_in.at[span], wide_sems.at[0, part]),
             pltpu.make_async_copy(proj.at[pl.ds(base, each)], proj_in.at[span], wide_sems.at[1, part]),
         ]
-        for i in range(each):
-            n = part * each + i
-            copies.append(
-                pltpu.make_async_copy(
-                    received.at[slot_of[base + i]], inter_in.at[n], inter_sems.at[n]
-                )
-            )
         loads.append(copies)
+    whole = pltpu.make_async_copy(received, inter_in, inter_sem)
+    whole.start()
     for copy in loads[0]:
         copy.start()
     for copy in smalls:
@@ -493,10 +489,19 @@
             preferred_element_type=F32,
             precision=lax.Precision.HIGHEST,
         )
+
+    def stores(part, k):
+        span, place_out = pl.ds(part * each + k * PAIR, PAIR), pl.ds(k * PAIR, PAIR)
+        return [
+            pltpu.make_async_copy(source.at[span], outs[i].at[place_out], out_sems.at[i, k])
+            for i, source in ((parts + part, send), (part, keep))
+        ]
+
     line = lax.broadcasted_iota(jnp.int32, (EXTRA, width), 0)
     nothing = jnp.zeros((EXTRA, width), BF)
     first = place[0] == 0
 
+    whole.wait()
     for part, offset in enumerate(order):
         for copy in loads[part]:
             copy.wait()
@@ -506,19 +511,19 @@
 
         @pl.loop(0, share)
         def _(k, part=part, offset=offset):
-            base = lax.rem(place[1] + offset, chunks) * each + k * pair
-            n = part * each + k * pair
-
-            def product(left, right):
-                both = jnp.concatenate([right[n + i] for i in range(pair)], axis=1)
+            base = lax.rem(place[1] + offset, chunks) * each + k * PAIR
+            n = part * each + k * PAIR
+
+            def product(left, *right):
+                both = jnp.concatenate(right, axis=1)
                 return jnp.dot(left[...], both, preferred_element_type=F32).astype(BF)
 
-            of_v = product(low_grad_t, inter_in)
-            of_u = product(low_t, proj_in)
-            of_h = product(d_hidden_t, crossed_in)
+            of_v = product(low_grad_t, *[inter_in[slot_of[base + i]] for i in range(PAIR)])
+            of_u = product(low_t, *[proj_in[n + i] for i in range(PAIR)])
+            of_h = product(d_hidden_t, *[crossed_in[n + i] for i in range(PAIR)])
 
             def fill(one, other):
-                for i in range(pair):
+                for i in range(PAIR):
                     lanes = slice(i * width, (i + 1) * width)
                     f = base + i
                     cross = cross_bias_grad[:, pl.ds(pl.multiple_of(f * width, width), width)]
@@ -542,14 +547,13 @@
             def _():
                 fill(send, keep)
 
-        span = pl.ds(part * each, each)
-        pltpu.make_async_copy(send.at[span], outs[parts + part], out_sems.at[parts + part]).start()
-        pltpu.make_async_copy(keep.at[span], outs[part], out_sems.at[part]).start()
+            for copy in stores(part, k):
+                copy.start()
 
     for part in range(parts):
-        span = pl.ds(part * each, each)
-        pltpu.make_async_copy(send.at[span], outs[parts + part], out_sems.at[parts + part]).wait()
-        pltpu.make_async_copy(keep.at[span], outs[part], out_sems.at[part]).wait()
+        for k in range(share):
+            for copy in stores(part, k):
+                copy.wait()
 
 
 def gradients(order, place, fmap, received, crossed, proj, low, low_grad, d_hidden, *small):
@@ -567,7 +571,8 @@
         in_specs=[smem, smem] + [hbm] * 6 + [vmem] * 3,
         out_specs=[hbm] * (2 * parts),
         out_shape=[part] * (2 * parts),
-        scratch_shapes=[pltpu.VMEM((held, batch, width), BF)] * 3
+        scratch_shapes=[pltpu.VMEM((features, batch, width), BF)]
+        + [pltpu.VMEM((held, batch, width), BF)] * 2
         + [
             pltpu.VMEM((batch, rank), BF),
             pltpu.VMEM((batch, rank), BF),
@@ -580,9 +585,9 @@
             pltpu.VMEM((held, 2, rank + EXTRA, width), BF),
             pltpu.SMEM((features,), jnp.int32),
             pltpu.SemaphoreType.DMA((3,)),
-            pltpu.SemaphoreType.DMA((held,)),
+            pltpu.SemaphoreType.DMA,
             pltpu.SemaphoreType.DMA((2, parts)),
-            pltpu.SemaphoreType.DMA((2 * parts,)),
+            pltpu.SemaphoreType.DMA((2 * parts, features // len(ORDER) // PAIR)),
         ],
         compiler_params=pltpu.CompilerParams(vmem_limit_bytes=GRADIENTS_VMEM),
         cost_estimate=pl.CostEstimate(
@@ -592,6 +597,69 @@
         ),
     )(place, fmap, received, crossed, proj, low, low_grad, d_hidden, *small)
     return outs[:parts], outs[parts:]
+
+
+def fold_kernel(own, swapped, from_following, from_preceding, out):
+    features, _, lines, width = own.shape
+    quarters = out.shape[0] // features
+    rank = lines - EXTRA
+
+    @pl.loop(0, features)
+    def _(f):
+        total = own[f].astype(F32) + swapped[f].astype(F32)
+        total = total + from_following[f].astype(F32) + from_preceding[f].astype(F32)
+        filler = jnp.zeros((width - EXTRA, width), F32)
+        extra = jnp.concatenate([total[0, rank:], filler], axis=0)
+        across = [total[0, :rank].T, total[1, :rank].T, extra.T]
+        across = jnp.concatenate(across, axis=1).astype(BF)
+        for j in range(quarters):
+            out[f * quarters + j] = across[j * width // quarters : (j + 1) * width // quarters]
+
+
+def fold(quarters, *parts):
+    features, _, lines, width = parts[0].shape
+    vmem = pl.BlockSpec(memory_space=pltpu.VMEM)
+    shape = (features * quarters, width // quarters, 2 * (lines - EXTRA) + width)
+    return pl.pallas_call(
+        fold_kernel,
+        name="fold",
+        in_specs=[vmem] * 4,
+        out_specs=vmem,
+        out_shape=jax.ShapeDtypeStruct(shape, BF),
+        compiler_params=pltpu.CompilerParams(vmem_limit_bytes=VMEM),
+    )(*parts)
+
+
+def finish_kernel(pieces, grad_v, grad_u, grad_h, cross_bias, hidden_bias, out_weight):
+    sources = pieces.shape[0]
+    rank = grad_v.shape[1]
+    sums = []
+    for core in range(2):
+        total = pieces[core].astype(F32)
+        for source in range(core + 2, sources, 2):
+            total = total + pieces[source].astype(F32)
+        sums.append(total)
+    grad_v[...] = sums[0][:, :rank]
+    grad_u[...] = sums[0][:, rank : 2 * rank]
+    grad_h[...] = sums[1][:, : 2 * rank]
+    small = sums[0][:, 2 * rank :].T
+    cross_bias[...] = small[0:1]
+    hidden_bias[...] = small[1:2, : hidden_bias.shape[1]]
+    out_weight[...] = small[2:3, : out_weight.shape[1]]
+
+
+def finish(pieces, rank, units, per):
+    share = pieces.shape[1]
+    vmem = pl.BlockSpec(memory_space=pltpu.VMEM)
+    shapes = ((share, rank), (share, rank), (share, units), (1, share), (1, per), (1, per))
+    return pl.pallas_call(
+        finish_kernel,
+        name="finish",
+        in_specs=[vmem],
+        out_specs=[vmem] * 6,
+        out_shape=[jax.ShapeDtypeStruct(shape, F32) for shape in shapes],
+        compiler_params=pltpu.CompilerParams(vmem_limit_bytes=VMEM),
+    )(pieces)
 
 
 def neighbours(axis):
@@ -692,36 +760,30 @@
         hidden_g,
         out_g,
     )
+    others = [lax.ppermute(sent, "core", [(0, 1), (1, 0)]) for sent in send]
     halves = []
-    for mine, sent in zip(keep, send):
-        other = lax.ppermute(sent, "core", [(0, 1), (1, 0)])
+    for mine, other in zip(keep[:3], others):
         cuts = (slice(0, each // 2), slice(each // 2, each))
         halves.append([add(mine[cut], other[cut]) for cut in cuts])
-
     local = scatter(touched, incidence, returned.reshape(samples, width), rows, roles)
     parts = lax.all_to_all(local, "role", split_axis=0, concat_axis=0, tiled=True)
-    others, parts = lax.optimization_barrier((ring_parts("role", *halves[:3]), parts))
-    role_sum = add(jnp.concatenate(halves[3], axis=0), *others)
-    pieces = lax.all_to_all(
-        role_sum.reshape(each * 2, rank + EXTRA, width),
-        ("x", "zh", "zl"),
-        split_axis=0,
-        concat_axis=0,
-        tiled=True,
-    )
-    piece = jnp.sum(pieces.astype(F32), axis=0)
-    shares = lax.all_to_all(piece.T, ("zl", "core"), split_axis=0, concat_axis=0, tiled=True)
-    shares = shares.reshape(quarters, share, rank + EXTRA)
-    grad_v = shares[0, :, :rank]
-    grad_u = shares[2, :, :rank].T
-    grad_h = jnp.concatenate([shares[1, :, :rank], shares[3, :, :rank]], axis=1)
-    grad_cb = shares[0, :, rank]
-    grad_hb = shares[0, :per, rank + 1]
-    grad_ow = shares[0, :per, rank + 2]
-
+    quarters = 4
+    folded = fold(quarters, keep[3], others[3], *ring_parts("role", *halves))
+    folded, parts = lax.optimization_barrier((folded, parts))
+    pieces = lax.all_to_all(folded, dp, split_axis=0, concat_axis=0, tiled=True)
+    per = units // (features * quarters)
+    grad_v, grad_u, grad_h, grad_cb, grad_hb, grad_ow = finish(pieces, rank, units, per)
     part = add(*parts)
     table_grad = spread_rows(role.reshape(1), ring_spread("role", part), roles)
-    return (table_grad, grad_v, grad_u, grad_cb, grad_h, grad_hb, grad_ow)
+    return (
+        table_grad,
+        grad_v,
+        grad_u.T,
+        grad_cb.reshape(-1),
+        grad_h,
+        grad_hb.reshape(-1),
+        grad_ow.reshape(-1),
+    )
 
 
 def solution(mesh):

time: 204 us -> 193 us (0.946)
  other arithmetic: 10.6 us -> 5.24 us
  starting transfers between devices: 46.3 us -> 41.5 us
  Pallas kernels: 53.6 us -> 56.1 us
    pallas_call x0 -> x2, Pallas kernels: none -> 6.56 us  [the longest x1 4.46 us: fold(): pl.pallas_call(fold_kernel, name='fold', in_specs=[vmem] * 4, out_specs=v...]
    ppermute x4, waiting for transfers between devices: 8.36 us -> 13.4 us  [neighbours(): lax.ppermute(value, axis, up)]
    convert_element_type x5 -> x3, other arithmetic: 6.86 us -> 2.34 us  [add(): return total.astype(BF)]
    all_to_all x1, waiting for transfers between devices: 10.5 us -> 6.04 us  [body(): lax.all_to_all(local, 'role', split_axis=0, concat_axis=0, tiled=True)]
    all_to_all x2 -> x1, waiting for transfers between devices: 5.59 us -> 1.3 us  [body(): pieces = lax.all_to_all(folded, dp, split_axis=0, concat_axis=0, tiled=True)]
    all_to_all x2 -> x1, starting transfers between devices: 14.1 us -> 9.78 us  [body(): pieces = lax.all_to_all(folded, dp, split_axis=0, concat_axis=0, tiled=True)]
  transfers between devices with their start and end apart: 17 -> 16, of which waited for: 10 -> 10; matrix products, arithmetic and copies ran while one was open for 4% -> 3% of each run, Pallas kernels for 11% -> 13%
where the time goes in v4:
time: 193 us; the launch traced here: 192 us
  waiting for transfers between devices  81.3 us (42%)
  Pallas kernels  56.1 us (29%)
  starting transfers between devices  41.5 us (22%)
  local copies, waits for them, and re-layouts  7.17 us (4%)
  other arithmetic  5.24 us (3%)
    all_to_all x1, waiting for transfers between devices, body(): lax.all_to_all(pooled.reshape(features, batch, width), dp, split_axis=0,...  37.8 us
    ppermute x4, waiting for transfers between devices, neighbours(): lax.ppermute(value, axis, down)  18.1 us
    pallas_call x1, Pallas kernels, dense(): pl.pallas_call(functools.partial(dense_kernel, scale), name='dense', in_s...  17.2 us
    ppermute x4, waiting for transfers between devices, neighbours(): lax.ppermute(value, axis, up)  13.4 us
    pallas_call x1, Pallas kernels, gradients(): pl.pallas_call(functools.partial(gradients_kernel, order), name='gradient...  11.7 us
    pallas_call x1, Pallas kernels, pool(): pl.pallas_call(pool_kernel, name='pool', in_specs=[pl.BlockSpec(memory_sp...  11.6 us
    ppermute x4, starting transfers between devices, neighbours(): lax.ppermute(value, axis, down)  11.6 us
    all_to_all x1, starting transfers between devices, body(): pieces = lax.all_to_all(folded, dp, split_axis=0, concat_axis=0, tiled=True)  9.78 us
  transfers between devices with their start and end apart: 16, of which 10 were waited for; matrix products, arithmetic and copies ran while one was open for 3% of the time, Pallas kernels for 13%

profile of v4, /device:TPU:1, one launch (start us, length us, event | category | flops | bytes accessed | tf_op | source)
XLA Modules:
  0.0 192.1 jit_solution(1086541169897046142)
XLA Ops:
  0.6 11.6 %pool.1 = (bf16[12288,128]{1,0:T(8,128)(2,1)}, bf16[96,128,128]{2,1,0:T(8,128)(2,1)}) custom-call(s32[16,96]{1,0:T(8,128)} %bitcast.26, bf16[4096,128]{1,0:T(8,128)(2,1)} %table.1, s32[16,12288]{1,0:T(8,128)} %bitcast.23, s32[16,12288]{1,0:T(8,128)} %bitcast.24), custom_call_target="tpu_custom_call" | custom-call | tf_op jit(solution)/shard_map/pool/pallas_call | solution.py:97
  12.2 0.0 copy-start.11
  12.3 0.0 copy-start.10
  12.3 9.4 %all-to-all-start = ((bf16[32,384,128]{2,1,0:T(8,128)(2,1)}), bf16[32,384,128]{2,1,0:T(8,128)(2,1)S(1)}, u32[]{:S(2)}, u32[]{:S(2)}) async-start(bf16[32,384,128]{2,1,0:T(8,128)(2,1)} %bitcast.22), calls=%async_computation | async-start | bytes 6291456 | tf_op jit(solution)/shard_map/all_to_all | solution.py:726
  21.7 0.6 reshape.57.out_weight
  22.3 0.8 reshape.62.labels
  23.1 0.6 pad_add_fusion.place
  23.7 37.8 %all-to-all-done.received = bf16[32,384,128]{2,1,0:T(8,128)(2,1)S(1)} async-done(((bf16[32,384,128]{2,1,0:T(8,128)(2,1)}), bf16[32,384,128]{2,1,0:T(8,128)(2,1)S(1)}, u32[]{:S(2)}, u32[]{:S(2)}) %all-to-all-start) | async-done | bytes 3145760 | tf_op jit(solution)/shard_map/all_to_all | solution.py:726
  61.5 1.7 copy-done
  63.2 17.2 %dense.1 = (bf16[32,384,128]{2,1,0:T(8,128)(2,1)}, bf16[32,384,128]{2,1,0:T(8,128)(2,1)}, bf16[32,384,128]{2,1,0:T(8,128)(2,1)}, bf16[384,256]{1,0:T(8,128)(2,1)...) custom-call(s32[32]{0:T(128)} %fmap.3, ...), custom_call_target="tpu_custom_call" | custom-call | tf_op jit(solution)/shard_map/dense/pallas_call | solution.py:380
  80.4 5.0 %all-to-all-start.1 = ((bf16[32,384,128]{2,1,0:T(8,128)(2,1)}), bf16[32,384,128]{2,1,0:T(8,128)(2,1)S(1)}, u32[]{:S(2)}, u32[]{:S(2)}) async-start(bf16[32,384,128]{2,1,0:T(8,128)(2,1)} %get-tuple-element.52), calls=%async_computation.1 | async-start | bytes 6291456 | tf_op jit(solution)/shard_map/all_to_all | solution.py:741
  85.4 11.7 %gradients.1 = (bf16[8,2,272,128]{3,2,1,0:T(8,128)(2,1)}, bf16[8,2,272,128]{3,2,1,0:T(8,128)(2,1)}, bf16[8,2,272,128]{3,2,1,0:T(8,128)(2,1)}, bf16[8,2,272,128]{...) custom-call(s32[2]{0:T(128)} %pad_add_fusion.place, ...), custom_call_target="tpu_custom_call" | custom-call | flops 3221225472 | bytes 16777216 | tf_op jit(solution)/shard_map/gradients/pallas_call | solution.py:568
  97.0 0.3 collective-permute-start.2
  97.3 0.3 collective-permute-start.1
  97.6 0.2 collective-permute-start.5
  97.9 2.2 %collective-permute-done.2 = bf16[8,2,272,128]{3,2,1,0:T(8,128)(2,1)S(1)} collective-permute-done((bf16[8,2,272,128]{3,2,1,0:T(8,128)(2,1)}, bf16[8,2,272,128]{3,2,1,0:T(8,128)(2,1)S(1)}, u32[]{:S(2)}, u32[]{:S(2)}) %collective-permute-start.2) | collective-permute-done | bytes 1114144 | tf_op jit(solution)/shard_map/ppermute | solution.py:763
  100.1 1.6 add_convert_fusion.1
  101.7 2.8 %collective-permute-start.3 = (bf16[4,2,272,128]{3,2,1,0:T(8,128)(2,1)S(1)}, bf16[4,2,272,128]{3,2,1,0:T(8,128)(2,1)S(1)}, u32[]{:S(2)}, u32[]{:S(2)}) collective-permute-start(bf16[4,2,272,128]{3,2,1,0:T(8,128)(2,1)S(1)} %get-tuple-element.64), channel_id=1, source_target_pairs={{0,96},{32,0},{64,32},{96,64},{1,97},{33,1},{65,33},{97,65},{2,98}... | collective-permute-start | bytes 1671176 | tf_op jit(solution)/shard_map/ppermute | solution.py:671
  104.5 0.0 collective-permute-start.6
  104.5 0.5 collective-permute-start
  105.0 11.3 %collective-permute-done.3 = bf16[4,2,272,128]{3,2,1,0:T(8,128)(2,1)S(1)} collective-permute-done((bf16[4,2,272,128]{3,2,1,0:T(8,128)(2,1)S(1)}, bf16[4,2,272,128]{3,2,1,0:T(8,128)(2,1)S(1)}, u32[]{:S(2)}, u32[]{:S(2)}) %collective-permute-start.3) | collective-permute-done | bytes 557088 | tf_op jit(solution)/shard_map/ppermute | solution.py:671
  116.3 0.4 add_convert_fusion.5
  116.7 1.1 pad_maximum_fusion
  117.7 3.4 %collective-permute-start.4 = (bf16[8,2,272,128]{3,2,1,0:T(8,128)(2,1)}, bf16[8,2,272,128]{3,2,1,0:T(8,128)(2,1)}, u32[]{:S(2)}, u32[]{:S(2)}) collective-permute-start(bf16[8,2,272,128]{3,2,1,0:T(8,128)(2,1)} %pad_maximum_fusion), channel_id=1, source_target_pairs={{0,96},{32,0},{64,32},{96,64},{1,97},{33,1},{65,33},{97,65},{2,98}... | collective-permute-start | bytes 3342344 | tf_op jit(solution)/shard_map/ppermute | solution.py:671
  121.2 0.4 add_convert_fusion.3
  121.5 1.1 pad_maximum_fusion.1
  122.6 2.5 %all-to-all-done.1 = bf16[32,384,128]{2,1,0:T(8,128)(2,1)S(1)} async-done(((bf16[32,384,128]{2,1,0:T(8,128)(2,1)}), bf16[32,384,128]{2,1,0:T(8,128)(2,1)S(1)}, u32[]{:S(2)}, u32[]{:S(2)}) %all-to-all-start.1) | async-done | bytes 3145760 | tf_op jit(solution)/shard_map/all_to_all | solution.py:741
  125.1 1.7 copy-done.2
  126.8 6.4 %scatter.1 = bf16[4,1024,128]{2,1,0:T(8,128)(2,1)} custom-call(s32[16,96]{1,0:T(8,128)} %bitcast.27, bf16[96,128,128]{2,1,0:T(8,128)(2,1)} %get-tuple-element.51.incidence, bf16[12288,128]{1,0:T(8,128)(2,1)} %bitcast.21), custom_call_target="tpu_custom_call" | custom-call | flops 8589934592 | bytes 8388608 | tf_op jit(solution)/shard_map/scatter/pallas_call | solution.py:170
  133.3 4.2 %all-to-all-start.2 = ((bf16[4,1024,128]{2,1,0:T(8,128)(2,1)}), bf16[4,1024,128]{2,1,0:T(8,128)(2,1)S(1)}, u32[]{:S(2)}, u32[]{:S(2)}) async-start(bf16[4,1024,128]{2,1,0:T(8,128)(2,1)} %scatter.1), calls=%async_computation.2 | async-start | bytes 2097152 | tf_op jit(solution)/shard_map/all_to_all | solution.py:769
  137.5 6.8 %collective-permute-done.4.from_following = bf16[8,2,272,128]{3,2,1,0:T(8,128)(2,1)} collective-permute-done((bf16[8,2,272,128]{3,2,1,0:T(8,128)(2,1)}, bf16[8,2,272,128]{3,2,1,0:T(8,128)(2,1)}, u32[]{:S(2)}, u32[]{:S(2)}) %collective-permute-start.4) | collective-permute-done | bytes 1114144 | tf_op jit(solution)/shard_map/ppermute | solution.py:671
  144.3 4.6 %collective-permute-done.7.from_preceding = bf16[8,2,272,128]{3,2,1,0:T(8,128)(2,1)} collective-permute-done((bf16[8,2,272,128]{3,2,1,0:T(8,128)(2,1)}, bf16[8,2,272,128]{3,2,1,0:T(8,128)(2,1)}, u32[]{:S(2)}, u32[]{:S(2)}) %collective-permute-start.7) | collective-permute-done | bytes 1114144 | tf_op jit(solution)/shard_map/ppermute | solution.py:670
  148.9 4.5 %fold.1 = bf16[32,32,640]{2,1,0:T(8,128)(2,1)} custom-call(bf16[8,2,272,128]{3,2,1,0:T(8,128)(2,1)} %get-tuple-element.43.own, bf16[8,2,272,128]{3,2,1,0:T(8,128)(2,1)} %collective-permute-done.swapped, bf16[8,2,272,128]{3,2,1,0:T(8,128)(2,1)} %collective-permute-done.4.from_following, bf16[8,2,272,128]{3,2,1,0:T(8,128)(2,1)} %collective-permute-done.7.from_preceding), custom_call_target="tpu_custom_call" | custom-call | tf_op jit(solution)/shard_map/fold/pallas_call | solution.py:623
  153.3 6.0 %all-to-all-done.2 = bf16[4,1024,128]{2,1,0:T(8,128)(2,1)S(1)} async-done(((bf16[4,1024,128]{2,1,0:T(8,128)(2,1)}), bf16[4,1024,128]{2,1,0:T(8,128)(2,1)S(1)}, u32[]{:S(2)}, u32[]{:S(2)}) %all-to-all-start.2) | async-done | bytes 1048608 | tf_op jit(solution)/shard_map/all_to_all | solution.py:769
  159.4 9.8 %all-to-all-start.3 = ((bf16[32,32,640]{2,1,0:T(8,128)(2,1)}), bf16[32,32,640]{2,1,0:T(8,128)(2,1)S(1)}, u32[]{:S(2)}, u32[]{:S(2)}) async-start(bf16[32,32,640]{2,1,0:T(8,128)(2,1)} %fold.1), calls=%async_computation.3 | async-start | bytes 2621440 | tf_op jit(solution)/shard_map/all_to_all | solution.py:773
  169.2 0.1 fusion.own
  169.3 0.1 collective-permute-start.10
  169.4 2.7 %collective-permute-start.8 = (bf16[1024,128]{1,0:T(8,128)(2,1)S(1)}, bf16[1024,128]{1,0:T(8,128)(2,1)S(1)}, u32[]{:S(2)}, u32[]{:S(2)}) collective-permute-start(bf16[1024,128]{1,0:T(8,128)(2,1)S(1)} %fusion.own), channel_id=1, source_target_pairs={{0,96},{32,0},{64,32},{96,64},{1,97},{33,1},{65,33},{97,65},{2,98}... | collective-permute-start | bytes 786440 | tf_op jit(solution)/shard_map/ppermute | solution.py:671
  172.1 6.2 %collective-permute-done.10.preceding = bf16[1024,128]{1,0:T(8,128)(2,1)S(1)} collective-permute-done((bf16[1024,128]{1,0:T(8,128)(2,1)S(1)}, bf16[1024,128]{1,0:T(8,128)(2,1)S(1)}, u32[]{:S(2)}, u32[]{:S(2)}) %collective-permute-start.10) | collective-permute-done | bytes 262176 | tf_op jit(solution)/shard_map/ppermute | solution.py:670
  178.3 0.1 collective-permute-start.11
  178.4 2.7 %collective-permute-start.9 = (bf16[512,128]{1,0:T(8,128)(2,1)S(1)}, bf16[512,128]{1,0:T(8,128)(2,1)S(1)}, u32[]{:S(2)}, u32[]{:S(2)}) collective-permute-start(bf16[512,128]{1,0:T(8,128)(2,1)S(1)} %slice.62), channel_id=1, source_target_pairs={{0,96},{32,0},{64,32},{96,64},{1,97},{33,1},{65,33},{97,65},{2,98}... | collective-permute-start | bytes 393224 | tf_op jit(solution)/shard_map/ppermute | solution.py:671
  181.1 2.6 %collective-permute-done.11.opposite_b = bf16[512,128]{1,0:T(8,128)(2,1)S(1)} collective-permute-done((bf16[512,128]{1,0:T(8,128)(2,1)S(1)}, bf16[512,128]{1,0:T(8,128)(2,1)S(1)}, u32[]{:S(2)}, u32[]{:S(2)}) %collective-permute-start.11) | collective-permute-done | bytes 131104 | tf_op jit(solution)/shard_map/ppermute | solution.py:670
  183.7 0.6 copy-done.8
  184.3 0.7 copy-done.9
  185.0 2.7 %spread_rows.1 = f32[4096,128]{1,0:T(8,128)} custom-call(s32[1]{0:T(128)} %bitcast.role, bf16[1024,128]{1,0:T(8,128)(2,1)} %copy-done.5, bf16[1024,128]{1,0:T(8,128)(2,1)} %copy-done.7, bf16[512,128]{1,0:T(8,128)(2,1)} %copy-done.9, bf16[512,128]{1,0:T(8,128)(2,1)} %copy-done.8, bf16[1024,128]{1,0:T(8,128)(2,1)} %copy-done.6), custom_call_target="tpu_custom_call" | custom-call | tf_op jit(solution)/shard_map/spread_rows/pallas_call | solution.py:206
  187.7 1.3 all-to-all-done.3.pieces
  189.0 1.1 copy-done.1
  190.0 2.1 %finish.1 = (f32[32,256]{1,0:T(8,128)}, f32[32,256]{1,0:T(8,128)}, f32[32,512]{1,0:T(8,128)}, f32[1,32]{1,0:T(1,128)}, f32[1,4]{1,0:T(1,128)}, /*index=5*/f32[1,4]{1,0:T(1,128)}) custom-call(bf16[32,32,640]{2,1,0:T(8,128)(2,1)} %copy-done.1), custom_call_target="tpu_custom_call" | custom-call | tf_op jit(solution)/shard_map/finish/pallas_call | solution.py:655
  (26 shorter events, 0.1 us)
Async XLA Ops:
  12.2 9.5 %copy-start.11 = (bf16[512]{0:T(512)(128)(2,1)S(1)}, bf16[512]{0:T(512)(128)(2,1)}, u32[]{:S(2)}) copy-start(bf16[512]{0:T(512)(128)(2,1)} %param.23) | copy-start | bytes 3076
  12.3 10.1 %copy-start.10 = (s32[384]{0:T(512)S(1)}, s32[384]{0:T(512)}, u32[]{:S(2)}) copy-start(s32[384]{0:T(512)} %param.17) | copy-start | bytes 4612
  12.3 49.2 %all-to-all-start = ((bf16[32,384,128]{2,1,0:T(8,128)(2,1)}), bf16[32,384,128]{2,1,0:T(8,128)(2,1)S(1)}, u32[]{:S(2)}, u32[]{:S(2)}) async-start(bf16[32,384,128]{2,1,0:T(8,128)(2,1)} %bitcast.22), calls=%async_computation | async-start | bytes 6291456 | tf_op jit(solution)/shard_map/all_to_all | solution.py:726
  61.5 1.7 copy-start
  80.4 44.8 %all-to-all-start.1 = ((bf16[32,384,128]{2,1,0:T(8,128)(2,1)}), bf16[32,384,128]{2,1,0:T(8,128)(2,1)S(1)}, u32[]{:S(2)}, u32[]{:S(2)}) async-start(bf16[32,384,128]{2,1,0:T(8,128)(2,1)} %get-tuple-element.52), calls=%async_computation.1 | async-start | bytes 6291456 | tf_op jit(solution)/shard_map/all_to_all | solution.py:741
  97.0 3.0 %collective-permute-start.2 = (bf16[8,2,272,128]{3,2,1,0:T(8,128)(2,1)}, bf16[8,2,272,128]{3,2,1,0:T(8,128)(2,1)S(1)}, u32[]{:S(2)}, u32[]{:S(2)}) collective-permute-start(bf16[8,2,272,128]{3,2,1,0:T(8,128)(2,1)} %get-tuple-element.48), channel_id=1, source_target_pairs={{0,1},{1,0},{2,3},{3,2},{4,5},{5,4},{6,7},{7,6},{8,9},{9,8},{10,11... | collective-permute-start | bytes 3342344 | tf_op jit(solution)/shard_map/ppermute | solution.py:763
  97.3 7.7 %collective-permute-start.1 = (bf16[8,2,272,128]{3,2,1,0:T(8,128)(2,1)}, bf16[8,2,272,128]{3,2,1,0:T(8,128)(2,1)S(1)}, u32[]{:S(2)}, u32[]{:S(2)}) collective-permute-start(bf16[8,2,272,128]{3,2,1,0:T(8,128)(2,1)} %get-tuple-element.46), channel_id=1, source_target_pairs={{0,1},{1,0},{2,3},{3,2},{4,5},{5,4},{6,7},{7,6},{8,9},{9,8},{10,11... | collective-permute-start | bytes 3342344 | tf_op jit(solution)/shard_map/ppermute | solution.py:763
  97.6 23.6 %collective-permute-start.5 = (bf16[8,2,272,128]{3,2,1,0:T(8,128)(2,1)}, bf16[8,2,272,128]{3,2,1,0:T(8,128)(2,1)S(1)}, u32[]{:S(2)}, u32[]{:S(2)}) collective-permute-start(bf16[8,2,272,128]{3,2,1,0:T(8,128)(2,1)} %get-tuple-element.50), channel_id=1, source_target_pairs={{0,1},{1,0},{2,3},{3,2},{4,5},{5,4},{6,7},{7,6},{8,9},{9,8},{10,11... | collective-permute-start | bytes 3342344 | tf_op jit(solution)/shard_map/ppermute | solution.py:763
  100.1 16.2 %copy-start.4 = (bf16[8,2,272,128]{3,2,1,0:T(8,128)(2,1)S(1)}, bf16[8,2,272,128]{3,2,1,0:T(8,128)(2,1)}, u32[]{:S(2)}) copy-start(bf16[8,2,272,128]{3,2,1,0:T(8,128)(2,1)} %get-tuple-element.45) | copy-start | bytes 3342340
  101.7 14.6 %collective-permute-start.3 = (bf16[4,2,272,128]{3,2,1,0:T(8,128)(2,1)S(1)}, bf16[4,2,272,128]{3,2,1,0:T(8,128)(2,1)S(1)}, u32[]{:S(2)}, u32[]{:S(2)}) collective-permute-start(bf16[4,2,272,128]{3,2,1,0:T(8,128)(2,1)S(1)} %get-tuple-element.64), channel_id=1, source_target_pairs={{0,96},{32,0},{64,32},{96,64},{1,97},{33,1},{65,33},{97,65},{2,98}... | collective-permute-start | bytes 1671176 | tf_op jit(solution)/shard_map/ppermute | solution.py:671
  104.5 16.7 %collective-permute-start.6 = (bf16[4,2,272,128]{3,2,1,0:T(8,128)(2,1)S(1)}, bf16[4,2,272,128]{3,2,1,0:T(8,128)(2,1)S(1)}, u32[]{:S(2)}, u32[]{:S(2)}) collective-permute-start(bf16[4,2,272,128]{3,2,1,0:T(8,128)(2,1)S(1)} %get-tuple-element.63), channel_id=1, source_target_pairs={{0,32},{32,64},{64,96},{96,0},{1,33},{33,65},{65,97},{97,1},{2,34}... | collective-permute-start | bytes 1671176 | tf_op jit(solution)/shard_map/ppermute | solution.py:670
  104.5 33.0 %collective-permute-start = (bf16[8,2,272,128]{3,2,1,0:T(8,128)(2,1)}, bf16[8,2,272,128]{3,2,1,0:T(8,128)(2,1)}, u32[]{:S(2)}, u32[]{:S(2)}) collective-permute-start(bf16[8,2,272,128]{3,2,1,0:T(8,128)(2,1)} %get-tuple-element.44), channel_id=1, source_target_pairs={{0,1},{1,0},{2,3},{3,2},{4,5},{5,4},{6,7},{7,6},{8,9},{9,8},{10,11... | collective-permute-start | bytes 3342344 | tf_op jit(solution)/shard_map/ppermute | solution.py:763
  116.6 4.5 %copy-start.3 = (bf16[8,2,272,128]{3,2,1,0:T(8,128)(2,1)S(1)}, bf16[8,2,272,128]{3,2,1,0:T(8,128)(2,1)}, u32[]{:S(2)}) copy-start(bf16[8,2,272,128]{3,2,1,0:T(8,128)(2,1)} %get-tuple-element.49) | copy-start | bytes 3342340
  117.7 26.5 %collective-permute-start.4 = (bf16[8,2,272,128]{3,2,1,0:T(8,128)(2,1)}, bf16[8,2,272,128]{3,2,1,0:T(8,128)(2,1)}, u32[]{:S(2)}, u32[]{:S(2)}) collective-permute-start(bf16[8,2,272,128]{3,2,1,0:T(8,128)(2,1)} %pad_maximum_fusion), channel_id=1, source_target_pairs={{0,96},{32,0},{64,32},{96,64},{1,97},{33,1},{65,33},{97,65},{2,98}... | collective-permute-start | bytes 3342344 | tf_op jit(solution)/shard_map/ppermute | solution.py:671
  122.6 26.3 %collective-permute-start.7 = (bf16[8,2,272,128]{3,2,1,0:T(8,128)(2,1)}, bf16[8,2,272,128]{3,2,1,0:T(8,128)(2,1)}, u32[]{:S(2)}, u32[]{:S(2)}) collective-permute-start(bf16[8,2,272,128]{3,2,1,0:T(8,128)(2,1)} %pad_maximum_fusion.1), channel_id=1, source_target_pairs={{0,32},{32,64},{64,96},{96,0},{1,33},{33,65},{65,97},{97,1},{2,34}... | collective-permute-start | bytes 3342344 | tf_op jit(solution)/shard_map/ppermute | solution.py:670
  125.1 1.7 copy-start.2
  133.3 26.1 %all-to-all-start.2 = ((bf16[4,1024,128]{2,1,0:T(8,128)(2,1)}), bf16[4,1024,128]{2,1,0:T(8,128)(2,1)S(1)}, u32[]{:S(2)}, u32[]{:S(2)}) async-start(bf16[4,1024,128]{2,1,0:T(8,128)(2,1)} %scatter.1), calls=%async_computation.2 | async-start | bytes 2097152 | tf_op jit(solution)/shard_map/all_to_all | solution.py:769
  159.4 29.6 %all-to-all-start.3 = ((bf16[32,32,640]{2,1,0:T(8,128)(2,1)}), bf16[32,32,640]{2,1,0:T(8,128)(2,1)S(1)}, u32[]{:S(2)}, u32[]{:S(2)}) async-start(bf16[32,32,640]{2,1,0:T(8,128)(2,1)} %fold.1), calls=%async_computation.3 | async-start | bytes 2621440 | tf_op jit(solution)/shard_map/all_to_all | solution.py:773
  169.3 14.4 %copy-start.5 = (bf16[1024,128]{1,0:T(8,128)(2,1)}, bf16[1024,128]{1,0:T(8,128)(2,1)S(1)}, u32[]{:S(2)}) copy-start(bf16[1024,128]{1,0:T(8,128)(2,1)S(1)} %fusion.own) | copy-start | bytes 786436
  169.3 9.0 %collective-permute-start.10 = (bf16[1024,128]{1,0:T(8,128)(2,1)S(1)}, bf16[1024,128]{1,0:T(8,128)(2,1)S(1)}, u32[]{:S(2)}, u32[]{:S(2)}) collective-permute-start(bf16[1024,128]{1,0:T(8,128)(2,1)S(1)} %fusion.own), channel_id=1, source_target_pairs={{0,32},{32,64},{64,96},{96,0},{1,33},{33,65},{65,97},{97,1},{2,34}... | collective-permute-start | bytes 786440 | tf_op jit(solution)/shard_map/ppermute | solution.py:670
  169.4 9.0 %collective-permute-start.8 = (bf16[1024,128]{1,0:T(8,128)(2,1)S(1)}, bf16[1024,128]{1,0:T(8,128)(2,1)S(1)}, u32[]{:S(2)}, u32[]{:S(2)}) collective-permute-start(bf16[1024,128]{1,0:T(8,128)(2,1)S(1)} %fusion.own), channel_id=1, source_target_pairs={{0,96},{32,0},{64,32},{96,64},{1,97},{33,1},{65,33},{97,65},{2,98}... | collective-permute-start | bytes 786440 | tf_op jit(solution)/shard_map/ppermute | solution.py:671
  178.3 5.4 %copy-start.6 = (bf16[1024,128]{1,0:T(8,128)(2,1)}, bf16[1024,128]{1,0:T(8,128)(2,1)S(1)}, u32[]{:S(2)}) copy-start(bf16[1024,128]{1,0:T(8,128)(2,1)S(1)} %collective-permute-done.10.preceding) | copy-start | bytes 786436
  178.3 5.4 %collective-permute-start.11 = (bf16[512,128]{1,0:T(8,128)(2,1)S(1)}, bf16[512,128]{1,0:T(8,128)(2,1)S(1)}, u32[]{:S(2)}, u32[]{:S(2)}) collective-permute-start(bf16[512,128]{1,0:T(8,128)(2,1)S(1)} %slice.63), channel_id=1, source_target_pairs={{0,32},{32,64},{64,96},{96,0},{1,33},{33,65},{65,97},{97,1},{2,34}... | collective-permute-start | bytes 393224 | tf_op jit(solution)/shard_map/ppermute | solution.py:670
  178.4 5.3 %copy-start.7 = (bf16[1024,128]{1,0:T(8,128)(2,1)}, bf16[1024,128]{1,0:T(8,128)(2,1)S(1)}, u32[]{:S(2)}) copy-start(bf16[1024,128]{1,0:T(8,128)(2,1)S(1)} %collective-permute-done.8.following) | copy-start | bytes 786436
  178.4 5.3 %collective-permute-start.9 = (bf16[512,128]{1,0:T(8,128)(2,1)S(1)}, bf16[512,128]{1,0:T(8,128)(2,1)S(1)}, u32[]{:S(2)}, u32[]{:S(2)}) collective-permute-start(bf16[512,128]{1,0:T(8,128)(2,1)S(1)} %slice.62), channel_id=1, source_target_pairs={{0,96},{32,0},{64,32},{96,64},{1,97},{33,1},{65,33},{97,65},{2,98}... | collective-permute-start | bytes 393224 | tf_op jit(solution)/shard_map/ppermute | solution.py:671
  183.7 0.6 copy-start.8
  184.3 0.7 copy-start.9
  189.0 1.1 copy-start.1

commit v5 on v4

--- a/solution.py
+++ b/solution.py
@@ -17,9 +17,10 @@
 ORDER = (2, 1, 3, 0)
 VMEM = 60 << 20
 POOL_VMEM = VMEM
-DENSE_VMEM = VMEM
-GRADIENTS_VMEM = VMEM
-SCATTER_VMEM = VMEM
+DENSE_VMEM = 52 << 20
+GRADIENTS_VMEM = 52 << 20
+SMALL_VMEM = 40 << 20
+SCATTER_VMEM = 52 << 20
 
 BF = jnp.bfloat16
 F32 = jnp.float32
@@ -119,33 +120,27 @@
 
 
 def scatter_kernel(touched, incidence, grad, out, *scratch):
-    sums, (tiles_in, grads_in, sems) = scratch[:-3], scratch[-3:]
+    sums, (tiles_in, sems) = scratch[:-2], scratch[-2:]
     tiles, tile, _ = incidence.shape
     chunks, rows, _ = out.shape
     steps = tiles // STEP_TILES
 
-    def loads(step):
+    def load(step):
         part = pl.ds(step * STEP_TILES, STEP_TILES)
-        span = pl.ds(step * STEP_TILES * tile, STEP_TILES * tile)
-        return (
-            pltpu.make_async_copy(incidence.at[part], tiles_in.at[part], sems.at[0, step]),
-            pltpu.make_async_copy(grad.at[span], grads_in.at[span], sems.at[1, step]),
-        )
+        return pltpu.make_async_copy(incidence.at[part], tiles_in.at[part], sems.at[step])
 
     for step in range(steps):
-        for copy in loads(step):
-            copy.start()
+        load(step).start()
     for acc in sums:
         acc[...] = jnp.zeros_like(acc)
 
     @pl.loop(0, steps)
     def _(step):
-        for copy in loads(step):
-            copy.wait()
+        load(step).wait()
         for i in range(STEP_TILES):
             t = step * STEP_TILES + i
             product = jnp.dot(
-                tiles_in[t], grads_in[pl.ds(t * tile, tile), :], preferred_element_type=F32
+                tiles_in[t], grad[pl.ds(t * tile, tile), :], preferred_element_type=F32
             )
             for k in range(touched.shape[0]):
                 acc = sums[k % len(sums)]
@@ -170,14 +165,13 @@
     return pl.pallas_call(
         scatter_kernel,
         name="scatter",
-        in_specs=[smem, hbm, hbm],
+        in_specs=[smem, hbm, vmem],
         out_specs=vmem,
         out_shape=jax.ShapeDtypeStruct((chunks, rows // chunks, width), BF),
         scratch_shapes=[pltpu.VMEM((rows, width), F32)] * 4
         + [
             pltpu.VMEM(incidence.shape, BF),
-            pltpu.VMEM(grad.shape, BF),
-            pltpu.SemaphoreType.DMA((2, steps)),
+            pltpu.SemaphoreType.DMA((steps,)),
         ],
         compiler_params=pltpu.CompilerParams(vmem_limit_bytes=SCATTER_VMEM),
         cost_estimate=pl.CostEstimate(flops=1 << 33, bytes_accessed=8 << 20, transcendentals=0),
@@ -209,7 +203,7 @@
         in_specs=[pl.BlockSpec(memory_space=pltpu.SMEM)] + [vmem] * 5,
         out_specs=vmem,
         out_shape=jax.ShapeDtypeStruct((chunks * rows, width), F32),
-        compiler_params=pltpu.CompilerParams(vmem_limit_bytes=VMEM),
+        compiler_params=pltpu.CompilerParams(vmem_limit_bytes=SMALL_VMEM),
     )(role, *pieces)
 
 
@@ -380,7 +374,7 @@
     return pl.pallas_call(
         functools.partial(dense_kernel, scale),
         name="dense",
-        in_specs=[smem, hbm, vmem, hbm, hbm, vmem, hbm, vmem, vmem],
+        in_specs=[smem, vmem, vmem, hbm, hbm, vmem, hbm, vmem, vmem],
         out_specs=[hbm] * 6 + [vmem] * 3,
         out_shape=[
             jax.ShapeDtypeStruct(received.shape, BF),
@@ -568,7 +562,7 @@
     outs = pl.pallas_call(
         functools.partial(gradients_kernel, order),
         name="gradients",
-        in_specs=[smem, smem] + [hbm] * 6 + [vmem] * 3,
+        in_specs=[smem, smem, vmem] + [hbm] * 5 + [vmem] * 3,
         out_specs=[hbm] * (2 * parts),
         out_shape=[part] * (2 * parts),
         scratch_shapes=[pltpu.VMEM((features, batch, width), BF)]
@@ -626,7 +620,7 @@
         in_specs=[vmem] * 4,
         out_specs=vmem,
         out_shape=jax.ShapeDtypeStruct(shape, BF),
-        compiler_params=pltpu.CompilerParams(vmem_limit_bytes=VMEM),
+        compiler_params=pltpu.CompilerParams(vmem_limit_bytes=SMALL_VMEM),
     )(*parts)
 
 
@@ -658,7 +652,7 @@
         in_specs=[vmem],
         out_specs=[vmem] * 6,
         out_shape=[jax.ShapeDtypeStruct(shape, F32) for shape in shapes],
-        compiler_params=pltpu.CompilerParams(vmem_limit_bytes=VMEM),
+        compiler_params=pltpu.CompilerParams(vmem_limit_bytes=SMALL_VMEM),
     )(pieces)
 
 

time: 193 us -> 188 us (0.974)
  local copies, waits for them, and re-layouts: 7.17 us -> 1.14 us
  waiting for transfers between devices: 81.3 us -> 85.9 us
  Pallas kernels: 56.1 us -> 52.3 us
    unnamed x24 -> x20, local copies, waits for them, and re-layouts: 5.78 us -> 1.01 us
where the time goes in v5:
time: 188 us; the launch traced here: 187 us
  waiting for transfers between devices  85.9 us (46%)
  Pallas kernels  52.3 us (28%)
  starting transfers between devices  42.1 us (22%)
  other arithmetic  4.62 us (2%)
    all_to_all x1, waiting for transfers between devices, body(): lax.all_to_all(pooled.reshape(features, batch, width), dp, split_axis=0,...  39.6 us
    ppermute x4, waiting for transfers between devices, neighbours(): lax.ppermute(value, axis, down)  18 us
    pallas_call x1, Pallas kernels, dense(): pl.pallas_call(functools.partial(dense_kernel, scale), name='dense', in_s...  16.2 us
    ppermute x4, waiting for transfers between devices, neighbours(): lax.ppermute(value, axis, up)  13.4 us
    pallas_call x1, Pallas kernels, gradients(): pl.pallas_call(functools.partial(gradients_kernel, order), name='gradient...  12.5 us
    ppermute x4, starting transfers between devices, neighbours(): lax.ppermute(value, axis, down)  11.7 us
    pallas_call x1, Pallas kernels, pool(): pl.pallas_call(pool_kernel, name='pool', in_specs=[pl.BlockSpec(memory_sp...  11.6 us
    all_to_all x1, starting transfers between devices, body(): pieces = lax.all_to_all(folded, dp, split_axis=0, concat_axis=0, tiled=True)  9.74 us
  transfers between devices with their start and end apart: 16, of which 10 were waited for; matrix products, arithmetic and copies ran while one was open for 3% of the time, Pallas kernels for 13%

profile of v5, /device:TPU:1, one launch (start us, length us, event | category | flops | bytes accessed | tf_op | source)
XLA Modules:
  0.0 187.0 jit_solution(4783269876725974985)
XLA Ops:
  0.6 11.6 %pool.1 = (bf16[12288,128]{1,0:T(8,128)(2,1)}, bf16[96,128,128]{2,1,0:T(8,128)(2,1)}) custom-call(s32[16,96]{1,0:T(8,128)} %bitcast.22, bf16[4096,128]{1,0:T(8,128)(2,1)} %table.1, s32[16,12288]{1,0:T(8,128)} %bitcast.26, s32[16,12288]{1,0:T(8,128)} %bitcast.27), custom_call_target="tpu_custom_call" | custom-call | tf_op jit(solution)/shard_map/pool/pallas_call | solution.py:98
  12.2 0.0 copy-start.9
  12.2 0.0 copy-start.8
  12.2 0.0 copy-start.2
  12.3 0.0 copy-start.4
  12.3 0.0 copy-start.5
  12.3 9.6 %all-to-all-start = ((bf16[32,384,128]{2,1,0:T(8,128)(2,1)}), bf16[32,384,128]{2,1,0:T(8,128)(2,1)}, u32[]{:S(2)}, u32[]{:S(2)}) async-start(bf16[32,384,128]{2,1,0:T(8,128)(2,1)} %bitcast.25), calls=%async_computation | async-start | bytes 6291456 | tf_op jit(solution)/shard_map/all_to_all | solution.py:720
  22.0 0.1 reshape.62.labels
  22.1 0.1 pad_add_fusion.place
  22.2 39.6 %all-to-all-done.received = bf16[32,384,128]{2,1,0:T(8,128)(2,1)} async-done(((bf16[32,384,128]{2,1,0:T(8,128)(2,1)}), bf16[32,384,128]{2,1,0:T(8,128)(2,1)}, u32[]{:S(2)}, u32[]{:S(2)}) %all-to-all-start) | async-done | bytes 3145760 | tf_op jit(solution)/shard_map/all_to_all | solution.py:720
  61.8 16.2 %dense.1 = (bf16[32,384,128]{2,1,0:T(8,128)(2,1)}, bf16[32,384,128]{2,1,0:T(8,128)(2,1)}, bf16[32,384,128]{2,1,0:T(8,128)(2,1)}, bf16[384,256]{1,0:T(8,128)(2,1)...) custom-call(s32[32]{0:T(128)S(1)} %copy-done.5, ...), custom_call_target="tpu_custom_call" | custom-call | tf_op jit(solution)/shard_map/dense/pallas_call | solution.py:374
  77.9 5.0 %all-to-all-start.1 = ((bf16[32,384,128]{2,1,0:T(8,128)(2,1)}), bf16[32,384,128]{2,1,0:T(8,128)(2,1)}, u32[]{:S(2)}, u32[]{:S(2)}) async-start(bf16[32,384,128]{2,1,0:T(8,128)(2,1)} %get-tuple-element.52), calls=%async_computation.1 | async-start | bytes 6291456 | tf_op jit(solution)/shard_map/all_to_all | solution.py:735
  83.0 12.5 %gradients.1 = (bf16[8,2,272,128]{3,2,1,0:T(8,128)(2,1)S(1)}, bf16[8,2,272,128]{3,2,1,0:T(8,128)(2,1)}, bf16[8,2,272,128]{3,2,1,0:T(8,128)(2,1)}, bf16[8,2,272,1...) custom-call(s32[2]{0:T(128)S(1)} %pad_add_fusion.place, ...), custom_call_target="tpu_custom_call" | custom-call | flops 3221225472 | bytes 16777216 | tf_op jit(solution)/shard_map/gradients/pallas_call | solution.py:562
  95.5 0.4 collective-permute-start.2
  95.9 0.2 collective-permute-start.1
  96.1 0.3 collective-permute-start.5
  96.4 2.1 %collective-permute-done.2 = bf16[8,2,272,128]{3,2,1,0:T(8,128)(2,1)S(1)} collective-permute-done((bf16[8,2,272,128]{3,2,1,0:T(8,128)(2,1)}, bf16[8,2,272,128]{3,2,1,0:T(8,128)(2,1)S(1)}, u32[]{:S(2)}, u32[]{:S(2)}) %collective-permute-start.2) | collective-permute-done | bytes 1114144 | tf_op jit(solution)/shard_map/ppermute | solution.py:757
  98.5 0.3 add_convert_fusion.1
  98.9 2.8 %collective-permute-start.3 = (bf16[4,2,272,128]{3,2,1,0:T(8,128)(2,1)S(1)}, bf16[4,2,272,128]{3,2,1,0:T(8,128)(2,1)S(1)}, u32[]{:S(2)}, u32[]{:S(2)}) collective-permute-start(bf16[4,2,272,128]{3,2,1,0:T(8,128)(2,1)S(1)} %get-tuple-element.64), channel_id=1, source_target_pairs={{0,96},{32,0},{64,32},{96,64},{1,97},{33,1},{65,33},{97,65},{2,98}... | collective-permute-start | bytes 1671176 | tf_op jit(solution)/shard_map/ppermute | solution.py:665
  101.6 0.6 collective-permute-start
  102.2 0.0 collective-permute-done.1
  102.2 11.1 %collective-permute-done.3 = bf16[4,2,272,128]{3,2,1,0:T(8,128)(2,1)S(1)} collective-permute-done((bf16[4,2,272,128]{3,2,1,0:T(8,128)(2,1)S(1)}, bf16[4,2,272,128]{3,2,1,0:T(8,128)(2,1)S(1)}, u32[]{:S(2)}, u32[]{:S(2)}) %collective-permute-start.3) | collective-permute-done | bytes 557088 | tf_op jit(solution)/shard_map/ppermute | solution.py:665
  113.3 0.4 add_convert_fusion.5
  113.7 0.0 copy-start.6
  113.7 1.1 pad_maximum_fusion
  114.8 3.5 %collective-permute-start.4 = (bf16[8,2,272,128]{3,2,1,0:T(8,128)(2,1)}, bf16[8,2,272,128]{3,2,1,0:T(8,128)(2,1)S(1)}, u32[]{:S(2)}, u32[]{:S(2)}) collective-permute-start(bf16[8,2,272,128]{3,2,1,0:T(8,128)(2,1)} %pad_maximum_fusion), channel_id=1, source_target_pairs={{0,96},{32,0},{64,32},{96,64},{1,97},{33,1},{65,33},{97,65},{2,98}... | collective-permute-start | bytes 3342344 | tf_op jit(solution)/shard_map/ppermute | solution.py:665
  118.3 0.4 add_convert_fusion.3
  118.7 0.0 copy-start.3
  118.7 1.1 pad_maximum_fusion.1
  119.8 3.0 %all-to-all-done.1 = bf16[32,384,128]{2,1,0:T(8,128)(2,1)} async-done(((bf16[32,384,128]{2,1,0:T(8,128)(2,1)}), bf16[32,384,128]{2,1,0:T(8,128)(2,1)}, u32[]{:S(2)}, u32[]{:S(2)}) %all-to-all-start.1) | async-done | bytes 3145760 | tf_op jit(solution)/shard_map/all_to_all | solution.py:735
  122.8 6.4 %scatter.1 = bf16[4,1024,128]{2,1,0:T(8,128)(2,1)S(1)} custom-call(s32[16,96]{1,0:T(8,128)S(1)} %bitcast.23, bf16[96,128,128]{2,1,0:T(8,128)(2,1)} %get-tuple-element.51.incidence, bf16[12288,128]{1,0:T(8,128)(2,1)} %bitcast.12.grad), custom_call_target="tpu_custom_call" | custom-call | flops 8589934592 | bytes 8388608 | tf_op jit(solution)/shard_map/scatter/pallas_call | solution.py:165
  129.2 1.0 copy-done.1
  130.2 4.4 %all-to-all-start.2 = ((bf16[4,1024,128]{2,1,0:T(8,128)(2,1)}), bf16[4,1024,128]{2,1,0:T(8,128)(2,1)}, u32[]{:S(2)}, u32[]{:S(2)}) async-start(bf16[4,1024,128]{2,1,0:T(8,128)(2,1)} %copy-done.1), calls=%async_computation.2 | async-start | bytes 2097152 | tf_op jit(solution)/shard_map/all_to_all | solution.py:763
  134.6 6.9 %collective-permute-done.4.from_following = bf16[8,2,272,128]{3,2,1,0:T(8,128)(2,1)S(1)} collective-permute-done((bf16[8,2,272,128]{3,2,1,0:T(8,128)(2,1)}, bf16[8,2,272,128]{3,2,1,0:T(8,128)(2,1)S(1)}, u32[]{:S(2)}, u32[]{:S(2)}) %collective-permute-start.4) | collective-permute-done | bytes 1114144 | tf_op jit(solution)/shard_map/ppermute | solution.py:665
  141.5 4.6 %collective-permute-done.7.from_preceding = bf16[8,2,272,128]{3,2,1,0:T(8,128)(2,1)} collective-permute-done((bf16[8,2,272,128]{3,2,1,0:T(8,128)(2,1)}, bf16[8,2,272,128]{3,2,1,0:T(8,128)(2,1)}, u32[]{:S(2)}, u32[]{:S(2)}) %collective-permute-start.7) | collective-permute-done | bytes 1114144 | tf_op jit(solution)/shard_map/ppermute | solution.py:664
  146.1 3.5 %fold.1 = bf16[32,32,640]{2,1,0:T(8,128)(2,1)} custom-call(bf16[8,2,272,128]{3,2,1,0:T(8,128)(2,1)S(1)} %copy-done, bf16[8,2,272,128]{3,2,1,0:T(8,128)(2,1)S(1)} %collective-permute-done.swapped, bf16[8,2,272,128]{3,2,1,0:T(8,128)(2,1)S(1)} %collective-permute-done.4.from_following, bf16[8,2,272,128]{3,2,1,0:T(8,128)(2,1)} %collective-permute-done.7.from_preceding), custom_call_target="tpu_custom_call" | custom-call | tf_op jit(solution)/shard_map/fold/pallas_call | solution.py:617
  149.5 7.1 %all-to-all-done.2 = bf16[4,1024,128]{2,1,0:T(8,128)(2,1)} async-done(((bf16[4,1024,128]{2,1,0:T(8,128)(2,1)}), bf16[4,1024,128]{2,1,0:T(8,128)(2,1)}, u32[]{:S(2)}, u32[]{:S(2)}) %all-to-all-start.2) | async-done | bytes 1048608 | tf_op jit(solution)/shard_map/all_to_all | solution.py:763
  156.7 9.7 %all-to-all-start.3 = ((bf16[32,32,640]{2,1,0:T(8,128)(2,1)}), bf16[32,32,640]{2,1,0:T(8,128)(2,1)S(1)}, u32[]{:S(2)}, u32[]{:S(2)}) async-start(bf16[32,32,640]{2,1,0:T(8,128)(2,1)} %fold.1), calls=%async_computation.3 | async-start | bytes 2621440 | tf_op jit(solution)/shard_map/all_to_all | solution.py:767
  166.4 1.3 fusion.own
  167.8 0.1 collective-permute-start.10
  167.8 2.7 %collective-permute-start.8 = (bf16[1024,128]{1,0:T(8,128)(2,1)S(1)}, bf16[1024,128]{1,0:T(8,128)(2,1)S(1)}, u32[]{:S(2)}, u32[]{:S(2)}) collective-permute-start(bf16[1024,128]{1,0:T(8,128)(2,1)S(1)} %fusion.own), channel_id=1, source_target_pairs={{0,96},{32,0},{64,32},{96,64},{1,97},{33,1},{65,33},{97,65},{2,98}... | collective-permute-start | bytes 786440 | tf_op jit(solution)/shard_map/ppermute | solution.py:665
  170.5 6.2 %collective-permute-done.10.preceding = bf16[1024,128]{1,0:T(8,128)(2,1)S(1)} collective-permute-done((bf16[1024,128]{1,0:T(8,128)(2,1)S(1)}, bf16[1024,128]{1,0:T(8,128)(2,1)S(1)}, u32[]{:S(2)}, u32[]{:S(2)}) %collective-permute-start.10) | collective-permute-done | bytes 262176 | tf_op jit(solution)/shard_map/ppermute | solution.py:664
  176.7 0.1 collective-permute-start.11
  176.8 2.7 %collective-permute-start.9 = (bf16[512,128]{1,0:T(8,128)(2,1)S(1)}, bf16[512,128]{1,0:T(8,128)(2,1)S(1)}, u32[]{:S(2)}, u32[]{:S(2)}) collective-permute-start(bf16[512,128]{1,0:T(8,128)(2,1)S(1)} %slice.62), channel_id=1, source_target_pairs={{0,96},{32,0},{64,32},{96,64},{1,97},{33,1},{65,33},{97,65},{2,98}... | collective-permute-start | bytes 393224 | tf_op jit(solution)/shard_map/ppermute | solution.py:665
  179.6 2.6 %collective-permute-done.11.opposite_b = bf16[512,128]{1,0:T(8,128)(2,1)S(1)} collective-permute-done((bf16[512,128]{1,0:T(8,128)(2,1)S(1)}, bf16[512,128]{1,0:T(8,128)(2,1)S(1)}, u32[]{:S(2)}, u32[]{:S(2)}) %collective-permute-start.11) | collective-permute-done | bytes 131104 | tf_op jit(solution)/shard_map/ppermute | solution.py:664
  182.1 1.5 spread_rows.1
  183.6 2.6 %all-to-all-done.3.pieces = bf16[32,32,640]{2,1,0:T(8,128)(2,1)S(1)} async-done(((bf16[32,32,640]{2,1,0:T(8,128)(2,1)}), bf16[32,32,640]{2,1,0:T(8,128)(2,1)S(1)}, u32[]{:S(2)}, u32[]{:S(2)}) %all-to-all-start.3) | async-done | bytes 1310752 | tf_op jit(solution)/shard_map/all_to_all | solution.py:767
  186.2 0.8 finish.1
  (22 shorter events, 0.1 us)
Async XLA Ops:
  12.2 9.7 %copy-start.9 = (bf16[512]{0:T(512)(128)(2,1)S(1)}, bf16[512]{0:T(512)(128)(2,1)}, u32[]{:S(2)}) copy-start(bf16[512]{0:T(512)(128)(2,1)} %param.23) | copy-start | bytes 3076
  12.2 9.7 %copy-start.8 = (s32[384]{0:T(512)S(1)}, s32[384]{0:T(512)}, u32[]{:S(2)}) copy-start(s32[384]{0:T(512)} %param.17) | copy-start | bytes 4612
  12.2 49.5 %copy-start.2 = (f32[4096]{0:T(1024)S(1)}, f32[4096]{0:T(1024)}, u32[]{:S(2)}) copy-start(f32[4096]{0:T(1024)} %param.20) | copy-start | bytes 49156
  12.3 49.5 %copy-start.4 = (f32[512]{0:T(512)S(1)}, f32[512]{0:T(512)}, u32[]{:S(2)}) copy-start(f32[512]{0:T(512)} %param.22) | copy-start | bytes 6148
  12.3 49.5 %copy-start.5 = (s32[32]{0:T(128)S(1)}, s32[32]{0:T(128)}, u32[]{:S(2)}) copy-start(s32[32]{0:T(128)} %fmap.3) | copy-start | bytes 388
  12.3 49.5 %all-to-all-start = ((bf16[32,384,128]{2,1,0:T(8,128)(2,1)}), bf16[32,384,128]{2,1,0:T(8,128)(2,1)}, u32[]{:S(2)}, u32[]{:S(2)}) async-start(bf16[32,384,128]{2,1,0:T(8,128)(2,1)} %bitcast.25), calls=%async_computation | async-start | bytes 6291456 | tf_op jit(solution)/shard_map/all_to_all | solution.py:720
  77.9 44.9 %all-to-all-start.1 = ((bf16[32,384,128]{2,1,0:T(8,128)(2,1)}), bf16[32,384,128]{2,1,0:T(8,128)(2,1)}, u32[]{:S(2)}, u32[]{:S(2)}) async-start(bf16[32,384,128]{2,1,0:T(8,128)(2,1)} %get-tuple-element.52), calls=%async_computation.1 | async-start | bytes 6291456 | tf_op jit(solution)/shard_map/all_to_all | solution.py:735
  95.5 3.0 %collective-permute-start.2 = (bf16[8,2,272,128]{3,2,1,0:T(8,128)(2,1)}, bf16[8,2,272,128]{3,2,1,0:T(8,128)(2,1)S(1)}, u32[]{:S(2)}, u32[]{:S(2)}) collective-permute-start(bf16[8,2,272,128]{3,2,1,0:T(8,128)(2,1)} %get-tuple-element.48), channel_id=1, source_target_pairs={{0,1},{1,0},{2,3},{3,2},{4,5},{5,4},{6,7},{7,6},{8,9},{9,8},{10,11... | collective-permute-start | bytes 3342344 | tf_op jit(solution)/shard_map/ppermute | solution.py:757
  95.9 6.3 %collective-permute-start.1 = (bf16[8,2,272,128]{3,2,1,0:T(8,128)(2,1)}, bf16[8,2,272,128]{3,2,1,0:T(8,128)(2,1)S(1)}, u32[]{:S(2)}, u32[]{:S(2)}) collective-permute-start(bf16[8,2,272,128]{3,2,1,0:T(8,128)(2,1)} %get-tuple-element.46), channel_id=1, source_target_pairs={{0,1},{1,0},{2,3},{3,2},{4,5},{5,4},{6,7},{7,6},{8,9},{9,8},{10,11... | collective-permute-start | bytes 3342344 | tf_op jit(solution)/shard_map/ppermute | solution.py:757
  96.1 22.2 %collective-permute-start.5 = (bf16[8,2,272,128]{3,2,1,0:T(8,128)(2,1)}, bf16[8,2,272,128]{3,2,1,0:T(8,128)(2,1)S(1)}, u32[]{:S(2)}, u32[]{:S(2)}) collective-permute-start(bf16[8,2,272,128]{3,2,1,0:T(8,128)(2,1)} %get-tuple-element.50), channel_id=1, source_target_pairs={{0,1},{1,0},{2,3},{3,2},{4,5},{5,4},{6,7},{7,6},{8,9},{9,8},{10,11... | collective-permute-start | bytes 3342344 | tf_op jit(solution)/shard_map/ppermute | solution.py:757
  98.5 14.8 %copy-start.7 = (bf16[8,2,272,128]{3,2,1,0:T(8,128)(2,1)S(1)}, bf16[8,2,272,128]{3,2,1,0:T(8,128)(2,1)}, u32[]{:S(2)}) copy-start(bf16[8,2,272,128]{3,2,1,0:T(8,128)(2,1)} %get-tuple-element.45) | copy-start | bytes 3342340
  98.9 14.5 %collective-permute-start.3 = (bf16[4,2,272,128]{3,2,1,0:T(8,128)(2,1)S(1)}, bf16[4,2,272,128]{3,2,1,0:T(8,128)(2,1)S(1)}, u32[]{:S(2)}, u32[]{:S(2)}) collective-permute-start(bf16[4,2,272,128]{3,2,1,0:T(8,128)(2,1)S(1)} %get-tuple-element.64), channel_id=1, source_target_pairs={{0,96},{32,0},{64,32},{96,64},{1,97},{33,1},{65,33},{97,65},{2,98}... | collective-permute-start | bytes 1671176 | tf_op jit(solution)/shard_map/ppermute | solution.py:665
  101.6 16.7 %collective-permute-start.6 = (bf16[4,2,272,128]{3,2,1,0:T(8,128)(2,1)S(1)}, bf16[4,2,272,128]{3,2,1,0:T(8,128)(2,1)S(1)}, u32[]{:S(2)}, u32[]{:S(2)}) collective-permute-start(bf16[4,2,272,128]{3,2,1,0:T(8,128)(2,1)S(1)} %get-tuple-element.63), channel_id=1, source_target_pairs={{0,32},{32,64},{64,96},{96,0},{1,33},{33,65},{65,97},{97,1},{2,34}... | collective-permute-start | bytes 1671176 | tf_op jit(solution)/shard_map/ppermute | solution.py:664
  101.6 32.9 %collective-permute-start = (bf16[8,2,272,128]{3,2,1,0:T(8,128)(2,1)}, bf16[8,2,272,128]{3,2,1,0:T(8,128)(2,1)S(1)}, u32[]{:S(2)}, u32[]{:S(2)}) collective-permute-start(bf16[8,2,272,128]{3,2,1,0:T(8,128)(2,1)} %get-tuple-element.44), channel_id=1, source_target_pairs={{0,1},{1,0},{2,3},{3,2},{4,5},{5,4},{6,7},{7,6},{8,9},{9,8},{10,11... | collective-permute-start | bytes 3342344 | tf_op jit(solution)/shard_map/ppermute | solution.py:757
  113.7 4.6 %copy-start.6 = (bf16[8,2,272,128]{3,2,1,0:T(8,128)(2,1)S(1)}, bf16[8,2,272,128]{3,2,1,0:T(8,128)(2,1)}, u32[]{:S(2)}) copy-start(bf16[8,2,272,128]{3,2,1,0:T(8,128)(2,1)} %get-tuple-element.49) | copy-start | bytes 3342340
  114.8 26.7 %collective-permute-start.4 = (bf16[8,2,272,128]{3,2,1,0:T(8,128)(2,1)}, bf16[8,2,272,128]{3,2,1,0:T(8,128)(2,1)S(1)}, u32[]{:S(2)}, u32[]{:S(2)}) collective-permute-start(bf16[8,2,272,128]{3,2,1,0:T(8,128)(2,1)} %pad_maximum_fusion), channel_id=1, source_target_pairs={{0,96},{32,0},{64,32},{96,64},{1,97},{33,1},{65,33},{97,65},{2,98}... | collective-permute-start | bytes 3342344 | tf_op jit(solution)/shard_map/ppermute | solution.py:665
  118.7 4.1 %copy-start.3 = (s32[1,96,16]{1,2,0:T(8,128)S(1)}, s32[1,96,16]{1,2,0:T(8,128)}, u32[]{:S(2)}) copy-start(s32[1,96,16]{1,2,0:T(8,128)} %param.13) | copy-start | bytes 18436
  119.8 26.3 %collective-permute-start.7 = (bf16[8,2,272,128]{3,2,1,0:T(8,128)(2,1)}, bf16[8,2,272,128]{3,2,1,0:T(8,128)(2,1)}, u32[]{:S(2)}, u32[]{:S(2)}) collective-permute-start(bf16[8,2,272,128]{3,2,1,0:T(8,128)(2,1)} %pad_maximum_fusion.1), channel_id=1, source_target_pairs={{0,32},{32,64},{64,96},{96,0},{1,33},{33,65},{65,97},{97,1},{2,34}... | collective-permute-start | bytes 3342344 | tf_op jit(solution)/shard_map/ppermute | solution.py:664
  129.2 1.0 copy-start.1
  130.2 15.9 %copy-start = (bf16[8,2,272,128]{3,2,1,0:T(8,128)(2,1)S(1)}, bf16[8,2,272,128]{3,2,1,0:T(8,128)(2,1)}, u32[]{:S(2)}) copy-start(bf16[8,2,272,128]{3,2,1,0:T(8,128)(2,1)} %get-tuple-element.43.own) | copy-start | bytes 3342340
  130.2 26.5 %all-to-all-start.2 = ((bf16[4,1024,128]{2,1,0:T(8,128)(2,1)}), bf16[4,1024,128]{2,1,0:T(8,128)(2,1)}, u32[]{:S(2)}, u32[]{:S(2)}) async-start(bf16[4,1024,128]{2,1,0:T(8,128)(2,1)} %copy-done.1), calls=%async_computation.2 | async-start | bytes 2097152 | tf_op jit(solution)/shard_map/all_to_all | solution.py:763
  156.7 29.5 %all-to-all-start.3 = ((bf16[32,32,640]{2,1,0:T(8,128)(2,1)}), bf16[32,32,640]{2,1,0:T(8,128)(2,1)S(1)}, u32[]{:S(2)}, u32[]{:S(2)}) async-start(bf16[32,32,640]{2,1,0:T(8,128)(2,1)} %fold.1), calls=%async_computation.3 | async-start | bytes 2621440 | tf_op jit(solution)/shard_map/all_to_all | solution.py:767
  167.8 9.0 %collective-permute-start.10 = (bf16[1024,128]{1,0:T(8,128)(2,1)S(1)}, bf16[1024,128]{1,0:T(8,128)(2,1)S(1)}, u32[]{:S(2)}, u32[]{:S(2)}) collective-permute-start(bf16[1024,128]{1,0:T(8,128)(2,1)S(1)} %fusion.own), channel_id=1, source_target_pairs={{0,32},{32,64},{64,96},{96,0},{1,33},{33,65},{65,97},{97,1},{2,34}... | collective-permute-start | bytes 786440 | tf_op jit(solution)/shard_map/ppermute | solution.py:664
  167.8 9.0 %collective-permute-start.8 = (bf16[1024,128]{1,0:T(8,128)(2,1)S(1)}, bf16[1024,128]{1,0:T(8,128)(2,1)S(1)}, u32[]{:S(2)}, u32[]{:S(2)}) collective-permute-start(bf16[1024,128]{1,0:T(8,128)(2,1)S(1)} %fusion.own), channel_id=1, source_target_pairs={{0,96},{32,0},{64,32},{96,64},{1,97},{33,1},{65,33},{97,65},{2,98}... | collective-permute-start | bytes 786440 | tf_op jit(solution)/shard_map/ppermute | solution.py:665
  176.7 5.4 %collective-permute-start.11 = (bf16[512,128]{1,0:T(8,128)(2,1)S(1)}, bf16[512,128]{1,0:T(8,128)(2,1)S(1)}, u32[]{:S(2)}, u32[]{:S(2)}) collective-permute-start(bf16[512,128]{1,0:T(8,128)(2,1)S(1)} %slice.63), channel_id=1, source_target_pairs={{0,32},{32,64},{64,96},{96,0},{1,33},{33,65},{65,97},{97,1},{2,34}... | collective-permute-start | bytes 393224 | tf_op jit(solution)/shard_map/ppermute | solution.py:664
  176.8 5.3 %collective-permute-start.9 = (bf16[512,128]{1,0:T(8,128)(2,1)S(1)}, bf16[512,128]{1,0:T(8,128)(2,1)S(1)}, u32[]{:S(2)}, u32[]{:S(2)}) collective-permute-start(bf16[512,128]{1,0:T(8,128)(2,1)S(1)} %slice.62), channel_id=1, source_target_pairs={{0,96},{32,0},{64,32},{96,64},{1,97},{33,1},{65,33},{97,65},{2,98}... | collective-permute-start | bytes 393224 | tf_op jit(solution)/shard_map/ppermute | solution.py:665

commit v6 on v5

--- a/solution.py
+++ b/solution.py
@@ -10,7 +10,7 @@
 
 BLK = 8
 LOSS_SCALE = 65536.0
-STEP_TILES = 16
+STEP_TILES = 24
 WIDE = 2048
 EXTRA = 16
 PAIR = 4
@@ -227,7 +227,6 @@
     cross_bias_grad,
     hidden_bias_grad,
     out_weight_grad,
-    inter,
     crossed,
     proj_low,
     held,
@@ -241,7 +240,6 @@
     hidden,
     low_sum,
     slot_of,
-    in_sem,
     weight_sems,
     small_sems,
     wide_sems,
@@ -256,8 +254,6 @@
         for i, (source, target) in enumerate(((v_hbm, v), (u_hbm, u), (h_hbm, h)))
     ]
     weights[0].start()
-    load = pltpu.make_async_copy(received, inter, in_sem)
-    load.start()
     weights[1].start()
     weights[2].start()
 
@@ -267,7 +263,7 @@
 
     def of_block(b):
         slots = [slot_of[b * per_block + i] for i in range(per_block)]
-        return jnp.concatenate([inter[slot] for slot in slots], axis=1).astype(F32)
+        return jnp.concatenate([received[slot] for slot in slots], axis=1).astype(F32)
 
     def put(target, b, value):
         for i in range(per_block):
@@ -285,12 +281,11 @@
     hidden[...] = jnp.broadcast_to(hidden_bias[...], hidden.shape)
     hidden_bias_grad[...] = jnp.zeros_like(hidden_bias_grad)
     out_weight_grad[...] = jnp.zeros_like(out_weight_grad)
-    load.wait()
     weights[0].wait()
     for b in range(blocks):
         slots = range(b * per_block, (b + 1) * per_block)
         places = [pl.ds(pl.multiple_of(fmap[s] * width, width), width) for s in slots]
-        left = jnp.concatenate([inter[s] for s in slots], axis=1)
+        left = jnp.concatenate([received[s] for s in slots], axis=1)
         right = jnp.concatenate([v[place, :] for place in places], axis=0)
         low_sum[...] += jnp.dot(left, right, preferred_element_type=F32)
 
@@ -312,7 +307,7 @@
         hidden[...] += jnp.dot(product, h[cols, :], preferred_element_type=F32)
         store(0, crossed, crossed_hbm, b).start()
 
-    chunk = 64
+    chunk = 192
 
     @pl.loop(0, batch // chunk)
     def _(r):
@@ -390,7 +385,6 @@
         scratch_shapes=[
             pltpu.VMEM(received.shape, BF),
             pltpu.VMEM(received.shape, BF),
-            pltpu.VMEM(received.shape, BF),
             pltpu.VMEM((batch, total_width), F32),
             pltpu.VMEM(received.shape, BF),
             pltpu.VMEM(v.shape, BF),
@@ -402,7 +396,6 @@
             pltpu.VMEM((batch, units), F32),
             pltpu.VMEM((batch, rank), F32),
             pltpu.SMEM((features,), jnp.int32),
-            pltpu.SemaphoreType.DMA,
             pltpu.SemaphoreType.DMA((3,)),
             pltpu.SemaphoreType.DMA((3,)),
             pltpu.SemaphoreType.DMA((3, total_width // WIDE)),
@@ -428,9 +421,9 @@
 ):
     parts, chunks = len(order), len(ORDER)
     outs = rest[: 2 * parts]
-    inter_in, crossed_in, proj_in, low, low_grad, d_hidden = rest[2 * parts : 2 * parts + 6]
-    low_t, low_grad_t, d_hidden_t, small, keep, send = rest[2 * parts + 6 : -5]
-    slot_of, small_sems, inter_sem, wide_sems, out_sems = rest[-5:]
+    crossed_in, proj_in, low, low_grad, d_hidden = rest[2 * parts : 2 * parts + 5]
+    low_t, low_grad_t, d_hidden_t, small, keep, send = rest[2 * parts + 5 : -4]
+    slot_of, small_sems, wide_sems, out_sems = rest[-4:]
     features = fmap.shape[0]
     width = keep.shape[-1]
     rank = low_t.shape[0]
@@ -456,8 +449,6 @@
             pltpu.make_async_copy(proj.at[pl.ds(base, each)], proj_in.at[span], wide_sems.at[1, part]),
         ]
         loads.append(copies)
-    whole = pltpu.make_async_copy(received, inter_in, inter_sem)
-    whole.start()
     for copy in loads[0]:
         copy.start()
     for copy in smalls:
@@ -495,7 +486,6 @@
     nothing = jnp.zeros((EXTRA, width), BF)
     first = place[0] == 0
 
-    whole.wait()
     for part, offset in enumerate(order):
         for copy in loads[part]:
             copy.wait()
@@ -512,7 +502,7 @@
                 both = jnp.concatenate(right, axis=1)
                 return jnp.dot(left[...], both, preferred_element_type=F32).astype(BF)
 
-            of_v = product(low_grad_t, *[inter_in[slot_of[base + i]] for i in range(PAIR)])
+            of_v = product(low_grad_t, *[received[slot_of[base + i]] for i in range(PAIR)])
             of_u = product(low_t, *[proj_in[n + i] for i in range(PAIR)])
             of_h = product(d_hidden_t, *[crossed_in[n + i] for i in range(PAIR)])
 
@@ -565,8 +555,7 @@
         in_specs=[smem, smem, vmem] + [hbm] * 5 + [vmem] * 3,
         out_specs=[hbm] * (2 * parts),
         out_shape=[part] * (2 * parts),
-        scratch_shapes=[pltpu.VMEM((features, batch, width), BF)]
-        + [pltpu.VMEM((held, batch, width), BF)] * 2
+        scratch_shapes=[pltpu.VMEM((held, batch, width), BF)] * 2
         + [
             pltpu.VMEM((batch, rank), BF),
             pltpu.VMEM((batch, rank), BF),
@@ -579,7 +568,6 @@
             pltpu.VMEM((held, 2, rank + EXTRA, width), BF),
             pltpu.SMEM((features,), jnp.int32),
             pltpu.SemaphoreType.DMA((3,)),
-            pltpu.SemaphoreType.DMA,
             pltpu.SemaphoreType.DMA((2, parts)),
             pltpu.SemaphoreType.DMA((2 * parts, features // len(ORDER) // PAIR)),
         ],

time: 188 us -> 187 us (level)
  no operation moved by 1% of the time
where the time goes in v6:
time: 187 us; the launch traced here: 186 us
  waiting for transfers between devices  86.1 us (46%)
  Pallas kernels  50.9 us (27%)
  starting transfers between devices  42.3 us (23%)
  other arithmetic  4.62 us (2%)
    all_to_all x1, waiting for transfers between devices, body(): lax.all_to_all(pooled.reshape(features, batch, width), dp, split_axis=0,...  39.6 us
    ppermute x4, waiting for transfers between devices, neighbours(): lax.ppermute(value, axis, down)  18.2 us
    pallas_call x1, Pallas kernels, dense(): pl.pallas_call(functools.partial(dense_kernel, scale), name='dense', in_s...  15.3 us
    ppermute x4, waiting for transfers between devices, neighbours(): lax.ppermute(value, axis, up)  13.4 us
    pallas_call x1, Pallas kernels, gradients(): pl.pallas_call(functools.partial(gradients_kernel, order), name='gradient...  12.3 us
    ppermute x4, starting transfers between devices, neighbours(): lax.ppermute(value, axis, down)  11.7 us
    pallas_call x1, Pallas kernels, pool(): pl.pallas_call(pool_kernel, name='pool', in_specs=[pl.BlockSpec(memory_sp...  11.4 us
    all_to_all x1, starting transfers between devices, body(): pieces = lax.all_to_all(folded, dp, split_axis=0, concat_axis=0, tiled=True)  9.71 us
  transfers between devices with their start and end apart: 16, of which 10 were waited for; matrix products, arithmetic and copies ran while one was open for 3% of the time, Pallas kernels for 13%

profile of v6, /device:TPU:1, one launch (start us, length us, event | category | flops | bytes accessed | tf_op | source)
XLA Modules:
  0.0 185.9 jit_solution(708522790432327384)
XLA Ops:
  0.6 11.4 %pool.1 = (bf16[12288,128]{1,0:T(8,128)(2,1)}, bf16[96,128,128]{2,1,0:T(8,128)(2,1)}) custom-call(s32[16,96]{1,0:T(8,128)} %bitcast.22, bf16[4096,128]{1,0:T(8,128)(2,1)} %table.1, s32[16,12288]{1,0:T(8,128)} %bitcast.26, s32[16,12288]{1,0:T(8,128)} %bitcast.27), custom_call_target="tpu_custom_call" | custom-call | tf_op jit(solution)/shard_map/pool/pallas_call | solution.py:98
  12.0 0.0 copy-start.9
  12.0 0.0 copy-start.8
  12.1 0.0 copy-start.2
  12.1 0.0 copy-start.4
  12.1 0.0 copy-start.5
  12.1 9.6 %all-to-all-start = ((bf16[32,384,128]{2,1,0:T(8,128)(2,1)}), bf16[32,384,128]{2,1,0:T(8,128)(2,1)}, u32[]{:S(2)}, u32[]{:S(2)}) async-start(bf16[32,384,128]{2,1,0:T(8,128)(2,1)} %bitcast.25), calls=%async_computation | async-start | bytes 6291456 | tf_op jit(solution)/shard_map/all_to_all | solution.py:708
  21.7 0.1 reshape.62.labels
  21.9 0.1 pad_add_fusion.place
  21.9 39.6 %all-to-all-done.received = bf16[32,384,128]{2,1,0:T(8,128)(2,1)} async-done(((bf16[32,384,128]{2,1,0:T(8,128)(2,1)}), bf16[32,384,128]{2,1,0:T(8,128)(2,1)}, u32[]{:S(2)}, u32[]{:S(2)}) %all-to-all-start) | async-done | bytes 3145760 | tf_op jit(solution)/shard_map/all_to_all | solution.py:708
  61.5 15.3 %dense.1 = (bf16[32,384,128]{2,1,0:T(8,128)(2,1)}, bf16[32,384,128]{2,1,0:T(8,128)(2,1)}, bf16[32,384,128]{2,1,0:T(8,128)(2,1)}, bf16[384,256]{1,0:T(8,128)(2,1)...) custom-call(s32[32]{0:T(128)S(1)} %copy-done.5, ...), custom_call_target="tpu_custom_call" | custom-call | tf_op jit(solution)/shard_map/dense/pallas_call | solution.py:369
  76.9 5.0 %all-to-all-start.1 = ((bf16[32,384,128]{2,1,0:T(8,128)(2,1)}), bf16[32,384,128]{2,1,0:T(8,128)(2,1)}, u32[]{:S(2)}, u32[]{:S(2)}) async-start(bf16[32,384,128]{2,1,0:T(8,128)(2,1)} %get-tuple-element.52), calls=%async_computation.1 | async-start | bytes 6291456 | tf_op jit(solution)/shard_map/all_to_all | solution.py:723
  81.9 12.3 %gradients.1 = (bf16[8,2,272,128]{3,2,1,0:T(8,128)(2,1)S(1)}, bf16[8,2,272,128]{3,2,1,0:T(8,128)(2,1)}, bf16[8,2,272,128]{3,2,1,0:T(8,128)(2,1)}, bf16[8,2,272,1...) custom-call(s32[2]{0:T(128)S(1)} %pad_add_fusion.place, ...), custom_call_target="tpu_custom_call" | custom-call | flops 3221225472 | bytes 16777216 | tf_op jit(solution)/shard_map/gradients/pallas_call | solution.py:552
  94.2 0.6 collective-permute-start.2
  94.8 0.2 collective-permute-start.1
  95.0 0.3 collective-permute-start.5
  95.3 2.1 %collective-permute-done.2 = bf16[8,2,272,128]{3,2,1,0:T(8,128)(2,1)S(1)} collective-permute-done((bf16[8,2,272,128]{3,2,1,0:T(8,128)(2,1)}, bf16[8,2,272,128]{3,2,1,0:T(8,128)(2,1)S(1)}, u32[]{:S(2)}, u32[]{:S(2)}) %collective-permute-start.2) | collective-permute-done | bytes 1114144 | tf_op jit(solution)/shard_map/ppermute | solution.py:745
  97.4 0.3 add_convert_fusion.1
  97.7 2.8 %collective-permute-start.3 = (bf16[4,2,272,128]{3,2,1,0:T(8,128)(2,1)S(1)}, bf16[4,2,272,128]{3,2,1,0:T(8,128)(2,1)S(1)}, u32[]{:S(2)}, u32[]{:S(2)}) collective-permute-start(bf16[4,2,272,128]{3,2,1,0:T(8,128)(2,1)S(1)} %get-tuple-element.64), channel_id=1, source_target_pairs={{0,96},{32,0},{64,32},{96,64},{1,97},{33,1},{65,33},{97,65},{2,98}... | collective-permute-start | bytes 1671176 | tf_op jit(solution)/shard_map/ppermute | solution.py:653
  100.5 0.0 collective-permute-start.6
  100.6 0.6 collective-permute-start
  101.1 11.1 %collective-permute-done.3 = bf16[4,2,272,128]{3,2,1,0:T(8,128)(2,1)S(1)} collective-permute-done((bf16[4,2,272,128]{3,2,1,0:T(8,128)(2,1)S(1)}, bf16[4,2,272,128]{3,2,1,0:T(8,128)(2,1)S(1)}, u32[]{:S(2)}, u32[]{:S(2)}) %collective-permute-start.3) | collective-permute-done | bytes 557088 | tf_op jit(solution)/shard_map/ppermute | solution.py:653
  112.3 0.4 add_convert_fusion.5
  112.6 0.0 copy-start.6
  112.6 1.1 pad_maximum_fusion
  113.7 3.5 %collective-permute-start.4 = (bf16[8,2,272,128]{3,2,1,0:T(8,128)(2,1)}, bf16[8,2,272,128]{3,2,1,0:T(8,128)(2,1)S(1)}, u32[]{:S(2)}, u32[]{:S(2)}) collective-permute-start(bf16[8,2,272,128]{3,2,1,0:T(8,128)(2,1)} %pad_maximum_fusion), channel_id=1, source_target_pairs={{0,96},{32,0},{64,32},{96,64},{1,97},{33,1},{65,33},{97,65},{2,98}... | collective-permute-start | bytes 3342344 | tf_op jit(solution)/shard_map/ppermute | solution.py:653
  117.3 0.4 add_convert_fusion.3
  117.6 0.0 copy-start.3
  117.7 1.1 pad_maximum_fusion.1
  118.7 3.0 %all-to-all-done.1 = bf16[32,384,128]{2,1,0:T(8,128)(2,1)} async-done(((bf16[32,384,128]{2,1,0:T(8,128)(2,1)}), bf16[32,384,128]{2,1,0:T(8,128)(2,1)}, u32[]{:S(2)}, u32[]{:S(2)}) %all-to-all-start.1) | async-done | bytes 3145760 | tf_op jit(solution)/shard_map/all_to_all | solution.py:723
  121.7 6.2 %scatter.1 = bf16[4,1024,128]{2,1,0:T(8,128)(2,1)S(1)} custom-call(s32[16,96]{1,0:T(8,128)S(1)} %bitcast.23, bf16[96,128,128]{2,1,0:T(8,128)(2,1)} %get-tuple-element.51.incidence, bf16[12288,128]{1,0:T(8,128)(2,1)} %bitcast.12.grad), custom_call_target="tpu_custom_call" | custom-call | flops 8589934592 | bytes 8388608 | tf_op jit(solution)/shard_map/scatter/pallas_call | solution.py:165
  128.0 1.0 copy-done.1
  129.0 4.4 %all-to-all-start.2 = ((bf16[4,1024,128]{2,1,0:T(8,128)(2,1)}), bf16[4,1024,128]{2,1,0:T(8,128)(2,1)}, u32[]{:S(2)}, u32[]{:S(2)}) async-start(bf16[4,1024,128]{2,1,0:T(8,128)(2,1)} %copy-done.1), calls=%async_computation.2 | async-start | bytes 2097152 | tf_op jit(solution)/shard_map/all_to_all | solution.py:751
  133.4 7.0 %collective-permute-done.4.from_following = bf16[8,2,272,128]{3,2,1,0:T(8,128)(2,1)S(1)} collective-permute-done((bf16[8,2,272,128]{3,2,1,0:T(8,128)(2,1)}, bf16[8,2,272,128]{3,2,1,0:T(8,128)(2,1)S(1)}, u32[]{:S(2)}, u32[]{:S(2)}) %collective-permute-start.4) | collective-permute-done | bytes 1114144 | tf_op jit(solution)/shard_map/ppermute | solution.py:653
  140.4 4.6 %collective-permute-done.7.from_preceding = bf16[8,2,272,128]{3,2,1,0:T(8,128)(2,1)} collective-permute-done((bf16[8,2,272,128]{3,2,1,0:T(8,128)(2,1)}, bf16[8,2,272,128]{3,2,1,0:T(8,128)(2,1)}, u32[]{:S(2)}, u32[]{:S(2)}) %collective-permute-start.7) | collective-permute-done | bytes 1114144 | tf_op jit(solution)/shard_map/ppermute | solution.py:652
  145.0 3.5 %fold.1 = bf16[32,32,640]{2,1,0:T(8,128)(2,1)} custom-call(bf16[8,2,272,128]{3,2,1,0:T(8,128)(2,1)S(1)} %copy-done, bf16[8,2,272,128]{3,2,1,0:T(8,128)(2,1)S(1)} %collective-permute-done.swapped, bf16[8,2,272,128]{3,2,1,0:T(8,128)(2,1)S(1)} %collective-permute-done.4.from_following, bf16[8,2,272,128]{3,2,1,0:T(8,128)(2,1)} %collective-permute-done.7.from_preceding), custom_call_target="tpu_custom_call" | custom-call | tf_op jit(solution)/shard_map/fold/pallas_call | solution.py:605
  148.5 7.1 %all-to-all-done.2 = bf16[4,1024,128]{2,1,0:T(8,128)(2,1)} async-done(((bf16[4,1024,128]{2,1,0:T(8,128)(2,1)}), bf16[4,1024,128]{2,1,0:T(8,128)(2,1)}, u32[]{:S(2)}, u32[]{:S(2)}) %all-to-all-start.2) | async-done | bytes 1048608 | tf_op jit(solution)/shard_map/all_to_all | solution.py:751
  155.6 9.7 %all-to-all-start.3 = ((bf16[32,32,640]{2,1,0:T(8,128)(2,1)}), bf16[32,32,640]{2,1,0:T(8,128)(2,1)S(1)}, u32[]{:S(2)}, u32[]{:S(2)}) async-start(bf16[32,32,640]{2,1,0:T(8,128)(2,1)} %fold.1), calls=%async_computation.3 | async-start | bytes 2621440 | tf_op jit(solution)/shard_map/all_to_all | solution.py:755
  165.3 1.3 fusion.own
  166.7 0.1 collective-permute-start.10
  166.7 2.7 %collective-permute-start.8 = (bf16[1024,128]{1,0:T(8,128)(2,1)S(1)}, bf16[1024,128]{1,0:T(8,128)(2,1)S(1)}, u32[]{:S(2)}, u32[]{:S(2)}) collective-permute-start(bf16[1024,128]{1,0:T(8,128)(2,1)S(1)} %fusion.own), channel_id=1, source_target_pairs={{0,96},{32,0},{64,32},{96,64},{1,97},{33,1},{65,33},{97,65},{2,98}... | collective-permute-start | bytes 786440 | tf_op jit(solution)/shard_map/ppermute | solution.py:653
  169.4 6.2 %collective-permute-done.10.preceding = bf16[1024,128]{1,0:T(8,128)(2,1)S(1)} collective-permute-done((bf16[1024,128]{1,0:T(8,128)(2,1)S(1)}, bf16[1024,128]{1,0:T(8,128)(2,1)S(1)}, u32[]{:S(2)}, u32[]{:S(2)}) %collective-permute-start.10) | collective-permute-done | bytes 262176 | tf_op jit(solution)/shard_map/ppermute | solution.py:652
  175.6 0.1 collective-permute-start.11
  175.7 2.7 %collective-permute-start.9 = (bf16[512,128]{1,0:T(8,128)(2,1)S(1)}, bf16[512,128]{1,0:T(8,128)(2,1)S(1)}, u32[]{:S(2)}, u32[]{:S(2)}) collective-permute-start(bf16[512,128]{1,0:T(8,128)(2,1)S(1)} %slice.62), channel_id=1, source_target_pairs={{0,96},{32,0},{64,32},{96,64},{1,97},{33,1},{65,33},{97,65},{2,98}... | collective-permute-start | bytes 393224 | tf_op jit(solution)/shard_map/ppermute | solution.py:653
  178.5 2.6 %collective-permute-done.11.opposite_b = bf16[512,128]{1,0:T(8,128)(2,1)S(1)} collective-permute-done((bf16[512,128]{1,0:T(8,128)(2,1)S(1)}, bf16[512,128]{1,0:T(8,128)(2,1)S(1)}, u32[]{:S(2)}, u32[]{:S(2)}) %collective-permute-start.11) | collective-permute-done | bytes 131104 | tf_op jit(solution)/shard_map/ppermute | solution.py:652
  181.0 1.5 spread_rows.1
  182.5 2.6 %all-to-all-done.3.pieces = bf16[32,32,640]{2,1,0:T(8,128)(2,1)S(1)} async-done(((bf16[32,32,640]{2,1,0:T(8,128)(2,1)}), bf16[32,32,640]{2,1,0:T(8,128)(2,1)S(1)}, u32[]{:S(2)}, u32[]{:S(2)}) %all-to-all-start.3) | async-done | bytes 1310752 | tf_op jit(solution)/shard_map/all_to_all | solution.py:755
  185.1 0.8 finish.1
  (22 shorter events, 0.1 us)
Async XLA Ops:
  12.0 9.7 %copy-start.9 = (bf16[512]{0:T(512)(128)(2,1)S(1)}, bf16[512]{0:T(512)(128)(2,1)}, u32[]{:S(2)}) copy-start(bf16[512]{0:T(512)(128)(2,1)} %param.23) | copy-start | bytes 3076
  12.0 9.7 %copy-start.8 = (s32[384]{0:T(512)S(1)}, s32[384]{0:T(512)}, u32[]{:S(2)}) copy-start(s32[384]{0:T(512)} %param.17) | copy-start | bytes 4612
  12.1 49.5 %copy-start.2 = (f32[4096]{0:T(1024)S(1)}, f32[4096]{0:T(1024)}, u32[]{:S(2)}) copy-start(f32[4096]{0:T(1024)} %param.20) | copy-start | bytes 49156
  12.1 49.5 %copy-start.4 = (f32[512]{0:T(512)S(1)}, f32[512]{0:T(512)}, u32[]{:S(2)}) copy-start(f32[512]{0:T(512)} %param.22) | copy-start | bytes 6148
  12.1 49.5 %copy-start.5 = (s32[32]{0:T(128)S(1)}, s32[32]{0:T(128)}, u32[]{:S(2)}) copy-start(s32[32]{0:T(128)} %fmap.3) | copy-start | bytes 388
  12.1 49.4 %all-to-all-start = ((bf16[32,384,128]{2,1,0:T(8,128)(2,1)}), bf16[32,384,128]{2,1,0:T(8,128)(2,1)}, u32[]{:S(2)}, u32[]{:S(2)}) async-start(bf16[32,384,128]{2,1,0:T(8,128)(2,1)} %bitcast.25), calls=%async_computation | async-start | bytes 6291456 | tf_op jit(solution)/shard_map/all_to_all | solution.py:708
  76.9 44.9 %all-to-all-start.1 = ((bf16[32,384,128]{2,1,0:T(8,128)(2,1)}), bf16[32,384,128]{2,1,0:T(8,128)(2,1)}, u32[]{:S(2)}, u32[]{:S(2)}) async-start(bf16[32,384,128]{2,1,0:T(8,128)(2,1)} %get-tuple-element.52), calls=%async_computation.1 | async-start | bytes 6291456 | tf_op jit(solution)/shard_map/all_to_all | solution.py:723
  94.2 3.2 %collective-permute-start.2 = (bf16[8,2,272,128]{3,2,1,0:T(8,128)(2,1)}, bf16[8,2,272,128]{3,2,1,0:T(8,128)(2,1)S(1)}, u32[]{:S(2)}, u32[]{:S(2)}) collective-permute-start(bf16[8,2,272,128]{3,2,1,0:T(8,128)(2,1)} %get-tuple-element.48), channel_id=1, source_target_pairs={{0,1},{1,0},{2,3},{3,2},{4,5},{5,4},{6,7},{7,6},{8,9},{9,8},{10,11... | collective-permute-start | bytes 3342344 | tf_op jit(solution)/shard_map/ppermute | solution.py:745
  94.8 6.4 %collective-permute-start.1 = (bf16[8,2,272,128]{3,2,1,0:T(8,128)(2,1)}, bf16[8,2,272,128]{3,2,1,0:T(8,128)(2,1)S(1)}, u32[]{:S(2)}, u32[]{:S(2)}) collective-permute-start(bf16[8,2,272,128]{3,2,1,0:T(8,128)(2,1)} %get-tuple-element.46), channel_id=1, source_target_pairs={{0,1},{1,0},{2,3},{3,2},{4,5},{5,4},{6,7},{7,6},{8,9},{9,8},{10,11... | collective-permute-start | bytes 3342344 | tf_op jit(solution)/shard_map/ppermute | solution.py:745
  95.0 22.3 %collective-permute-start.5 = (bf16[8,2,272,128]{3,2,1,0:T(8,128)(2,1)}, bf16[8,2,272,128]{3,2,1,0:T(8,128)(2,1)S(1)}, u32[]{:S(2)}, u32[]{:S(2)}) collective-permute-start(bf16[8,2,272,128]{3,2,1,0:T(8,128)(2,1)} %get-tuple-element.50), channel_id=1, source_target_pairs={{0,1},{1,0},{2,3},{3,2},{4,5},{5,4},{6,7},{7,6},{8,9},{9,8},{10,11... | collective-permute-start | bytes 3342344 | tf_op jit(solution)/shard_map/ppermute | solution.py:745
  97.4 14.8 %copy-start.7 = (bf16[8,2,272,128]{3,2,1,0:T(8,128)(2,1)S(1)}, bf16[8,2,272,128]{3,2,1,0:T(8,128)(2,1)}, u32[]{:S(2)}) copy-start(bf16[8,2,272,128]{3,2,1,0:T(8,128)(2,1)} %get-tuple-element.45) | copy-start | bytes 3342340
  97.7 14.5 %collective-permute-start.3 = (bf16[4,2,272,128]{3,2,1,0:T(8,128)(2,1)S(1)}, bf16[4,2,272,128]{3,2,1,0:T(8,128)(2,1)S(1)}, u32[]{:S(2)}, u32[]{:S(2)}) collective-permute-start(bf16[4,2,272,128]{3,2,1,0:T(8,128)(2,1)S(1)} %get-tuple-element.64), channel_id=1, source_target_pairs={{0,96},{32,0},{64,32},{96,64},{1,97},{33,1},{65,33},{97,65},{2,98}... | collective-permute-start | bytes 1671176 | tf_op jit(solution)/shard_map/ppermute | solution.py:653
  100.5 16.7 %collective-permute-start.6 = (bf16[4,2,272,128]{3,2,1,0:T(8,128)(2,1)S(1)}, bf16[4,2,272,128]{3,2,1,0:T(8,128)(2,1)S(1)}, u32[]{:S(2)}, u32[]{:S(2)}) collective-permute-start(bf16[4,2,272,128]{3,2,1,0:T(8,128)(2,1)S(1)} %get-tuple-element.63), channel_id=1, source_target_pairs={{0,32},{32,64},{64,96},{96,0},{1,33},{33,65},{65,97},{97,1},{2,34}... | collective-permute-start | bytes 1671176 | tf_op jit(solution)/shard_map/ppermute | solution.py:652
  100.6 32.8 %collective-permute-start = (bf16[8,2,272,128]{3,2,1,0:T(8,128)(2,1)}, bf16[8,2,272,128]{3,2,1,0:T(8,128)(2,1)S(1)}, u32[]{:S(2)}, u32[]{:S(2)}) collective-permute-start(bf16[8,2,272,128]{3,2,1,0:T(8,128)(2,1)} %get-tuple-element.44), channel_id=1, source_target_pairs={{0,1},{1,0},{2,3},{3,2},{4,5},{5,4},{6,7},{7,6},{8,9},{9,8},{10,11... | collective-permute-start | bytes 3342344 | tf_op jit(solution)/shard_map/ppermute | solution.py:745
  112.6 4.6 %copy-start.6 = (bf16[8,2,272,128]{3,2,1,0:T(8,128)(2,1)S(1)}, bf16[8,2,272,128]{3,2,1,0:T(8,128)(2,1)}, u32[]{:S(2)}) copy-start(bf16[8,2,272,128]{3,2,1,0:T(8,128)(2,1)} %get-tuple-element.49) | copy-start | bytes 3342340
  113.7 26.7 %collective-permute-start.4 = (bf16[8,2,272,128]{3,2,1,0:T(8,128)(2,1)}, bf16[8,2,272,128]{3,2,1,0:T(8,128)(2,1)S(1)}, u32[]{:S(2)}, u32[]{:S(2)}) collective-permute-start(bf16[8,2,272,128]{3,2,1,0:T(8,128)(2,1)} %pad_maximum_fusion), channel_id=1, source_target_pairs={{0,96},{32,0},{64,32},{96,64},{1,97},{33,1},{65,33},{97,65},{2,98}... | collective-permute-start | bytes 3342344 | tf_op jit(solution)/shard_map/ppermute | solution.py:653
  117.6 4.1 %copy-start.3 = (s32[1,96,16]{1,2,0:T(8,128)S(1)}, s32[1,96,16]{1,2,0:T(8,128)}, u32[]{:S(2)}) copy-start(s32[1,96,16]{1,2,0:T(8,128)} %param.13) | copy-start | bytes 18436
  118.7 26.3 %collective-permute-start.7 = (bf16[8,2,272,128]{3,2,1,0:T(8,128)(2,1)}, bf16[8,2,272,128]{3,2,1,0:T(8,128)(2,1)}, u32[]{:S(2)}, u32[]{:S(2)}) collective-permute-start(bf16[8,2,272,128]{3,2,1,0:T(8,128)(2,1)} %pad_maximum_fusion.1), channel_id=1, source_target_pairs={{0,32},{32,64},{64,96},{96,0},{1,33},{33,65},{65,97},{97,1},{2,34}... | collective-permute-start | bytes 3342344 | tf_op jit(solution)/shard_map/ppermute | solution.py:652
  128.0 1.0 copy-start.1
  129.0 16.1 %copy-start = (bf16[8,2,272,128]{3,2,1,0:T(8,128)(2,1)S(1)}, bf16[8,2,272,128]{3,2,1,0:T(8,128)(2,1)}, u32[]{:S(2)}) copy-start(bf16[8,2,272,128]{3,2,1,0:T(8,128)(2,1)} %get-tuple-element.43.own) | copy-start | bytes 3342340
  129.0 26.7 %all-to-all-start.2 = ((bf16[4,1024,128]{2,1,0:T(8,128)(2,1)}), bf16[4,1024,128]{2,1,0:T(8,128)(2,1)}, u32[]{:S(2)}, u32[]{:S(2)}) async-start(bf16[4,1024,128]{2,1,0:T(8,128)(2,1)} %copy-done.1), calls=%async_computation.2 | async-start | bytes 2097152 | tf_op jit(solution)/shard_map/all_to_all | solution.py:751
  155.6 29.5 %all-to-all-start.3 = ((bf16[32,32,640]{2,1,0:T(8,128)(2,1)}), bf16[32,32,640]{2,1,0:T(8,128)(2,1)S(1)}, u32[]{:S(2)}, u32[]{:S(2)}) async-start(bf16[32,32,640]{2,1,0:T(8,128)(2,1)} %fold.1), calls=%async_computation.3 | async-start | bytes 2621440 | tf_op jit(solution)/shard_map/all_to_all | solution.py:755
  166.7 9.0 %collective-permute-start.10 = (bf16[1024,128]{1,0:T(8,128)(2,1)S(1)}, bf16[1024,128]{1,0:T(8,128)(2,1)S(1)}, u32[]{:S(2)}, u32[]{:S(2)}) collective-permute-start(bf16[1024,128]{1,0:T(8,128)(2,1)S(1)} %fusion.own), channel_id=1, source_target_pairs={{0,32},{32,64},{64,96},{96,0},{1,33},{33,65},{65,97},{97,1},{2,34}... | collective-permute-start | bytes 786440 | tf_op jit(solution)/shard_map/ppermute | solution.py:652
  166.7 9.0 %collective-permute-start.8 = (bf16[1024,128]{1,0:T(8,128)(2,1)S(1)}, bf16[1024,128]{1,0:T(8,128)(2,1)S(1)}, u32[]{:S(2)}, u32[]{:S(2)}) collective-permute-start(bf16[1024,128]{1,0:T(8,128)(2,1)S(1)} %fusion.own), channel_id=1, source_target_pairs={{0,96},{32,0},{64,32},{96,64},{1,97},{33,1},{65,33},{97,65},{2,98}... | collective-permute-start | bytes 786440 | tf_op jit(solution)/shard_map/ppermute | solution.py:653
  175.6 5.4 %collective-permute-start.11 = (bf16[512,128]{1,0:T(8,128)(2,1)S(1)}, bf16[512,128]{1,0:T(8,128)(2,1)S(1)}, u32[]{:S(2)}, u32[]{:S(2)}) collective-permute-start(bf16[512,128]{1,0:T(8,128)(2,1)S(1)} %slice.63), channel_id=1, source_target_pairs={{0,32},{32,64},{64,96},{96,0},{1,33},{33,65},{65,97},{97,1},{2,34}... | collective-permute-start | bytes 393224 | tf_op jit(solution)/shard_map/ppermute | solution.py:652
  175.7 5.3 %collective-permute-start.9 = (bf16[512,128]{1,0:T(8,128)(2,1)S(1)}, bf16[512,128]{1,0:T(8,128)(2,1)S(1)}, u32[]{:S(2)}, u32[]{:S(2)}) collective-permute-start(bf16[512,128]{1,0:T(8,128)(2,1)S(1)} %slice.62), channel_id=1, source_target_pairs={{0,96},{32,0},{64,32},{96,64},{1,97},{33,1},{65,33},{97,65},{2,98}... | collective-permute-start | bytes 393224 | tf_op jit(solution)/shard_map/ppermute | solution.py:653

commit v7 on v6

--- a/solution.py
+++ b/solution.py
@@ -120,7 +120,7 @@
 
 
 def scatter_kernel(touched, incidence, grad, out, *scratch):
-    sums, (tiles_in, sems) = scratch[:-2], scratch[-2:]
+    sums, (tiles_in, held, sems, out_sems) = scratch[:-4], scratch[-4:]
     tiles, tile, _ = incidence.shape
     chunks, rows, _ = out.shape
     steps = tiles // STEP_TILES
@@ -152,7 +152,10 @@
         total = sums[0][place, :]
         for acc in sums[1:]:
             total = total + acc[place, :]
-        out[i] = total.astype(out.dtype)
+        held[i] = total.astype(out.dtype)
+        pltpu.make_async_copy(held.at[i], out.at[i], out_sems.at[i]).start()
+    for i in range(chunks):
+        pltpu.make_async_copy(held.at[i], out.at[i], out_sems.at[i]).wait()
 
 
 def scatter(touched, incidence, grad, rows, chunks):
@@ -166,12 +169,14 @@
         scatter_kernel,
         name="scatter",
         in_specs=[smem, hbm, vmem],
-        out_specs=vmem,
+        out_specs=hbm,
         out_shape=jax.ShapeDtypeStruct((chunks, rows // chunks, width), BF),
         scratch_shapes=[pltpu.VMEM((rows, width), F32)] * 4
         + [
             pltpu.VMEM(incidence.shape, BF),
+            pltpu.VMEM((chunks, rows // chunks, width), BF),
             pltpu.SemaphoreType.DMA((steps,)),
+            pltpu.SemaphoreType.DMA((chunks,)),
         ],
         compiler_params=pltpu.CompilerParams(vmem_limit_bytes=SCATTER_VMEM),
         cost_estimate=pl.CostEstimate(flops=1 << 33, bytes_accessed=8 << 20, transcendentals=0),

time: 187 us -> 187 us (level)
  no operation moved by 1% of the time
where the time goes in v7:
time: 187 us; the launch traced here: 186 us
  waiting for transfers between devices  85.9 us (46%)
  Pallas kernels  51 us (27%)
  starting transfers between devices  42.3 us (23%)
  other arithmetic  4.62 us (2%)
    all_to_all x1, waiting for transfers between devices, body(): lax.all_to_all(pooled.reshape(features, batch, width), dp, split_axis=0,...  39.6 us
    ppermute x4, waiting for transfers between devices, neighbours(): lax.ppermute(value, axis, down)  18 us
    pallas_call x1, Pallas kernels, dense(): pl.pallas_call(functools.partial(dense_kernel, scale), name='dense', in_s...  15.3 us
    ppermute x4, waiting for transfers between devices, neighbours(): lax.ppermute(value, axis, up)  13.4 us
    pallas_call x1, Pallas kernels, gradients(): pl.pallas_call(functools.partial(gradients_kernel, order), name='gradient...  12.3 us
    ppermute x4, starting transfers between devices, neighbours(): lax.ppermute(value, axis, down)  11.7 us
    pallas_call x1, Pallas kernels, pool(): pl.pallas_call(pool_kernel, name='pool', in_specs=[pl.BlockSpec(memory_sp...  11.4 us
    all_to_all x1, starting transfers between devices, body(): pieces = lax.all_to_all(folded, dp, split_axis=0, concat_axis=0, tiled=True)  9.74 us
  transfers between devices with their start and end apart: 16, of which 10 were waited for; matrix products, arithmetic and copies ran while one was open for 3% of the time, Pallas kernels for 13%

profile of v7, /device:TPU:1, one launch (start us, length us, event | category | flops | bytes accessed | tf_op | source)
XLA Modules:
  0.0 185.9 jit_solution(1398648177293605086)
XLA Ops:
  0.6 11.4 %pool.1 = (bf16[12288,128]{1,0:T(8,128)(2,1)}, bf16[96,128,128]{2,1,0:T(8,128)(2,1)}) custom-call(s32[16,96]{1,0:T(8,128)} %bitcast.22, bf16[4096,128]{1,0:T(8,128)(2,1)} %table.1, s32[16,12288]{1,0:T(8,128)} %bitcast.26, s32[16,12288]{1,0:T(8,128)} %bitcast.27), custom_call_target="tpu_custom_call" | custom-call | tf_op jit(solution)/shard_map/pool/pallas_call | solution.py:98
  12.0 0.0 copy-start.9
  12.0 0.0 copy-start.8
  12.0 0.0 copy-start.2
  12.1 0.0 copy-start.4
  12.1 0.0 copy-start.5
  12.1 9.6 %all-to-all-start = ((bf16[32,384,128]{2,1,0:T(8,128)(2,1)}), bf16[32,384,128]{2,1,0:T(8,128)(2,1)}, u32[]{:S(2)}, u32[]{:S(2)}) async-start(bf16[32,384,128]{2,1,0:T(8,128)(2,1)} %bitcast.25), calls=%async_computation | async-start | bytes 6291456 | tf_op jit(solution)/shard_map/all_to_all | solution.py:713
  21.7 0.1 reshape.62.labels
  21.9 0.1 pad_add_fusion.place
  21.9 39.6 %all-to-all-done.received = bf16[32,384,128]{2,1,0:T(8,128)(2,1)} async-done(((bf16[32,384,128]{2,1,0:T(8,128)(2,1)}), bf16[32,384,128]{2,1,0:T(8,128)(2,1)}, u32[]{:S(2)}, u32[]{:S(2)}) %all-to-all-start) | async-done | bytes 3145760 | tf_op jit(solution)/shard_map/all_to_all | solution.py:713
  61.5 15.3 %dense.1 = (bf16[32,384,128]{2,1,0:T(8,128)(2,1)}, bf16[32,384,128]{2,1,0:T(8,128)(2,1)}, bf16[32,384,128]{2,1,0:T(8,128)(2,1)}, bf16[384,256]{1,0:T(8,128)(2,1)...) custom-call(s32[32]{0:T(128)S(1)} %copy-done.5, ...), custom_call_target="tpu_custom_call" | custom-call | tf_op jit(solution)/shard_map/dense/pallas_call | solution.py:374
  76.8 5.0 %all-to-all-start.1 = ((bf16[32,384,128]{2,1,0:T(8,128)(2,1)}), bf16[32,384,128]{2,1,0:T(8,128)(2,1)}, u32[]{:S(2)}, u32[]{:S(2)}) async-start(bf16[32,384,128]{2,1,0:T(8,128)(2,1)} %get-tuple-element.52), calls=%async_computation.1 | async-start | bytes 6291456 | tf_op jit(solution)/shard_map/all_to_all | solution.py:728
  81.9 12.3 %gradients.1 = (bf16[8,2,272,128]{3,2,1,0:T(8,128)(2,1)S(1)}, bf16[8,2,272,128]{3,2,1,0:T(8,128)(2,1)}, bf16[8,2,272,128]{3,2,1,0:T(8,128)(2,1)}, bf16[8,2,272,1...) custom-call(s32[2]{0:T(128)S(1)} %pad_add_fusion.place, ...), custom_call_target="tpu_custom_call" | custom-call | flops 3221225472 | bytes 16777216 | tf_op jit(solution)/shard_map/gradients/pallas_call | solution.py:557
  94.2 0.6 collective-permute-start.2
  94.8 0.2 collective-permute-start.1
  95.0 0.3 collective-permute-start.5
  95.3 2.1 %collective-permute-done.2 = bf16[8,2,272,128]{3,2,1,0:T(8,128)(2,1)S(1)} collective-permute-done((bf16[8,2,272,128]{3,2,1,0:T(8,128)(2,1)}, bf16[8,2,272,128]{3,2,1,0:T(8,128)(2,1)S(1)}, u32[]{:S(2)}, u32[]{:S(2)}) %collective-permute-start.2) | collective-permute-done | bytes 1114144 | tf_op jit(solution)/shard_map/ppermute | solution.py:750
  97.4 0.3 add_convert_fusion.1
  97.7 2.8 %collective-permute-start.3 = (bf16[4,2,272,128]{3,2,1,0:T(8,128)(2,1)S(1)}, bf16[4,2,272,128]{3,2,1,0:T(8,128)(2,1)S(1)}, u32[]{:S(2)}, u32[]{:S(2)}) collective-permute-start(bf16[4,2,272,128]{3,2,1,0:T(8,128)(2,1)S(1)} %get-tuple-element.64), channel_id=1, source_target_pairs={{0,96},{32,0},{64,32},{96,64},{1,97},{33,1},{65,33},{97,65},{2,98}... | collective-permute-start | bytes 1671176 | tf_op jit(solution)/shard_map/ppermute | solution.py:658
  100.5 0.0 collective-permute-start.6
  100.5 0.6 collective-permute-start
  101.1 11.1 %collective-permute-done.3 = bf16[4,2,272,128]{3,2,1,0:T(8,128)(2,1)S(1)} collective-permute-done((bf16[4,2,272,128]{3,2,1,0:T(8,128)(2,1)S(1)}, bf16[4,2,272,128]{3,2,1,0:T(8,128)(2,1)S(1)}, u32[]{:S(2)}, u32[]{:S(2)}) %collective-permute-start.3) | collective-permute-done | bytes 557088 | tf_op jit(solution)/shard_map/ppermute | solution.py:658
  112.2 0.4 add_convert_fusion.5
  112.6 0.0 copy-start.6
  112.6 1.1 pad_maximum_fusion
  113.7 3.5 %collective-permute-start.4 = (bf16[8,2,272,128]{3,2,1,0:T(8,128)(2,1)}, bf16[8,2,272,128]{3,2,1,0:T(8,128)(2,1)S(1)}, u32[]{:S(2)}, u32[]{:S(2)}) collective-permute-start(bf16[8,2,272,128]{3,2,1,0:T(8,128)(2,1)} %pad_maximum_fusion), channel_id=1, source_target_pairs={{0,96},{32,0},{64,32},{96,64},{1,97},{33,1},{65,33},{97,65},{2,98}... | collective-permute-start | bytes 3342344 | tf_op jit(solution)/shard_map/ppermute | solution.py:658
  117.2 0.4 add_convert_fusion.3
  117.6 0.0 copy-start.3
  117.6 1.1 pad_maximum_fusion.1
  118.7 3.0 %all-to-all-done.1 = bf16[32,384,128]{2,1,0:T(8,128)(2,1)} async-done(((bf16[32,384,128]{2,1,0:T(8,128)(2,1)}), bf16[32,384,128]{2,1,0:T(8,128)(2,1)}, u32[]{:S(2)}, u32[]{:S(2)}) %all-to-all-start.1) | async-done | bytes 3145760 | tf_op jit(solution)/shard_map/all_to_all | solution.py:728
  121.7 6.4 %scatter.1 = bf16[4,1024,128]{2,1,0:T(8,128)(2,1)S(1)} custom-call(s32[16,96]{1,0:T(8,128)S(1)} %bitcast.23, bf16[96,128,128]{2,1,0:T(8,128)(2,1)} %get-tuple-element.51.incidence, bf16[12288,128]{1,0:T(8,128)(2,1)} %bitcast.12.grad), custom_call_target="tpu_custom_call" | custom-call | flops 8589934592 | bytes 8388608 | tf_op jit(solution)/shard_map/scatter/pallas_call | solution.py:168
  128.1 1.0 copy-done.1
  129.1 4.4 %all-to-all-start.2 = ((bf16[4,1024,128]{2,1,0:T(8,128)(2,1)}), bf16[4,1024,128]{2,1,0:T(8,128)(2,1)}, u32[]{:S(2)}, u32[]{:S(2)}) async-start(bf16[4,1024,128]{2,1,0:T(8,128)(2,1)} %copy-done.1), calls=%async_computation.2 | async-start | bytes 2097152 | tf_op jit(solution)/shard_map/all_to_all | solution.py:756
  133.5 6.9 %collective-permute-done.4.from_following = bf16[8,2,272,128]{3,2,1,0:T(8,128)(2,1)S(1)} collective-permute-done((bf16[8,2,272,128]{3,2,1,0:T(8,128)(2,1)}, bf16[8,2,272,128]{3,2,1,0:T(8,128)(2,1)S(1)}, u32[]{:S(2)}, u32[]{:S(2)}) %collective-permute-start.4) | collective-permute-done | bytes 1114144 | tf_op jit(solution)/shard_map/ppermute | solution.py:658
  140.3 4.6 %collective-permute-done.7.from_preceding = bf16[8,2,272,128]{3,2,1,0:T(8,128)(2,1)} collective-permute-done((bf16[8,2,272,128]{3,2,1,0:T(8,128)(2,1)}, bf16[8,2,272,128]{3,2,1,0:T(8,128)(2,1)}, u32[]{:S(2)}, u32[]{:S(2)}) %collective-permute-start.7) | collective-permute-done | bytes 1114144 | tf_op jit(solution)/shard_map/ppermute | solution.py:657
  145.0 3.5 %fold.1 = bf16[32,32,640]{2,1,0:T(8,128)(2,1)} custom-call(bf16[8,2,272,128]{3,2,1,0:T(8,128)(2,1)S(1)} %copy-done, bf16[8,2,272,128]{3,2,1,0:T(8,128)(2,1)S(1)} %collective-permute-done.swapped, bf16[8,2,272,128]{3,2,1,0:T(8,128)(2,1)S(1)} %collective-permute-done.4.from_following, bf16[8,2,272,128]{3,2,1,0:T(8,128)(2,1)} %collective-permute-done.7.from_preceding), custom_call_target="tpu_custom_call" | custom-call | tf_op jit(solution)/shard_map/fold/pallas_call | solution.py:610
  148.4 7.1 %all-to-all-done.2 = bf16[4,1024,128]{2,1,0:T(8,128)(2,1)} async-done(((bf16[4,1024,128]{2,1,0:T(8,128)(2,1)}), bf16[4,1024,128]{2,1,0:T(8,128)(2,1)}, u32[]{:S(2)}, u32[]{:S(2)}) %all-to-all-start.2) | async-done | bytes 1048608 | tf_op jit(solution)/shard_map/all_to_all | solution.py:756
  155.6 9.7 %all-to-all-start.3 = ((bf16[32,32,640]{2,1,0:T(8,128)(2,1)}), bf16[32,32,640]{2,1,0:T(8,128)(2,1)S(1)}, u32[]{:S(2)}, u32[]{:S(2)}) async-start(bf16[32,32,640]{2,1,0:T(8,128)(2,1)} %fold.1), calls=%async_computation.3 | async-start | bytes 2621440 | tf_op jit(solution)/shard_map/all_to_all | solution.py:760
  165.3 1.3 fusion.own
  166.6 0.1 collective-permute-start.10
  166.7 2.7 %collective-permute-start.8 = (bf16[1024,128]{1,0:T(8,128)(2,1)S(1)}, bf16[1024,128]{1,0:T(8,128)(2,1)S(1)}, u32[]{:S(2)}, u32[]{:S(2)}) collective-permute-start(bf16[1024,128]{1,0:T(8,128)(2,1)S(1)} %fusion.own), channel_id=1, source_target_pairs={{0,96},{32,0},{64,32},{96,64},{1,97},{33,1},{65,33},{97,65},{2,98}... | collective-permute-start | bytes 786440 | tf_op jit(solution)/shard_map/ppermute | solution.py:658
  169.4 6.2 %collective-permute-done.10.preceding = bf16[1024,128]{1,0:T(8,128)(2,1)S(1)} collective-permute-done((bf16[1024,128]{1,0:T(8,128)(2,1)S(1)}, bf16[1024,128]{1,0:T(8,128)(2,1)S(1)}, u32[]{:S(2)}, u32[]{:S(2)}) %collective-permute-start.10) | collective-permute-done | bytes 262176 | tf_op jit(solution)/shard_map/ppermute | solution.py:657
  175.6 0.1 collective-permute-start.11
  175.7 2.7 %collective-permute-start.9 = (bf16[512,128]{1,0:T(8,128)(2,1)S(1)}, bf16[512,128]{1,0:T(8,128)(2,1)S(1)}, u32[]{:S(2)}, u32[]{:S(2)}) collective-permute-start(bf16[512,128]{1,0:T(8,128)(2,1)S(1)} %slice.62), channel_id=1, source_target_pairs={{0,96},{32,0},{64,32},{96,64},{1,97},{33,1},{65,33},{97,65},{2,98}... | collective-permute-start | bytes 393224 | tf_op jit(solution)/shard_map/ppermute | solution.py:658
  178.4 2.6 %collective-permute-done.11.opposite_b = bf16[512,128]{1,0:T(8,128)(2,1)S(1)} collective-permute-done((bf16[512,128]{1,0:T(8,128)(2,1)S(1)}, bf16[512,128]{1,0:T(8,128)(2,1)S(1)}, u32[]{:S(2)}, u32[]{:S(2)}) %collective-permute-start.11) | collective-permute-done | bytes 131104 | tf_op jit(solution)/shard_map/ppermute | solution.py:657
  181.0 1.5 spread_rows.1
  182.4 2.6 %all-to-all-done.3.pieces = bf16[32,32,640]{2,1,0:T(8,128)(2,1)S(1)} async-done(((bf16[32,32,640]{2,1,0:T(8,128)(2,1)}), bf16[32,32,640]{2,1,0:T(8,128)(2,1)S(1)}, u32[]{:S(2)}, u32[]{:S(2)}) %all-to-all-start.3) | async-done | bytes 1310752 | tf_op jit(solution)/shard_map/all_to_all | solution.py:760
  185.1 0.8 finish.1
  (22 shorter events, 0.1 us)
Async XLA Ops:
  12.0 9.7 %copy-start.9 = (bf16[512]{0:T(512)(128)(2,1)S(1)}, bf16[512]{0:T(512)(128)(2,1)}, u32[]{:S(2)}) copy-start(bf16[512]{0:T(512)(128)(2,1)} %param.23) | copy-start | bytes 3076
  12.0 9.7 %copy-start.8 = (s32[384]{0:T(512)S(1)}, s32[384]{0:T(512)}, u32[]{:S(2)}) copy-start(s32[384]{0:T(512)} %param.17) | copy-start | bytes 4612
  12.0 49.5 %copy-start.2 = (f32[4096]{0:T(1024)S(1)}, f32[4096]{0:T(1024)}, u32[]{:S(2)}) copy-start(f32[4096]{0:T(1024)} %param.20) | copy-start | bytes 49156
  12.1 49.5 %copy-start.4 = (f32[512]{0:T(512)S(1)}, f32[512]{0:T(512)}, u32[]{:S(2)}) copy-start(f32[512]{0:T(512)} %param.22) | copy-start | bytes 6148
  12.1 49.5 %copy-start.5 = (s32[32]{0:T(128)S(1)}, s32[32]{0:T(128)}, u32[]{:S(2)}) copy-start(s32[32]{0:T(128)} %fmap.3) | copy-start | bytes 388
  12.1 49.5 %all-to-all-start = ((bf16[32,384,128]{2,1,0:T(8,128)(2,1)}), bf16[32,384,128]{2,1,0:T(8,128)(2,1)}, u32[]{:S(2)}, u32[]{:S(2)}) async-start(bf16[32,384,128]{2,1,0:T(8,128)(2,1)} %bitcast.25), calls=%async_computation | async-start | bytes 6291456 | tf_op jit(solution)/shard_map/all_to_all | solution.py:713
  76.8 44.9 %all-to-all-start.1 = ((bf16[32,384,128]{2,1,0:T(8,128)(2,1)}), bf16[32,384,128]{2,1,0:T(8,128)(2,1)}, u32[]{:S(2)}, u32[]{:S(2)}) async-start(bf16[32,384,128]{2,1,0:T(8,128)(2,1)} %get-tuple-element.52), calls=%async_computation.1 | async-start | bytes 6291456 | tf_op jit(solution)/shard_map/all_to_all | solution.py:728
  94.2 3.2 %collective-permute-start.2 = (bf16[8,2,272,128]{3,2,1,0:T(8,128)(2,1)}, bf16[8,2,272,128]{3,2,1,0:T(8,128)(2,1)S(1)}, u32[]{:S(2)}, u32[]{:S(2)}) collective-permute-start(bf16[8,2,272,128]{3,2,1,0:T(8,128)(2,1)} %get-tuple-element.48), channel_id=1, source_target_pairs={{0,1},{1,0},{2,3},{3,2},{4,5},{5,4},{6,7},{7,6},{8,9},{9,8},{10,11... | collective-permute-start | bytes 3342344 | tf_op jit(solution)/shard_map/ppermute | solution.py:750
  94.8 6.3 %collective-permute-start.1 = (bf16[8,2,272,128]{3,2,1,0:T(8,128)(2,1)}, bf16[8,2,272,128]{3,2,1,0:T(8,128)(2,1)S(1)}, u32[]{:S(2)}, u32[]{:S(2)}) collective-permute-start(bf16[8,2,272,128]{3,2,1,0:T(8,128)(2,1)} %get-tuple-element.46), channel_id=1, source_target_pairs={{0,1},{1,0},{2,3},{3,2},{4,5},{5,4},{6,7},{7,6},{8,9},{9,8},{10,11... | collective-permute-start | bytes 3342344 | tf_op jit(solution)/shard_map/ppermute | solution.py:750
  95.0 22.2 %collective-permute-start.5 = (bf16[8,2,272,128]{3,2,1,0:T(8,128)(2,1)}, bf16[8,2,272,128]{3,2,1,0:T(8,128)(2,1)S(1)}, u32[]{:S(2)}, u32[]{:S(2)}) collective-permute-start(bf16[8,2,272,128]{3,2,1,0:T(8,128)(2,1)} %get-tuple-element.50), channel_id=1, source_target_pairs={{0,1},{1,0},{2,3},{3,2},{4,5},{5,4},{6,7},{7,6},{8,9},{9,8},{10,11... | collective-permute-start | bytes 3342344 | tf_op jit(solution)/shard_map/ppermute | solution.py:750
  97.4 14.8 %copy-start.7 = (bf16[8,2,272,128]{3,2,1,0:T(8,128)(2,1)S(1)}, bf16[8,2,272,128]{3,2,1,0:T(8,128)(2,1)}, u32[]{:S(2)}) copy-start(bf16[8,2,272,128]{3,2,1,0:T(8,128)(2,1)} %get-tuple-element.45) | copy-start | bytes 3342340
  97.7 14.5 %collective-permute-start.3 = (bf16[4,2,272,128]{3,2,1,0:T(8,128)(2,1)S(1)}, bf16[4,2,272,128]{3,2,1,0:T(8,128)(2,1)S(1)}, u32[]{:S(2)}, u32[]{:S(2)}) collective-permute-start(bf16[4,2,272,128]{3,2,1,0:T(8,128)(2,1)S(1)} %get-tuple-element.64), channel_id=1, source_target_pairs={{0,96},{32,0},{64,32},{96,64},{1,97},{33,1},{65,33},{97,65},{2,98}... | collective-permute-start | bytes 1671176 | tf_op jit(solution)/shard_map/ppermute | solution.py:658
  100.5 16.7 %collective-permute-start.6 = (bf16[4,2,272,128]{3,2,1,0:T(8,128)(2,1)S(1)}, bf16[4,2,272,128]{3,2,1,0:T(8,128)(2,1)S(1)}, u32[]{:S(2)}, u32[]{:S(2)}) collective-permute-start(bf16[4,2,272,128]{3,2,1,0:T(8,128)(2,1)S(1)} %get-tuple-element.63), channel_id=1, source_target_pairs={{0,32},{32,64},{64,96},{96,0},{1,33},{33,65},{65,97},{97,1},{2,34}... | collective-permute-start | bytes 1671176 | tf_op jit(solution)/shard_map/ppermute | solution.py:657
  100.5 33.0 %collective-permute-start = (bf16[8,2,272,128]{3,2,1,0:T(8,128)(2,1)}, bf16[8,2,272,128]{3,2,1,0:T(8,128)(2,1)S(1)}, u32[]{:S(2)}, u32[]{:S(2)}) collective-permute-start(bf16[8,2,272,128]{3,2,1,0:T(8,128)(2,1)} %get-tuple-element.44), channel_id=1, source_target_pairs={{0,1},{1,0},{2,3},{3,2},{4,5},{5,4},{6,7},{7,6},{8,9},{9,8},{10,11... | collective-permute-start | bytes 3342344 | tf_op jit(solution)/shard_map/ppermute | solution.py:750
  112.6 4.6 %copy-start.6 = (bf16[8,2,272,128]{3,2,1,0:T(8,128)(2,1)S(1)}, bf16[8,2,272,128]{3,2,1,0:T(8,128)(2,1)}, u32[]{:S(2)}) copy-start(bf16[8,2,272,128]{3,2,1,0:T(8,128)(2,1)} %get-tuple-element.49) | copy-start | bytes 3342340
  113.7 26.7 %collective-permute-start.4 = (bf16[8,2,272,128]{3,2,1,0:T(8,128)(2,1)}, bf16[8,2,272,128]{3,2,1,0:T(8,128)(2,1)S(1)}, u32[]{:S(2)}, u32[]{:S(2)}) collective-permute-start(bf16[8,2,272,128]{3,2,1,0:T(8,128)(2,1)} %pad_maximum_fusion), channel_id=1, source_target_pairs={{0,96},{32,0},{64,32},{96,64},{1,97},{33,1},{65,33},{97,65},{2,98}... | collective-permute-start | bytes 3342344 | tf_op jit(solution)/shard_map/ppermute | solution.py:658
  117.6 4.1 %copy-start.3 = (s32[1,96,16]{1,2,0:T(8,128)S(1)}, s32[1,96,16]{1,2,0:T(8,128)}, u32[]{:S(2)}) copy-start(s32[1,96,16]{1,2,0:T(8,128)} %param.13) | copy-start | bytes 18436
  118.7 26.3 %collective-permute-start.7 = (bf16[8,2,272,128]{3,2,1,0:T(8,128)(2,1)}, bf16[8,2,272,128]{3,2,1,0:T(8,128)(2,1)}, u32[]{:S(2)}, u32[]{:S(2)}) collective-permute-start(bf16[8,2,272,128]{3,2,1,0:T(8,128)(2,1)} %pad_maximum_fusion.1), channel_id=1, source_target_pairs={{0,32},{32,64},{64,96},{96,0},{1,33},{33,65},{65,97},{97,1},{2,34}... | collective-permute-start | bytes 3342344 | tf_op jit(solution)/shard_map/ppermute | solution.py:657
  128.1 1.0 copy-start.1
  129.1 15.9 %copy-start = (bf16[8,2,272,128]{3,2,1,0:T(8,128)(2,1)S(1)}, bf16[8,2,272,128]{3,2,1,0:T(8,128)(2,1)}, u32[]{:S(2)}) copy-start(bf16[8,2,272,128]{3,2,1,0:T(8,128)(2,1)} %get-tuple-element.43.own) | copy-start | bytes 3342340
  129.1 26.5 %all-to-all-start.2 = ((bf16[4,1024,128]{2,1,0:T(8,128)(2,1)}), bf16[4,1024,128]{2,1,0:T(8,128)(2,1)}, u32[]{:S(2)}, u32[]{:S(2)}) async-start(bf16[4,1024,128]{2,1,0:T(8,128)(2,1)} %copy-done.1), calls=%async_computation.2 | async-start | bytes 2097152 | tf_op jit(solution)/shard_map/all_to_all | solution.py:756
  155.6 29.5 %all-to-all-start.3 = ((bf16[32,32,640]{2,1,0:T(8,128)(2,1)}), bf16[32,32,640]{2,1,0:T(8,128)(2,1)S(1)}, u32[]{:S(2)}, u32[]{:S(2)}) async-start(bf16[32,32,640]{2,1,0:T(8,128)(2,1)} %fold.1), calls=%async_computation.3 | async-start | bytes 2621440 | tf_op jit(solution)/shard_map/all_to_all | solution.py:760
  166.6 9.0 %collective-permute-start.10 = (bf16[1024,128]{1,0:T(8,128)(2,1)S(1)}, bf16[1024,128]{1,0:T(8,128)(2,1)S(1)}, u32[]{:S(2)}, u32[]{:S(2)}) collective-permute-start(bf16[1024,128]{1,0:T(8,128)(2,1)S(1)} %fusion.own), channel_id=1, source_target_pairs={{0,32},{32,64},{64,96},{96,0},{1,33},{33,65},{65,97},{97,1},{2,34}... | collective-permute-start | bytes 786440 | tf_op jit(solution)/shard_map/ppermute | solution.py:657
  166.7 9.0 %collective-permute-start.8 = (bf16[1024,128]{1,0:T(8,128)(2,1)S(1)}, bf16[1024,128]{1,0:T(8,128)(2,1)S(1)}, u32[]{:S(2)}, u32[]{:S(2)}) collective-permute-start(bf16[1024,128]{1,0:T(8,128)(2,1)S(1)} %fusion.own), channel_id=1, source_target_pairs={{0,96},{32,0},{64,32},{96,64},{1,97},{33,1},{65,33},{97,65},{2,98}... | collective-permute-start | bytes 786440 | tf_op jit(solution)/shard_map/ppermute | solution.py:658
  175.6 5.4 %collective-permute-start.11 = (bf16[512,128]{1,0:T(8,128)(2,1)S(1)}, bf16[512,128]{1,0:T(8,128)(2,1)S(1)}, u32[]{:S(2)}, u32[]{:S(2)}) collective-permute-start(bf16[512,128]{1,0:T(8,128)(2,1)S(1)} %slice.63), channel_id=1, source_target_pairs={{0,32},{32,64},{64,96},{96,0},{1,33},{33,65},{65,97},{97,1},{2,34}... | collective-permute-start | bytes 393224 | tf_op jit(solution)/shard_map/ppermute | solution.py:657
  175.7 5.3 %collective-permute-start.9 = (bf16[512,128]{1,0:T(8,128)(2,1)S(1)}, bf16[512,128]{1,0:T(8,128)(2,1)S(1)}, u32[]{:S(2)}, u32[]{:S(2)}) collective-permute-start(bf16[512,128]{1,0:T(8,128)(2,1)S(1)} %slice.62), channel_id=1, source_target_pairs={{0,96},{32,0},{64,32},{96,64},{1,97},{33,1},{65,33},{97,65},{2,98}... | collective-permute-start | bytes 393224 | tf_op jit(solution)/shard_map/ppermute | solution.py:658
